TPU v7x, 32 devices: a whole 2x2x4 slice. The times are simulated.
32 devices in a mesh: dp: 16 (over z, y, x), section: 2 (over core).
Axes of the slice: x: 2, y: 2, z: 4, core: 2. Of those that a mesh axis runs over, the one named last changes fastest.
Arguments:
- images: float32 [64, 256, 48], P('dp'), may hold values from -1 to 1
- noise_draw: float32 [64, 256, 48], P('dp'), may hold values from -6 to 6
- labels: int32 [64], P('dp'), may hold values from 0 to 999
- class_drop: int32 [64], P('dp'), may hold values 0 or 1
- w_qkv: float32 [2, 768, 2304], P('section', 'dp'), may hold values from -0.21875 to 0.21875
- w_attn: float32 [2, 768, 768], P('section', 'dp'), may hold values from -0.625 to 0.625
- w_up: float32 [2, 768, 3072], P('section', 'dp'), may hold values from -0.21875 to 0.21875
- w_down: float32 [2, 3072, 768], P('section', 'dp'), may hold values from -0.109375 to 0.109375
- w_in: float32 [2, 48, 768], P('section', None, 'dp'), may hold values from -0.875 to 0.875
- w_head: float32 [2, 768, 96], P('section', 'dp'), may hold values from -0.109375 to 0.109375
- w_embed: float32 [2, 1256, 768], P('section', None, 'dp'), may hold values from -3 to 3
- w_norms: float32 [2, 6, 768], P('section', None, 'dp'), may hold values from -1.2 to 1.8
- moment_qkv: float32 [2, 768, 2304], P('section', 'dp'), may hold values from -1.4901161e-07 to 1.4901161e-07
- moment_attn: float32 [2, 768, 768], P('section', 'dp'), may hold values from -1.4901161e-07 to 1.4901161e-07
- moment_up: float32 [2, 768, 3072], P('section', 'dp'), may hold values from -1.4901161e-07 to 1.4901161e-07
- moment_down: float32 [2, 3072, 768], P('section', 'dp'), may hold values from -1.4901161e-07 to 1.4901161e-07
- moment_in: float32 [2, 48, 768], P('section', None, 'dp'), may hold values from -1.4901161e-07 to 1.4901161e-07
- moment_head: float32 [2, 768, 96], P('section', 'dp'), may hold values from -1.4901161e-07 to 1.4901161e-07
- moment_embed: float32 [2, 1256, 768], P('section', None, 'dp'), may hold values from -1e-06 to 1e-06
- moment_norms: float32 [2, 6, 768], P('section', None, 'dp'), may hold values from -1.4901161e-07 to 1.4901161e-07
- square_qkv: float32 [2, 768, 2304], P('section', 'dp'), may hold values from 3.2e-15 to 1.3e-14
- square_attn: float32 [2, 768, 768], P('section', 'dp'), may hold values from 3.2e-15 to 1.3e-14
- square_up: float32 [2, 768, 3072], P('section', 'dp'), may hold values from 3.2e-15 to 1.3e-14
- square_down: float32 [2, 3072, 768], P('section', 'dp'), may hold values from 3.2e-15 to 1.3e-14
- square_in: float32 [2, 48, 768], P('section', None, 'dp'), may hold values from 3.2e-15 to 1.3e-14
- square_head: float32 [2, 768, 96], P('section', 'dp'), may hold values from 3.2e-15 to 1.3e-14
- square_embed: float32 [2, 1256, 768], P('section', None, 'dp'), may hold values from 0 to 1e-13
- square_norms: float32 [2, 6, 768], P('section', None, 'dp'), may hold values from 3.2e-15 to 1.3e-14
Outputs:
- new_moment_qkv: float32 [2, 768, 2304], P('section', 'dp')
- new_moment_attn: float32 [2, 768, 768], P('section', 'dp')
- new_moment_up: float32 [2, 768, 3072], P('section', 'dp')
- new_moment_down: float32 [2, 3072, 768], P('section', 'dp')
- new_moment_in: float32 [2, 48, 768], P('section', None, 'dp')
- new_moment_head: float32 [2, 768, 96], P('section', 'dp')
- new_moment_embed: float32 [2, 1256, 768], P('section', None, 'dp')
- new_moment_norms: float32 [2, 6, 768], P('section', None, 'dp')
- new_square_qkv: float32 [2, 768, 2304], P('section', 'dp')
- new_square_attn: float32 [2, 768, 768], P('section', 'dp')
- new_square_up: float32 [2, 768, 3072], P('section', 'dp')
- new_square_down: float32 [2, 3072, 768], P('section', 'dp')
- new_square_in: float32 [2, 48, 768], P('section', None, 'dp')
- new_square_head: float32 [2, 768, 96], P('section', 'dp')
- new_square_embed: float32 [2, 1256, 768], P('section', None, 'dp')
- new_square_norms: float32 [2, 6, 768], P('section', None, 'dp')
- new_qkv: float32 [2, 768, 2304], P('section', 'dp')
- new_attn: float32 [2, 768, 768], P('section', 'dp')
- new_up: float32 [2, 768, 3072], P('section', 'dp')
- new_down: float32 [2, 3072, 768], P('section', 'dp')
- new_in: float32 [2, 48, 768], P('section', None, 'dp')
- new_head: float32 [2, 768, 96], P('section', 'dp')
- new_embed: float32 [2, 1256, 768], P('section', None, 'dp')
- new_norms: float32 [2, 6, 768], P('section', None, 'dp')
- loss_sum: float32 [], replicated
- grad_norm: float32 [], replicated
- activity: float32 [2, 3], replicated
All inputs are finite; a program needn't handle non-finite values. No bound on the sum of `class_drop` on one device may be relied on, other than what follows from the above.
Results may differ from a plain program's by a relative error of at most 0.011.
Values may be sent and summed in bfloat16 or wider, within the bound.
No kernel may reach another device: no remote copies, remote signals or barrier semaphores. Data moves between devices by JAX's collectives and lax.ppermute only.
A program may use at most 256 MiB of HBM per device.

v0:
```python
from functools import partial
import math

import jax
import jax.numpy as jnp
from jax import lax
from jax.sharding import PartitionSpec as P

D = 768
H = 12
HD = 64
PD = 48
P_SIZE = 256
MICRO = 2
STEP = 10


EPS_NORM = 1e-05
NOISE_SCALE = 0.05
CLIP_NORM = 0.001
BETA_ONE = 0.9
BETA_TWO = 0.95
LEARN_RATES = (0.01, 0.06, 0.01, 0.01, 0.08, 0.01, 0.25, 0.4)
WEIGHT_DECAY = 0.1
EPS_ADAM = 1e-10


def from_behind(value, axis, steps):
    count = lax.axis_size(axis)
    first, last = (max(0, -steps), min(count, count - steps))
    return lax.ppermute(value, axis, [(source, source + steps) for source in range(first, last)])


def round_plain(v):
    return lax.optimization_barrier(v.astype(jnp.bfloat16)).astype(jnp.float32)


def pass_plain(v):
    return v


def product_plain(left_side, right_side):
    return jnp.matmul(
        left_side.astype(jnp.bfloat16),
        right_side.astype(jnp.bfloat16),
        preferred_element_type=jnp.float32,
    )


def product_keep(left_side, right_side):
    return (product_plain(left_side, right_side), (left_side, right_side))


def product_back(kept, cotangent):
    left_side, right_side = kept
    narrow = cotangent.astype(jnp.bfloat16)
    left_low = left_side.astype(jnp.bfloat16)
    right_low = right_side.astype(jnp.bfloat16)
    left_grad = jnp.matmul(
        narrow, jnp.swapaxes(right_low, -1, -2), preferred_element_type=jnp.float32
    )
    if right_side.ndim == 2:
        right_grad = jnp.dot(
            left_low.reshape(-1, left_side.shape[-1]).T,
            narrow.reshape(-1, narrow.shape[-1]),
            preferred_element_type=jnp.float32,
        )
    else:
        right_grad = jnp.matmul(
            jnp.swapaxes(left_low, -1, -2), narrow, preferred_element_type=jnp.float32
        )
    return (left_grad, right_grad)


def make_tools():
    round_value = jax.custom_vjp(round_plain)
    round_grad = jax.custom_vjp(pass_plain)

    def value_keep(v):
        return (round_plain(v), None)

    def value_pass(kept, grad):
        return (grad,)

    def grad_keep(v):
        return (v, None)

    def grad_round(kept, grad):
        return (round_plain(grad),)

    round_value.defvjp(value_keep, value_pass)
    round_grad.defvjp(grad_keep, grad_round)
    product = jax.custom_vjp(product_plain)
    product.defvjp(product_keep, product_back)
    return (round_value, round_grad, product)


def layer_norm(values, gain, offset):
    center = values - jnp.mean(values, axis=-1, keepdims=True)
    spread = jnp.mean(center * center, axis=-1, keepdims=True)
    return center * lax.rsqrt(spread + EPS_NORM) * gain + offset


def flow_block(params, inputs, labels, keep, tools):
    round_value, round_grad, product = tools
    w_qkv, w_attn, w_up, w_down, w_in, w_head, w_embed, w_norms = params
    count_images = inputs.shape[0]
    hidden = round_grad(product(round_value(inputs), round_value(w_in)))
    classes = jnp.take(w_embed[P_SIZE:], labels, axis=0) * keep[:, None]
    hidden = hidden + w_embed[:P_SIZE][None] + classes[:, None, :]
    normed = layer_norm(hidden, w_norms[0], w_norms[1])
    joint = round_value(round_grad(product(round_value(normed), round_value(w_qkv))))
    joint = joint.reshape(count_images, P_SIZE, 3, H, HD).transpose(2, 0, 3, 1, 4)
    queries, key_rows, value_rows = (joint[0], joint[1], joint[2])
    scores = round_grad(product(queries, jnp.swapaxes(key_rows, -1, -2))) * HD ** (-0.5)
    causal = jnp.arange(P_SIZE)[:, None] >= jnp.arange(P_SIZE)[None, :]
    scores = jnp.where(causal, scores, -1e30)
    scores = scores - jnp.max(scores, axis=-1, keepdims=True)
    exps = jnp.exp(scores)
    probs = exps / jnp.sum(exps, axis=-1, keepdims=True)
    attended = round_value(round_grad(product(round_value(probs), value_rows)))
    attended = attended.transpose(0, 2, 1, 3).reshape(count_images, P_SIZE, H * HD)
    branch_attn = round_grad(product(attended, round_value(w_attn)))
    hidden = hidden + branch_attn
    normed = layer_norm(hidden, w_norms[2], w_norms[3])
    up_out = round_grad(product(round_value(normed), round_value(w_up)))
    branch_mlp = round_grad(
        product(round_value(jax.nn.gelu(up_out, approximate=False)), round_value(w_down))
    )
    hidden = hidden + branch_mlp
    normed = layer_norm(hidden, w_norms[4], w_norms[5])
    head_out = round_grad(product(round_value(normed), round_value(w_head)))
    padding = jnp.zeros((count_images, 1, PD), jnp.float32)
    shift = jnp.concatenate([padding, head_out[:, :-1, :PD]], axis=1)
    log_scale = jnp.concatenate([padding, head_out[:, :-1, PD:]], axis=1)
    latent = (inputs - shift) * jnp.exp(-log_scale)
    statistics = jnp.stack(
        [
            jnp.sum(hidden * hidden),
            jnp.sum(branch_attn * branch_attn),
            jnp.sum(branch_mlp * branch_mlp),
        ]
    )
    return (latent, jnp.sum(log_scale), statistics)


def run_block(params, inputs, labels, keep, tools):
    latent, log_det, statistics = flow_block(params, inputs, labels, keep, tools)
    return ((latent, log_det), statistics)


def add_parts(first_group, second_group):
    return tuple(
        (first_part + second_part for first_part, second_part in zip(first_group, second_group))
    )


def body(
    images,
    noise_draw,
    labels,
    class_drop,
    w_qkv,
    w_attn,
    w_up,
    w_down,
    w_in,
    w_head,
    w_embed,
    w_norms,
    moment_qkv,
    moment_attn,
    moment_up,
    moment_down,
    moment_in,
    moment_head,
    moment_embed,
    moment_norms,
    square_qkv,
    square_attn,
    square_up,
    square_down,
    square_in,
    square_head,
    square_embed,
    square_norms,
):
    tools = make_tools()
    weights = (w_qkv, w_attn, w_up, w_down, w_in, w_head, w_embed, w_norms)
    moments = (
        moment_qkv,
        moment_attn,
        moment_up,
        moment_down,
        moment_in,
        moment_head,
        moment_embed,
        moment_norms,
    )
    squares = (
        square_qkv,
        square_attn,
        square_up,
        square_down,
        square_in,
        square_head,
        square_embed,
        square_norms,
    )
    section_index = lax.axis_index("section")
    is_first = section_index == 0
    matrices = (
        lax.all_gather(w_qkv[0].astype(jnp.bfloat16), "dp", axis=0, tiled=True),
        lax.all_gather(w_attn[0].astype(jnp.bfloat16), "dp", axis=0, tiled=True),
        lax.all_gather(w_up[0].astype(jnp.bfloat16), "dp", axis=0, tiled=True),
        lax.all_gather(w_down[0].astype(jnp.bfloat16), "dp", axis=0, tiled=True),
        lax.all_gather(w_in[0].astype(jnp.bfloat16), "dp", axis=1, tiled=True),
        lax.all_gather(w_head[0].astype(jnp.bfloat16), "dp", axis=0, tiled=True),
    )
    table_parts = (
        lax.all_gather(w_embed[0], "dp", axis=1, tiled=True),
        lax.all_gather(w_norms[0], "dp", axis=1, tiled=True),
    )
    params = tuple((matrix.astype(jnp.float32) for matrix in matrices)) + tuple(table_parts)
    inputs_all = images + NOISE_SCALE * noise_draw
    keep_all = (1 - class_drop).astype(jnp.float32)
    micro_rows = images.shape[0] // MICRO
    total_images = images.shape[0] * lax.axis_size("dp")
    coefficient = 1.0 / (total_images * P_SIZE * PD * math.log(2.0))
    received = jnp.zeros((micro_rows, P_SIZE, PD), jnp.float32)
    records = []
    loss_local = jnp.zeros((), jnp.float32)
    stat_local = jnp.zeros((3,), jnp.float32)
    for time_step in range(MICRO + 1):
        batch_index = time_step - section_index
        valid = ((batch_index >= 0) & (batch_index < MICRO)).astype(jnp.float32)
        start = jnp.clip(batch_index, 0, MICRO - 1) * micro_rows
        own_inputs = lax.dynamic_slice_in_dim(inputs_all, start, micro_rows, 0)
        batch_labels = lax.dynamic_slice_in_dim(labels, start, micro_rows, 0)
        batch_keep = lax.dynamic_slice_in_dim(keep_all, start, micro_rows, 0)
        block_inputs = jnp.where(is_first, own_inputs, received[:, ::-1])
        runner = partial(run_block, labels=batch_labels, keep=batch_keep, tools=tools)
        outputs, backward, statistics = jax.vjp(runner, params, block_inputs, has_aux=True)
        latent, log_det = outputs
        loss_local = loss_local + valid * (
            log_det + jnp.where(is_first, 0.0, 0.5 * jnp.sum(latent * latent))
        )
        stat_local = stat_local + valid * statistics
        records.append((block_inputs, runner, backward, latent, valid))
        if time_step < MICRO:
            received = from_behind(latent, "section", 1)
    rows_local = jnp.where(jnp.arange(2)[:, None] == section_index, stat_local[None, :], 0.0)
    loss_sum, activity_sums = lax.psum((loss_local, rows_local), ("dp", "section"))
    accum = tuple((jnp.zeros_like(param) for param in params))
    back_received = jnp.zeros((micro_rows, P_SIZE, PD), jnp.float32)
    for time_step in range(MICRO + 1):
        block_inputs, runner, backward, latent, valid = records[MICRO - time_step]
        latent_grad = valid * jnp.where(is_first, back_received, coefficient * latent)
        param_grads, input_grad = backward((latent_grad, valid * coefficient))
        accum = add_parts(accum, param_grads)
        if time_step < MICRO:
            back_received = from_behind(input_grad[:, ::-1], "section", -1)
    shards = (
        lax.psum_scatter(accum[0], "dp", scatter_dimension=0, tiled=True),
        lax.psum_scatter(accum[1], "dp", scatter_dimension=0, tiled=True),
        lax.psum_scatter(accum[2], "dp", scatter_dimension=0, tiled=True),
        lax.psum_scatter(accum[3], "dp", scatter_dimension=0, tiled=True),
        lax.psum_scatter(accum[4], "dp", scatter_dimension=1, tiled=True),
        lax.psum_scatter(accum[5], "dp", scatter_dimension=0, tiled=True),
        lax.psum_scatter(accum[6], "dp", scatter_dimension=1, tiled=True),
        lax.psum_scatter(accum[7], "dp", scatter_dimension=1, tiled=True),
    )
    square_local = sum((jnp.sum(shard * shard) for shard in shards))
    grad_norm = jnp.sqrt(lax.psum(square_local, ("dp", "section")))
    factor = jnp.minimum(1.0, CLIP_NORM / grad_norm)
    new_moments, new_squares, new_weights = ([], [], [])
    for weight, moment, square, shard, rate in zip(weights, moments, squares, shards, LEARN_RATES):
        clipped = shard[None] * factor
        moment_next = BETA_ONE * moment + (1 - BETA_ONE) * clipped
        square_next = BETA_TWO * square + (1 - BETA_TWO) * clipped * clipped
        update = (
            moment_next
            / (1 - BETA_ONE**STEP)
            / (jnp.sqrt(square_next / (1 - BETA_TWO**STEP)) + EPS_ADAM)
        )
        new_moments.append(moment_next)
        new_squares.append(square_next)
        new_weights.append(weight - rate * (update + WEIGHT_DECAY * weight))
    activity = jnp.sqrt(activity_sums / (total_images * P_SIZE * D))
    return (
        new_moments[0],
        new_moments[1],
        new_moments[2],
        new_moments[3],
        new_moments[4],
        new_moments[5],
        new_moments[6],
        new_moments[7],
        new_squares[0],
        new_squares[1],
        new_squares[2],
        new_squares[3],
        new_squares[4],
        new_squares[5],
        new_squares[6],
        new_squares[7],
        new_weights[0],
        new_weights[1],
        new_weights[2],
        new_weights[3],
        new_weights[4],
        new_weights[5],
        new_weights[6],
        new_weights[7],
        loss_sum,
        grad_norm,
        activity,
    )


def solution(mesh):
    return jax.shard_map(
        body,
        mesh=mesh,
        in_specs=(
            P("dp", None, None),
            P("dp", None, None),
            P("dp"),
            P("dp"),
            P("section", "dp", None),
            P("section", "dp", None),
            P("section", "dp", None),
            P("section", "dp", None),
            P("section", None, "dp"),
            P("section", "dp", None),
            P("section", None, "dp"),
            P("section", None, "dp"),
            P("section", "dp", None),
            P("section", "dp", None),
            P("section", "dp", None),
            P("section", "dp", None),
            P("section", None, "dp"),
            P("section", "dp", None),
            P("section", None, "dp"),
            P("section", None, "dp"),
            P("section", "dp", None),
            P("section", "dp", None),
            P("section", "dp", None),
            P("section", "dp", None),
            P("section", None, "dp"),
            P("section", "dp", None),
            P("section", None, "dp"),
            P("section", None, "dp"),
        ),
        out_specs=(
            P("section", "dp", None),
            P("section", "dp", None),
            P("section", "dp", None),
            P("section", "dp", None),
            P("section", None, "dp"),
            P("section", "dp", None),
            P("section", None, "dp"),
            P("section", None, "dp"),
            P("section", "dp", None),
            P("section", "dp", None),
            P("section", "dp", None),
            P("section", "dp", None),
            P("section", None, "dp"),
            P("section", "dp", None),
            P("section", None, "dp"),
            P("section", None, "dp"),
            P("section", "dp", None),
            P("section", "dp", None),
            P("section", "dp", None),
            P("section", "dp", None),
            P("section", None, "dp"),
            P("section", "dp", None),
            P("section", None, "dp"),
            P("section", None, "dp"),
            P(),
            P(),
            P(),
        ),
        check_vma=False,
    )
```

profile of v0, /device:TPU:0, one launch (start us, length us, event | category | flops | bytes accessed | tf_op | source)
XLA Modules:
  0.0 1882.8 jit_solution(6768769776255129926)
XLA Ops:
  18.3 45.1 %all-gather = bf16[1,48,768]{1,0,2:T(2,128)(2,1)S(1)} all-gather(bf16[1,48,48]{1,0,2:T(2,128)(2,1)S(1)} %copy.306), channel_id=2, replica_groups=mesh['dp'=16,'section'=2] {'dp'}, dimensions={2}, use_global_device_ids=true | all-gather | bytes 78336 | tf_op jit(solution)/shard_map/all_gather | solution.py:217
  63.8 39.2 %all-gather.2 = f32[1,6,768]{1,0,2:T(1,128)S(1)} all-gather(f32[1,6,48]{1,0,2:T(1,128)S(1)} %copy.311), channel_id=4, replica_groups=mesh['dp'=16,'section'=2] {'dp'}, dimensions={2}, use_global_device_ids=true | all-gather | bytes 19584 | tf_op jit(solution)/shard_map/all_gather | solution.py:222
  103.0 12.9 slice_reduce_fusion.1
  115.9 38.8 %all-gather.7 = bf16[1,768,96]{2,1,0:T(8,128)(2,1)S(1)} all-gather(bf16[1,48,96]{2,1,0:T(8,128)(2,1)S(1)} %convert_element_type.248), channel_id=9, replica_groups=mesh['dp'=16,'section'=2] {'dp'}, dimensions={1}, use_global_device_ids=true | all-gather | bytes 156672 | tf_op jit(solution)/shard_map/all_gather | solution.py:218
  155.9 67.6 %all-gather.14.cloned.1.call-done = f32[1,1256,768]{1,0,2:T(1,128)} async-done(((f32[1,1256,48]{1,0,2:T(1,128)}), f32[1,1256,768]{1,0,2:T(1,128)}) %all-gather.14.cloned.1.call-update) | async-done | bytes 3858448 | tf_op jit(solution)/shard_map/all_gather | solution.py:221
  225.4 6.0 copy.423
  268.3 37.5 %all-gather.20.cloned.1.call-done = bf16[1,768,3072]{2,1,0:T(8,128)(2,1)} async-done(((bf16[1,48,3072]{2,1,0:T(8,128)(2,1)}), bf16[1,768,3072]{2,1,0:T(8,128)(2,1)}) %all-gather.20.cloned.1.call-update) | async-done | bytes 4718608 | tf_op jit(solution)/shard_map/all_gather | solution.py:215
  305.8 18.9 %multiply_convert_fusion.5 = (bf16[2,256,3072]{2,1,0:T(8,128)(2,1)}, f32[2,256,3072]{2,1,0:T(8,128)}, f32[2,256,3072]{2,1,0:T(8,128)}) fusion(bf16[2,256,768]{2,1,0:T(8,128)(2,1)S(1)} %add_convert_fusion.13, bf16[768,3072]{1,0:T(8,128)(2,1)} %bitcast.546), kind=kOutput, calls=%fused_computation.65 | convolution fusion | flops 2518155264 | bytes 21233664 | tf_op jit(solution)/shard_map/jvp()/dot_general | solution.py:43
  324.7 63.5 %all-gather.22.cloned.1.call-done = bf16[1,3072,768]{2,1,0:T(8,128)(2,1)} async-done(((bf16[1,192,768]{2,1,0:T(8,128)(2,1)}), bf16[1,3072,768]{2,1,0:T(8,128)(2,1)}) %all-gather.22.cloned.1.call-update) | async-done | bytes 4718608 | tf_op jit(solution)/shard_map/all_gather | solution.py:216
  388.2 6.7 fusion.200
  426.3 18.2 multiply_convert_fusion.4
  482.0 18.4 multiply_convert_fusion.3
  508.5 9.0 add_convert_fusion.2
  568.9 8.9 add_convert_fusion.1
  619.4 9.9 add_convert_fusion
  742.2 40.6 %reduce-scatter.29.cloned.1.call-done = f32[48,6]{1,0:T(8,128)} async-done(((f32[768,6]{1,0:T(8,128)}), f32[48,6]{1,0:T(8,128)}) %reduce-scatter.29.cloned.1.call-update) | async-done | bytes 1168
  784.2 125.0 %reduce-scatter.25.cloned.1.call-done = f32[48,48]{1,0:T(8,128)} async-done(((f32[768,48]{1,0:T(8,128)}), f32[48,48]{1,0:T(8,128)}) %reduce-scatter.25.cloned.1.call-update) | async-done | bytes 9232
  910.6 124.2 %reduce-scatter.23.cloned.1.call-done = f32[48,96]{1,0:T(8,128)} async-done(((f32[768,96]{1,0:T(8,128)}), f32[48,96]{1,0:T(8,128)}) %reduce-scatter.23.cloned.1.call-update) | async-done | bytes 18448 | tf_op jit(solution)/shard_map/reduce_scatter | solution.py:269
  1036.2 131.9 %reduce-scatter.17.cloned.1.call-done = f32[48,768]{1,0:T(8,128)} async-done(((f32[768,768]{1,0:T(8,128)}), f32[48,768]{1,0:T(8,128)}) %reduce-scatter.17.cloned.1.call-update) | async-done | bytes 147472 | tf_op jit(solution)/shard_map/reduce_scatter | solution.py:265
  1169.6 137.7 %reduce-scatter.27.cloned.1.call-done = f32[48,1256]{1,0:T(8,128)} async-done(((f32[768,1256]{1,0:T(8,128)}), f32[48,1256]{1,0:T(8,128)}) %reduce-scatter.27.cloned.1.call-update) | async-done | bytes 241168
  1309.4 154.0 %reduce-scatter.15.cloned.1.call-done = f32[48,2304]{1,0:T(8,128)} async-done(((f32[768,2304]{1,0:T(8,128)}), f32[48,2304]{1,0:T(8,128)}) %reduce-scatter.15.cloned.1.call-update) | async-done | bytes 442384 | tf_op jit(solution)/shard_map/reduce_scatter | solution.py:264
  1466.4 172.3 %reduce-scatter.19.cloned.1.call-done = f32[48,3072]{1,0:T(8,128)} async-done(((f32[768,3072]{1,0:T(8,128)}), f32[48,3072]{1,0:T(8,128)}) %reduce-scatter.19.cloned.1.call-update) | async-done | bytes 589840 | tf_op jit(solution)/shard_map/reduce_scatter | solution.py:266
  1641.2 174.2 %reduce-scatter.21.cloned.1.call-done = f32[192,768]{1,0:T(8,128)} async-done(((f32[3072,768]{1,0:T(8,128)}), f32[192,768]{1,0:T(8,128)}) %reduce-scatter.21.cloned.1.call-update) | async-done | bytes 589840 | tf_op jit(solution)/shard_map/reduce_scatter | solution.py:267
  1820.6 39.2 %all-reduce.45 = (f32[]{:T(128)}, f32[]{:T(128)}, f32[2,3]{1,0:T(2,128)S(1)}) all-reduce(f32[]{:T(128)S(6)} %add.639, f32[]{:T(128)S(6)} %add.684, f32[2,3]{1,0:T(2,128)S(1)} %broadcast_select_fusion), channel_id=1, replica_groups=mesh['dp'=16,'section'=2] {'dp','section'}, use_global_device_ids=true, to_apply=%region_94.96 | all-reduce | flops 8 | bytes 64 | tf_op jit(solution)/shard_map/psum | solution.py:274
  (893 shorter events, 354.1 us)
Async XLA Ops:
  7.3 148.6 %all-gather.18.cloned.1.call-start = ((), (), s32[]{:S(2)}) async-start(), calls=%async_computation.15 | async-start | bytes 1253376 | tf_op jit(solution)/shard_map/all_gather | solution.py:214
  9.0 146.9 %all-gather.16.cloned.1.call-start = ((), (), s32[]{:S(2)}) async-start(), calls=%async_computation.14 | async-start | bytes 3760128 | tf_op jit(solution)/shard_map/all_gather | solution.py:213
  10.8 212.7 %all-gather.14.cloned.1.call-start = ((), (), s32[]{:S(2)}) async-start(), calls=%async_computation.13 | async-start | bytes 4177920 | tf_op jit(solution)/shard_map/all_gather | solution.py:221
  12.8 293.1 %all-gather.20.cloned.1.call-start = ((), (), s32[]{:S(2)}) async-start(), calls=%async_computation.16 | async-start | bytes 5013504 | tf_op jit(solution)/shard_map/all_gather | solution.py:215
  14.6 373.5 %all-gather.22.cloned.1.call-start = ((), (), s32[]{:S(2)}) async-start(), calls=%async_computation.17 | async-start | bytes 5013504 | tf_op jit(solution)/shard_map/all_gather | solution.py:216
  15.5 767.3 %reduce-scatter.29.cloned.1.call-start = ((), (), s32[]{:S(2)}) async-start(), calls=%async_computation.20 | async-start | bytes 417792
  398.2 2.2 collective-permute-start
  451.5 3.2 collective-permute-start.1
  555.0 9.8 collective-permute-start.2
  613.4 3.5 collective-permute-start.3
  661.4 247.8 %reduce-scatter.25.cloned.1.call-start = ((), (), s32[]{:S(2)}) async-start(), calls=%async_computation.18 | async-start | bytes 417792
  666.3 368.5 %reduce-scatter.23.cloned.1.call-start = ((), (), s32[]{:S(2)}) async-start(), calls=%async_computation.12 | async-start | bytes 417792 | tf_op jit(solution)/shard_map/reduce_scatter | solution.py:269
  669.3 498.8 %reduce-scatter.17.cloned.1.call-start = ((), (), s32[]{:S(2)}) async-start(), calls=%async_computation.9 | async-start | bytes 2506752 | tf_op jit(solution)/shard_map/reduce_scatter | solution.py:265
  674.0 633.4 %reduce-scatter.27.cloned.1.call-start = ((), (), s32[]{:S(2)}) async-start(), calls=%async_computation.19 | async-start | bytes 4177920
  691.6 771.7 %reduce-scatter.15.cloned.1.call-start = ((), (), s32[]{:S(2)}) async-start(), calls=%async_computation.8 | async-start | bytes 7520256 | tf_op jit(solution)/shard_map/reduce_scatter | solution.py:264
  703.7 935.0 %reduce-scatter.19.cloned.1.call-start = ((), (), s32[]{:S(2)}) async-start(), calls=%async_computation.10 | async-start | bytes 10027008 | tf_op jit(solution)/shard_map/reduce_scatter | solution.py:266
  718.0 1097.4 %reduce-scatter.21.cloned.1.call-start = ((), (), s32[]{:S(2)}) async-start(), calls=%async_computation.11 | async-start | bytes 10027008 | tf_op jit(solution)/shard_map/reduce_scatter | solution.py:267
  732.2 1128.3 %copy-start.236 = (f32[1,6,48]{2,0,1:T(1,128)S(1)}, f32[1,6,48]{2,0,1:T(1,128)}, u32[]{:S(2)}) copy-start(f32[1,6,48]{2,0,1:T(1,128)} %param.41) | copy-start | bytes 3460
  732.2 1131.4 %copy-start.168 = (f32[1,48,48]{2,1,0:T(8,128)S(1)}, f32[1,48,48]{2,1,0:T(8,128)}, u32[]{:S(2)}) copy-start(f32[1,48,48]{2,1,0:T(8,128)} %param.38) | copy-start | bytes 27652
  732.2 1132.8 %copy-start.101 = (f32[1,1256,48]{1,2,0:T(8,128)S(1)}, f32[1,1256,48]{1,2,0:T(8,128)}, u32[]{:S(2)}) copy-start(f32[1,1256,48]{1,2,0:T(8,128)} %param.40) | copy-start | bytes 723460
  732.2 1136.3 %copy-start.91 = (f32[1,192,768]{2,1,0:T(8,128)S(1)}, f32[1,192,768]{2,1,0:T(8,128)}, u32[]{:S(2)}) copy-start(f32[1,192,768]{2,1,0:T(8,128)} %param.37) | copy-start | bytes 1769476
  732.2 1136.2 %copy-start.117 = (f32[1,192,768]{2,1,0:T(8,128)S(1)}, f32[1,192,768]{2,1,0:T(8,128)}, u32[]{:S(2)}) copy-start(f32[1,192,768]{2,1,0:T(8,128)} %param.53) | copy-start | bytes 1769476
  732.2 1136.2 %copy-start.118 = (f32[1,192,768]{2,1,0:T(8,128)S(1)}, f32[1,192,768]{2,1,0:T(8,128)}, u32[]{:S(2)}) copy-start(f32[1,192,768]{2,1,0:T(8,128)} %param.45) | copy-start | bytes 1769476
  1309.4 557.7 %copy-start.170 = (f32[48,96]{1,0:T(8,128)S(1)}, f32[48,96]{1,0:T(8,128)}, u32[]{:S(2)}) copy-start(f32[48,96]{1,0:T(8,128)} %reduce-scatter.23.cloned.1.call-done) | copy-start | bytes 55300
  (281 other events, 3888.1 us)
Sparse Core Ops, SparseCore 0:
  11.5 59.5 all-gather.17
  74.4 72.4 all-gather.15
  150.3 73.1 all-gather.13
  226.7 79.0 all-gather.19
  309.0 79.0 all-gather.21
  661.5 121.2 reduce-scatter.28
  788.7 120.4 reduce-scatter.24
  914.4 120.3 reduce-scatter.22
  1040.5 127.5 reduce-scatter.16
  1173.0 134.2 reduce-scatter.26
  1312.7 150.6 reduce-scatter.14
  1468.9 169.7 reduce-scatter.18
  1645.4 170.0 reduce-scatter.20
where the time goes:
time: 1890 us; the launch traced here: 1880 us
  waiting for transfers between devices  1230 us (65%)
  matrix products  227 us (12%)
  blocking collectives  162 us (9%)
  local copies, waits for them, and re-layouts  121 us (6%)
  other arithmetic  106 us (6%)
  between operations  29.2 us (2%)
    unnamed x16, waiting for transfers between devices  304 us
    reduce_scatter x1, waiting for transfers between devices, body(): lax.psum_scatter(accum[3], 'dp', scatter_dimension=0, tiled=True)  174 us
    reduce_scatter x1, waiting for transfers between devices, body(): lax.psum_scatter(accum[2], 'dp', scatter_dimension=0, tiled=True)  172 us
    reduce_scatter x1, waiting for transfers between devices, body(): lax.psum_scatter(accum[0], 'dp', scatter_dimension=0, tiled=True)  154 us
    reduce_scatter x1, waiting for transfers between devices, body(): lax.psum_scatter(accum[1], 'dp', scatter_dimension=0, tiled=True)  132 us
    reduce_scatter x1, waiting for transfers between devices, body(): lax.psum_scatter(accum[5], 'dp', scatter_dimension=0, tiled=True)  124 us
    dot_general x24, matrix products, product_plain(): jnp.matmul(left_side.astype(jnp.bfloat16), right_side.astype(jnp.bfloat16...  93.2 us
    all_gather x1, waiting for transfers between devices, body(): lax.all_gather(w_embed[0], 'dp', axis=1, tiled=True)  67.6 us
  transfers between devices with their start and end apart: 17, of which 13 were waited for; matrix products, arithmetic and copies ran while one was open for 9% of the time, Pallas kernels for 0%

commit v1 on v0

v1 whole, which is shorter than its diff:
```python
import math

import jax
import jax.numpy as jnp
from jax import lax
from jax.experimental import pallas as pl
from jax.experimental.pallas import tpu as pltpu
from jax.sharding import PartitionSpec as P

D = 768
H = 12
HD = 64
FF = 3072
PD = 48
CLS = 1000
P_SIZE = 256
STEP = 10
QKV = 3 * D

EPS_NORM = 1e-05
NOISE_SCALE = 0.05
CLIP_NORM = 0.001
BETA_ONE = 0.9
BETA_TWO = 0.95
LEARN_RATES = (0.01, 0.06, 0.01, 0.01, 0.08, 0.01, 0.25, 0.4)
WEIGHT_DECAY = 0.1
EPS_ADAM = 1e-10

BF = jnp.bfloat16
F32 = jnp.float32

S_HEAD = 2 * P_SIZE
S_NORM = S_HEAD + 2 * PD
S_IN = S_HEAD + 128
S_WIDTH = 768
FIRST_WIDTH = S_WIDTH + QKV + D
PAIR = 2 * HD
PAIRS = H // 2
TILE = 512
VMEM_BYTES = 56 << 20


def swap_pairs(count, bit):
    return [(source, source ^ (1 << bit)) for source in range(count)]


def exchange(value, axis, bit=0):
    return lax.ppermute(value, axis, swap_pairs(lax.axis_size(axis), bit))


def dp_bits():
    return lax.axis_size("dp").bit_length() - 1


def parity_of(bit):
    return (lax.axis_index("dp") >> bit) & 1


GATHER_ORDERS = ({"first": (0, 1, 2, 3), "up": (1, 2, 3, 0), "down": (2, 0, 1, 3)},)
SCATTER_ORDERS = (
    {"down": (0, 2, 1, 3), "up": (1, 2, 0, 3), "first": (0, 1, 2, 3), "last": (1, 2, 0, 3)},
    {"first": (2, 0, 3, 1)},
)


BY_COLLECTIVE = ((), ("down", "up"))
SPLIT = (0, "first")


def order_from(table, block, name):
    count = dp_bits()
    if count == 4:
        return table[block][name]
    first = {"first": 0, "up": 1, "down": 2, "last": 1}[name]
    return tuple((first + step) % count for step in range(count))


class Sequencer:
    def __init__(self):
        self.flights = []
        self.asked = []
        self.token = jnp.zeros((), F32)

    def tie(self, tree):
        leaves, kind = jax.tree.flatten(tree)
        tied = lax.optimization_barrier([self.token] + leaves)
        self.token = tied[0]
        return jax.tree.unflatten(kind, tied[1:])

    def launch(self, steps):
        flight = {"steps": steps, "done": False}
        self.asked.append((flight, next(steps)))
        return flight

    def turn(self):
        requests = []
        for flight, got in zip(self.flights, self.tie([flight["got"] for flight in self.flights])):
            try:
                requests.append((flight, flight["steps"].send(got)))
            except StopIteration as stop:
                flight["done"] = True
                flight["result"] = stop.value
        requests += self.asked
        values = self.tie([value for _, (value, _, _) in requests])
        self.flights, self.asked = [], []
        for value, (flight, (_, axis, bit)) in zip(values, requests):
            flight["got"] = exchange(value, axis, bit)
            self.flights.append(flight)

    def wait(self, *flights):
        while not all(flight["done"] for flight in flights):
            self.turn()
        return flights[0]["result"] if len(flights) == 1 else [f["result"] for f in flights]

    def compute(self, function, *values):
        return self.tie(function(*self.tie(values)))


def gather_steps(part, order):
    have = []
    held = part
    for bit in reversed(order):
        other = yield (held, "dp", bit)
        place = sum(1 for b in have if b > bit)
        swap = parity_of(bit) == 1
        held = jnp.stack([jnp.where(swap, other, held), jnp.where(swap, held, other)], axis=place)
        have.append(bit)
    return held.reshape((-1,) + part.shape[1:])


def weight_steps(part, order):
    mine = yield from gather_steps(part, order)
    other = yield (mine, "section", 0)
    return mine, other


def pair_steps(mine):
    other = yield (mine, "section", 0)
    return mine, other


def part_of(value, axis_index):
    starts = [axis_index.get(axis, 0) for axis in range(value.ndim)]
    sizes = [1 if axis in axis_index else extent for axis, extent in enumerate(value.shape)]
    sliced = lax.dynamic_slice(value, starts, sizes)
    return sliced.reshape([extent for axis, extent in enumerate(sizes) if axis not in axis_index])


def scatter_steps(mine, given, order):
    other = yield (given, "section", 0)
    result = yield from scatter_both((mine, other), order)
    return result


def scatter_both(both, order):
    count = dp_bits()
    rows = both[0].shape[0] >> count
    held = [value.reshape((2,) * count + (rows,) + value.shape[1:]) for value in both]
    left = sorted(range(count), reverse=True)
    chosen = [{} for _ in held]

    def piece(axis, index):
        parts = []
        for value, fixed in zip(held, chosen):
            free = [place for place in range(value.ndim) if place not in fixed]
            parts.append(part_of(value, {**fixed, free[axis]: index}).astype(F32))
        return sum(parts[1:], parts[0])

    for bit in order:
        axis = left.index(bit)
        parity = parity_of(bit)
        other = yield (piece(axis, 1 - parity).astype(BF), "dp", bit)
        for value, fixed in zip(held, chosen):
            free = [place for place in range(value.ndim) if place not in fixed]
            fixed[free[axis]] = parity
        if len(held) > 1:
            kept = sum(part_of(value, fixed).astype(F32) for value, fixed in zip(held, chosen))
            held, chosen = [kept.astype(BF)], [{}]
        held.append(other)
        chosen.append({})
        left.remove(bit)
    return sum(part_of(value, fixed).astype(F32) for value, fixed in zip(held, chosen))


def one_step(value, axis, bit=0):
    got = yield (value, axis, bit)
    return got


def one_pair(mine):
    other = yield (mine, "section", 0)
    return mine, other


def sum_pair(mine, given):
    other = yield (given, "section", 0)
    return mine, other


def down_columns(rows, width):
    count = rows.shape[0] // width
    return rows.reshape(count, width, D).transpose(1, 0, 2).reshape(width, count * D)


def down_rows(columns, width):
    count = columns.shape[1] // D
    return columns.reshape(-1, width, count, D).transpose(0, 2, 1, 3).reshape(-1, D)


def label_steps(labels):
    gathered = yield from gather_steps(labels[None], tuple(range(dp_bits())))
    return gathered.reshape(-1)


def class_steps(own, is_first, order):
    other = yield (own, "section", 0)
    both = jnp.concatenate([jnp.where(is_first, own, other), jnp.where(is_first, other, own)], axis=1)
    whole = yield from gather_steps(both, order)
    return whole


def sum_steps(values):
    other = yield (values, "section", 0)
    values = values + other
    for bit in range(dp_bits()):
        other = yield (values, "dp", bit)
        values = values + other
    return values


def dot(left, right):
    return lax.dot_general(left, right, (((1,), (0,)), ((), ())), preferred_element_type=F32)


def dot_nt(left, right):
    return lax.dot_general(left, right, (((1,), (1,)), ((), ())), preferred_element_type=F32)


def dot_tn(left, right):
    return lax.dot_general(left, right, (((0,), (0,)), ((), ())), preferred_element_type=F32)


def two_terms(value):
    high = lax.optimization_barrier(value.astype(BF))
    return high, (value - high.astype(F32)).astype(BF)


def three_terms(value):
    high = lax.optimization_barrier(value.astype(BF))
    return (high,) + two_terms(value - high.astype(F32))


def whole_spec(*shape):
    return pl.BlockSpec(shape, lambda *_: (0,) * len(shape))


def row_spec(width):
    return pl.BlockSpec((P_SIZE, width), lambda j: (j, 0))


def first_spec(index):
    return pl.BlockSpec((D, D), lambda *_: (0, index))


HEAD_SPEC = pl.BlockSpec((D, 128), lambda *_: (0, S_HEAD // 128))
IN_SPEC = pl.BlockSpec((D, 128), lambda *_: (0, S_IN // 128))


def shape_of(rows, columns, kind=F32):
    return jax.ShapeDtypeStruct((rows, columns), kind)


def call(kernel, name, flops, **fields):
    return pl.pallas_call(
        kernel,
        name=name,
        cost_estimate=pl.CostEstimate(flops=flops, bytes_accessed=flops // 256, transcendentals=0),
        compiler_params=pltpu.CompilerParams(vmem_limit_bytes=VMEM_BYTES),
        **fields,
    )


def iotas(rows, columns):
    return (
        lax.broadcasted_iota(jnp.int32, (rows, columns), 0),
        lax.broadcasted_iota(jnp.int32, (rows, columns), 1),
    )


def where_ones(condition):
    return jnp.where(condition, 1.0, 0.0).astype(BF)


def norm_parts(values):
    center = values - jnp.mean(values, axis=-1, keepdims=True)
    scale = lax.rsqrt(jnp.mean(center * center, axis=-1, keepdims=True) + EPS_NORM)
    return center, scale


def norm_rows(values, norms, which):
    center, scale = norm_parts(values)
    return (center * scale * norms[2 * which : 2 * which + 1] + norms[2 * which + 1 : 2 * which + 2]).astype(BF)


def norm_back_rows(values, norms, which, cotangent):
    center, scale = norm_parts(values)
    unit = center * scale
    inner = cotangent * norms[2 * which : 2 * which + 1]
    first = jnp.mean(inner, axis=-1, keepdims=True)
    second = jnp.mean(inner * unit, axis=-1, keepdims=True)
    gain_grad = jnp.sum(cotangent * unit, axis=0, keepdims=True)
    offset_grad = jnp.sum(cotangent, axis=0, keepdims=True)
    return scale * (inner - first - unit * second), gain_grad, offset_grad


def add_sums(sums_ref, *rows):
    @pl.when(pl.program_id(0) == 0)
    def _():
        sums_ref[...] = jnp.zeros_like(sums_ref)

    for index, row in enumerate(rows):
        sums_ref[index : index + 1, :] += row


def begin_kernel(x_ref, class_ref, small_ref, q_ref, k_ref, v_ref, hidden_ref, normed_ref, joint_ref, norms_ref):
    row, column = iotas(P_SIZE, P_SIZE)
    same = where_ones(row == column)
    hidden = dot_nt(same, small_ref[:, :P_SIZE]) + dot_nt(same, small_ref[:, P_SIZE:S_HEAD])
    hidden = hidden + dot_nt(x_ref[...].astype(BF), small_ref[:, S_IN : S_IN + PD])
    hidden = hidden + class_ref[pl.ds(pl.program_id(0), 1), :]
    row, column = iotas(8, 128)
    place = column - 2 * PD
    term = where_ones((row < 6) & ((place == row) | (place == row + 6) | (place == row + 12)))
    norms = dot_nt(term, small_ref[:, S_HEAD : S_HEAD + 128])
    hidden_ref[...] = hidden
    norms_ref[...] = norms
    normed = norm_rows(hidden, norms, 0)
    normed_ref[...] = normed
    for part, weight_ref in enumerate((q_ref, k_ref, v_ref)):
        joint_ref[:, part * D : (part + 1) * D] = dot(normed, weight_ref[...]).astype(BF)


def begin(inputs, classes, first):
    rows = inputs.shape[0]
    return call(
        begin_kernel,
        "embed_norm_project",
        2 * rows * D * 4 * D,
        grid=(rows // P_SIZE,),
        in_specs=[row_spec(PD), whole_spec(*classes.shape)] + [first_spec(part) for part in range(4)],
        out_specs=[row_spec(D), row_spec(D), row_spec(QKV), whole_spec(8, D)],
        out_shape=[shape_of(rows, D), shape_of(rows, D, BF), shape_of(rows, QKV, BF), shape_of(8, D)],
    )(inputs, classes, first, first, first, first)


def attention_end_kernel(attended_ref, weight_ref, hidden_ref, norms_ref, middle_ref, normed_ref, sums_ref):
    branch = dot(attended_ref[...], weight_ref[...])
    middle = hidden_ref[...] + branch
    middle_ref[...] = middle
    normed_ref[...] = norm_rows(middle, norms_ref[...], 1)
    add_sums(sums_ref, jnp.sum(branch * branch, axis=0, keepdims=True))


def attention_end(attended, first, hidden, norms):
    rows = attended.shape[0]
    return call(
        attention_end_kernel,
        "attention_end",
        2 * rows * D * D,
        grid=(rows // P_SIZE,),
        in_specs=[row_spec(D), first_spec(4), row_spec(D), whole_spec(8, D)],
        out_specs=[row_spec(D), row_spec(D), whole_spec(8, D)],
        out_shape=[shape_of(rows, D), shape_of(rows, D, BF), shape_of(8, D)],
    )(attended, first, hidden, norms)


def half_steps(columns):
    count = columns // TILE
    return 2 * count, lambda j: jnp.minimum(j, count - 1), lambda j: jnp.maximum(j - count, 0), count


def up_kernel(count, x_ref, one_ref, two_ref, active_one, active_two, slope_one, slope_two):
    def half(weight_ref, active_ref, slope_ref):
        u = dot(x_ref[...], weight_ref[...])
        t = pl.reciprocal(1.0 + (0.3275911 / math.sqrt(2.0)) * jnp.abs(u), approx=True)
        bell = jnp.exp(-0.5 * u * u)
        poly = t * (0.127414796 + t * (-0.142248368 + t * (0.7107068705 + t * (-0.7265760135 + t * 0.5307027145))))
        tail = poly * bell
        share = jnp.where(u >= 0, 1.0 - tail, tail)
        active_ref[...] = (u * share).astype(BF)
        slope_ref[...] = (share + u * bell * (1.0 / math.sqrt(2.0 * math.pi))).astype(BF)

    @pl.when(pl.program_id(0) < count)
    def _():
        half(one_ref, active_one, slope_one)

    @pl.when(pl.program_id(0) >= count)
    def _():
        half(two_ref, active_two, slope_two)


def up_halves(normed, one, two):
    rows, columns = normed.shape[0], one.shape[1]
    steps, at_one, at_two, count = half_steps(columns)
    tiles = [lambda j: (0, at_one(j)), lambda j: (0, at_two(j))]
    return call(
        lambda *refs: up_kernel(count, *refs),
        "up_gelu",
        4 * rows * D * columns,
        grid=(steps,),
        in_specs=[whole_spec(rows, D)] + [pl.BlockSpec((D, TILE), tile) for tile in tiles],
        out_specs=[pl.BlockSpec((rows, TILE), tile) for tile in tiles * 2],
        out_shape=[shape_of(rows, columns, BF)] * 4,
    )(normed, one, two)


def end_kernel(
    active_one, active_two, down_one, down_two, middle_ref, norms_ref, head_ref, x_ref,
    final_ref, normed_ref, shrink_ref, latent_ref, sums_ref,
):
    branch = dot(active_one[...], down_one[...]) + dot(active_two[...], down_two[...])
    final = middle_ref[...] + branch
    final_ref[...] = final
    normed = norm_rows(final, norms_ref[...], 2)
    normed_ref[...] = normed
    head_out = dot(normed, head_ref[...])
    row, _ = iotas(P_SIZE, 128)
    moved = jnp.where(row == 0, 0.0, pltpu.roll(head_out, 1, 0))
    log_scale = moved[:, PD : 2 * PD]
    shrink = jnp.exp(-log_scale)
    shrink_ref[...] = shrink
    latent_ref[...] = (x_ref[...] - moved[:, :PD]) * shrink
    _, lane = iotas(1, D)
    add_sums(
        sums_ref,
        jnp.sum(final * final, axis=0, keepdims=True),
        jnp.sum(branch * branch, axis=0, keepdims=True),
        jnp.where(lane == 0, jnp.sum(log_scale), 0.0),
    )


def end(actives, downs, middle, norms, first, inputs):
    rows, columns = actives[0].shape
    return call(
        end_kernel,
        "down_norm_head",
        4 * rows * D * columns,
        grid=(rows // P_SIZE,),
        in_specs=[row_spec(columns)] * 2
        + [whole_spec(columns, D)] * 2
        + [row_spec(D), whole_spec(8, D), HEAD_SPEC, row_spec(PD)],
        out_specs=[row_spec(D), row_spec(D), row_spec(PD), row_spec(PD), whole_spec(8, D)],
        out_shape=[
            shape_of(rows, D), shape_of(rows, D, BF), shape_of(rows, PD), shape_of(rows, PD), shape_of(8, D)
        ],
    )(*actives, *downs, middle, norms, first, inputs)


def head_back_kernel(
    coefficient, latent_grad_ref, shrink_ref, latent_ref, final_ref, norms_ref, head_ref, normed_ref,
    through_ref, flow_ref, low_ref, weight_ref, sums_ref,
):
    latent_grad = latent_grad_ref[...]
    through = latent_grad * shrink_ref[...]
    through_ref[...] = through
    scale_grad = coefficient - latent_grad * latent_ref[...]
    row, column = iotas(PD, 128)
    placed = dot((-through).astype(BF), where_ones(row == column))
    placed = placed + dot(scale_grad.astype(BF), where_ones(row + PD == column))
    row, _ = iotas(P_SIZE, 128)
    head_grad = jnp.where(row == P_SIZE - 1, 0.0, pltpu.roll(placed, P_SIZE - 1, 0)).astype(BF)
    flow, gain_grad, offset_grad = norm_back_rows(
        final_ref[...], norms_ref[...], 2, dot_nt(head_grad, head_ref[...])
    )
    flow_ref[...] = flow
    low_ref[...] = flow.astype(BF)

    @pl.when(pl.program_id(0) == 0)
    def _():
        weight_ref[...] = jnp.zeros_like(weight_ref)

    weight_ref[...] += dot_tn(normed_ref[...], head_grad)
    add_sums(sums_ref, gain_grad, offset_grad)


def head_back(coefficient, latent_grad, shrink, latent, final, norms, first, normed):
    rows = final.shape[0]
    return call(
        lambda *refs: head_back_kernel(coefficient, *refs),
        "head_back",
        4 * rows * D * 128,
        grid=(rows // P_SIZE,),
        in_specs=[row_spec(PD)] * 3 + [row_spec(D), whole_spec(8, D), HEAD_SPEC, row_spec(D)],
        out_specs=[row_spec(PD), row_spec(D), row_spec(D), whole_spec(D, 128), whole_spec(8, D)],
        out_shape=[
            shape_of(rows, PD), shape_of(rows, D), shape_of(rows, D, BF), shape_of(D, 128), shape_of(8, D)
        ],
    )(latent_grad, shrink, latent, final, norms, first, normed)


def down_grad_kernel(count, one_ref, two_ref, low_ref, out_one, out_two):
    @pl.when(pl.program_id(0) < count)
    def _():
        out_one[...] = dot_tn(one_ref[...], low_ref[...]).astype(BF)

    @pl.when(pl.program_id(0) >= count)
    def _():
        out_two[...] = dot_tn(two_ref[...], low_ref[...]).astype(BF)


def down_grads(one, two, low):
    rows, columns = one.shape
    steps, at_one, at_two, count = half_steps(columns)
    return call(
        lambda *refs: down_grad_kernel(count, *refs),
        "down_weight_grad",
        4 * rows * D * columns,
        grid=(steps,),
        in_specs=[
            pl.BlockSpec((rows, TILE), lambda j: (0, at_one(j))),
            pl.BlockSpec((rows, TILE), lambda j: (0, at_two(j))),
            whole_spec(rows, D),
        ],
        out_specs=[
            pl.BlockSpec((TILE, D), lambda j: (at_one(j), 0)),
            pl.BlockSpec((TILE, D), lambda j: (at_two(j), 0)),
        ],
        out_shape=[shape_of(columns, D, BF)] * 2,
    )(one, two, low)


def up_back_kernel(count, low_ref, normed_ref, *refs):
    def half(weight_ref, slope_ref, grad_ref, out_ref):
        grad = (dot_nt(low_ref[...], weight_ref[...]) * slope_ref[...].astype(F32)).astype(BF)
        grad_ref[...] = grad
        out_ref[...] = dot_tn(normed_ref[...], grad).astype(BF)

    @pl.when(pl.program_id(0) < count)
    def _():
        half(*refs[0::2])

    @pl.when(pl.program_id(0) >= count)
    def _():
        half(*refs[1::2])


def up_back(low, normed, downs, slopes):
    rows, columns = slopes[0].shape
    steps, at_one, at_two, count = half_steps(columns)
    by_column = [lambda j: (0, at_one(j)), lambda j: (0, at_two(j))]
    by_row = [lambda j: (at_one(j), 0), lambda j: (at_two(j), 0)]
    tiles = [pl.BlockSpec((rows, TILE), tile) for tile in by_column]
    return call(
        lambda *refs: up_back_kernel(count, *refs),
        "up_back",
        8 * rows * D * columns,
        grid=(steps,),
        in_specs=[whole_spec(rows, D)] * 2 + [pl.BlockSpec((TILE, D), tile) for tile in by_row] + tiles,
        out_specs=tiles + [pl.BlockSpec((D, TILE), tile) for tile in by_column],
        out_shape=[shape_of(rows, columns, BF)] * 2 + [shape_of(D, columns, BF)] * 2,
    )(low, normed, *downs, *slopes)


def middle_back_kernel(
    one_ref, two_ref, up_one, up_two, middle_ref, norms_ref, above_ref, weight_ref,
    wide_ref, low_ref, attended_ref, sums_ref,
):
    back = dot_nt(one_ref[...], up_one[...]) + dot_nt(two_ref[...], up_two[...])
    flow, gain_grad, offset_grad = norm_back_rows(middle_ref[...], norms_ref[...], 1, back)
    total = above_ref[...] + flow
    wide_ref[...] = total
    low = total.astype(BF)
    low_ref[...] = low
    attended_ref[...] = dot_nt(low, weight_ref[...]).astype(BF)
    add_sums(sums_ref, gain_grad, offset_grad)


def middle_back(grads, ups, middle, norms, above, first):
    rows, columns = grads[0].shape
    return call(
        middle_back_kernel,
        "middle_back",
        4 * rows * D * columns,
        grid=(rows // P_SIZE,),
        in_specs=[row_spec(columns)] * 2
        + [whole_spec(D, columns)] * 2
        + [row_spec(D), whole_spec(8, D), row_spec(D), first_spec(4)],
        out_specs=[row_spec(D), row_spec(D), row_spec(D), whole_spec(8, D)],
        out_shape=[shape_of(rows, D), shape_of(rows, D, BF), shape_of(rows, D, BF), shape_of(8, D)],
    )(*grads, *ups, middle, norms, above, first)


def input_back_kernel(
    joint_ref, q_ref, k_ref, v_ref, hidden_ref, norms_ref, above_ref, in_ref, through_ref, low_ref, out_ref, sums_ref
):
    back = sum(
        dot_nt(joint_ref[:, part * D : (part + 1) * D], weight_ref[...])
        for part, weight_ref in enumerate((q_ref, k_ref, v_ref))
    )
    flow, gain_grad, offset_grad = norm_back_rows(hidden_ref[...], norms_ref[...], 0, back)
    low = (above_ref[...] + flow).astype(BF)
    low_ref[...] = low
    out_ref[...] = through_ref[...] + dot(low, in_ref[...])[:, :PD]
    add_sums(sums_ref, gain_grad, offset_grad)


def input_back(joint_grad, first, hidden, norms, above, through):
    rows = hidden.shape[0]
    return call(
        input_back_kernel,
        "input_back",
        2 * rows * D * QKV,
        grid=(rows // P_SIZE,),
        in_specs=[row_spec(QKV)]
        + [first_spec(part) for part in range(1, 4)]
        + [row_spec(D), whole_spec(8, D), row_spec(D), IN_SPEC, row_spec(PD)],
        out_specs=[row_spec(D), row_spec(PD), whole_spec(8, D)],
        out_shape=[shape_of(rows, D, BF), shape_of(rows, PD), shape_of(8, D)],
    )(joint_grad, first, first, first, hidden, norms, above, first, through)


COLUMNS = 256
SOURCE_AT = (QKV + D) // COLUMNS


def first_grad_kernel(
    steps, section_ref, normed_ref, attended_ref, low_ref, joint_ref, middle_ref, source_ref, head_ref,
    sums_one, sums_two, sums_three, mine_ref, given_ref,
):
    step = pl.program_id(0)
    to_mine = (step >= steps // 2) == (section_ref[0] == 1)

    def put(value):
        @pl.when(to_mine)
        def _():
            mine_ref[...] = value

        @pl.when(jnp.logical_not(to_mine))
        def _():
            given_ref[...] = value

    @pl.when(step < QKV // COLUMNS)
    def _():
        put(dot_tn(normed_ref[...], joint_ref[...]).astype(BF))

    @pl.when((step >= QKV // COLUMNS) & (step < SOURCE_AT))
    def _():
        put(dot_tn(attended_ref[...], middle_ref[...]).astype(BF))

    @pl.when((step >= SOURCE_AT) & (step < steps - 1))
    def _():
        put(dot_tn(low_ref[...], source_ref[...]).astype(BF))

    @pl.when(step == steps - 1)
    def _():
        row, column = iotas(8, 128)
        rest = head_ref[...]
        for which, sums_ref in enumerate((sums_one, sums_two, sums_three)):
            place = where_ones((row < 2) & (column == row + 2 * PD + 2 * which))
            rest = rest + dot_tn(sums_ref[...].astype(BF), place)
        source = dot_tn(low_ref[...], source_ref[:, :128])
        put(jnp.concatenate([source, rest], axis=1).astype(BF))


def first_grads(section, normed, attended, low, joint_grad, low_middle, sources, head, sums):
    rows = normed.shape[0]
    steps = SOURCE_AT + sources.shape[1] // COLUMNS
    half = steps // 2

    def tile(offset, count):
        return pl.BlockSpec((rows, COLUMNS), lambda j, s: (0, jnp.clip(j - offset, 0, count - 1)))

    whole = pl.BlockSpec((rows, D), lambda j, s: (0, 0))
    small = pl.BlockSpec((8, D), lambda j, s: (0, 0))
    return call(
        lambda *refs: first_grad_kernel(steps, *refs),
        "first_weight_grad",
        2 * rows * D * (QKV + D + sources.shape[1]),
        grid_spec=pltpu.PrefetchScalarGridSpec(
            num_scalar_prefetch=1,
            grid=(steps,),
            in_specs=[
                whole,
                whole,
                whole,
                tile(0, QKV // COLUMNS),
                tile(QKV // COLUMNS, D // COLUMNS),
                tile(SOURCE_AT, sources.shape[1] // COLUMNS),
                pl.BlockSpec((D, 128), lambda j, s: (0, 0)),
                small,
                small,
                small,
            ],
            out_specs=[
                pl.BlockSpec((D, COLUMNS), lambda j, s: (0, jnp.clip(j - half * s[0], 0, half - 1))),
                pl.BlockSpec((D, COLUMNS), lambda j, s: (0, jnp.clip(j - half * (1 - s[0]), 0, half - 1))),
            ],
        ),
        out_shape=[shape_of(D, half * COLUMNS, BF)] * 2,
    )(section[None].astype(jnp.int32), normed, attended, low, joint_grad, low_middle, sources, head, *sums)


def head_mask(which, axis, scale=1.0):
    shape = (1, PAIR) if axis == 1 else (PAIR, 1)
    place = lax.broadcasted_iota(jnp.int32, shape, axis)
    return jnp.where((place >= HD * which) & (place < HD * (which + 1)), scale, 0.0).astype(BF)


def attend_kernel(q_ref, k_ref, v_ref, out_ref, probs_ref):
    queries, key_rows = q_ref[...], k_ref[...]
    values_t = v_ref[...].T
    key_at = lax.broadcasted_iota(jnp.int32, (P_SIZE, P_SIZE), 0)
    query_at = lax.broadcasted_iota(jnp.int32, (P_SIZE, P_SIZE), 1)
    causal = key_at <= query_at
    total = jnp.zeros((PAIR, P_SIZE), F32)
    for which in range(2):
        scores = dot_nt(key_rows, queries * head_mask(which, 1, HD ** (-0.5)))
        scores = jnp.where(causal, scores, -1e30)
        exps = jnp.exp(scores - jnp.max(scores, axis=0, keepdims=True))
        probs = (exps * (1.0 / jnp.sum(exps, axis=0, keepdims=True))).astype(BF)
        probs_ref[0, which] = probs
        total = total + dot(values_t * head_mask(which, 0), probs)
    out_ref[...] = total.T.astype(BF)


def attend(joint):
    count = joint.shape[0] // P_SIZE
    part = [pl.BlockSpec((P_SIZE, PAIR), lambda n, p, s=s: (n, s * PAIRS + p)) for s in range(3)]
    return pl.pallas_call(
        attend_kernel,
        grid=(count, PAIRS),
        in_specs=part,
        out_specs=[
            pl.BlockSpec((P_SIZE, PAIR), lambda n, p: (n, p)),
            pl.BlockSpec((1, 2, P_SIZE, P_SIZE), lambda n, p: (n, p, 0, 0)),
        ],
        out_shape=[
            jax.ShapeDtypeStruct((joint.shape[0], D), BF),
            jax.ShapeDtypeStruct((count, H, P_SIZE, P_SIZE), BF),
        ],
        cost_estimate=pl.CostEstimate(
            flops=8 * count * H * P_SIZE * P_SIZE * HD,
            bytes_accessed=2 * count * H * P_SIZE * P_SIZE + 8 * joint.shape[0] * D,
            transcendentals=count * H * P_SIZE * P_SIZE,
        ),
        compiler_params=pltpu.CompilerParams(vmem_limit_bytes=VMEM_BYTES),
        name="attention",
    )(joint, joint, joint)


def attend_back_kernel(q_ref, k_ref, v_ref, probs_ref, grad_ref, out_ref):
    pair = pl.program_id(1)
    queries, value_rows, grad = q_ref[...], v_ref[...], grad_ref[...]
    keys_t = k_ref[...].T
    query_grad = jnp.zeros((PAIR, P_SIZE), F32)
    key_grad = jnp.zeros((P_SIZE, PAIR), F32)
    value_grad = jnp.zeros((P_SIZE, PAIR), F32)
    for which in range(2):
        mask = head_mask(which, 1)
        probs = probs_ref[0, which]
        own_grad = grad * mask
        value_grad = value_grad + dot(probs, own_grad)
        prob_grad = dot_nt(value_rows, own_grad)
        wide = probs.astype(F32)
        total = jnp.sum(wide * prob_grad, axis=0, keepdims=True)
        score_grad = (wide * (prob_grad - total) * HD ** (-0.5)).astype(BF)
        key_grad = key_grad + dot(score_grad, queries * mask)
        query_grad = query_grad + dot(keys_t * head_mask(which, 0), score_grad)
    for part, value in enumerate((query_grad.T, key_grad, value_grad)):
        out_ref[:, pl.ds(pl.multiple_of(part * D + pair * PAIR, PAIR), PAIR)] = value.astype(BF)


def attend_back(joint, probs, grad):
    count = joint.shape[0] // P_SIZE
    part = [pl.BlockSpec((P_SIZE, PAIR), lambda n, p, s=s: (n, s * PAIRS + p)) for s in range(3)]
    return pl.pallas_call(
        attend_back_kernel,
        grid=(count, PAIRS),
        in_specs=part
        + [
            pl.BlockSpec((1, 2, P_SIZE, P_SIZE), lambda n, p: (n, p, 0, 0)),
            pl.BlockSpec((P_SIZE, PAIR), lambda n, p: (n, p)),
        ],
        out_specs=pl.BlockSpec((P_SIZE, QKV), lambda n, p: (n, 0)),
        out_shape=jax.ShapeDtypeStruct(joint.shape, BF),
        cost_estimate=pl.CostEstimate(
            flops=16 * count * H * P_SIZE * P_SIZE * HD,
            bytes_accessed=2 * count * H * P_SIZE * P_SIZE + 14 * joint.shape[0] * D,
            transcendentals=0,
        ),
        compiler_params=pltpu.CompilerParams(vmem_limit_bytes=VMEM_BYTES),
        name="attention_back",
    )(joint, joint, joint, probs, grad)


def place_halves(is_first, mine, other):
    return jnp.concatenate(
        [jnp.where(is_first, mine, other), jnp.where(is_first, other, mine)], axis=1
    )


def block_forward(seq, is_first, flights, classes, inputs, picks, between=lambda: None):
    count = inputs.shape[0] // P_SIZE
    first = seq.compute(place_halves, is_first, *seq.wait(flights["first"]))
    own = dot_nt(jnp.concatenate([picks, picks], axis=1), classes)
    hidden, normed_one, joint, norms = seq.compute(begin, inputs, own, first)
    attended, probs = seq.compute(attend, joint)
    middle, normed_two, sums_two = seq.compute(attention_end, attended, first, hidden, norms)
    ups = seq.wait(flights["up"])
    *actives, slope_one, slope_two = seq.compute(up_halves, normed_two, *ups)
    between()
    seq.turn()
    downs = seq.wait(flights["down"])
    final, normed_three, shrink, latent, sums = seq.compute(end, actives, downs, middle, norms, first, inputs)
    saved = dict(
        first=first, ups=ups, downs=downs, inputs=inputs, hidden=hidden, normed_one=normed_one, joint=joint,
        norms=norms, attended=attended, probs=probs, middle=middle, normed_two=normed_two, actives=actives,
        slopes=(slope_one, slope_two), final=final, normed_three=normed_three, shrink=shrink, latent=latent,
    )
    squares = jnp.stack([jnp.sum(sums[0]), jnp.sum(sums_two[0]), jnp.sum(sums[1]), jnp.sum(sums[2])])
    return saved, squares


def part_scattered(pieces, block, scattered):
    scattered = scattered.astype(F32)
    place = 0
    for name in BY_COLLECTIVE[block]:
        shape = pieces[name]["result"][0].shape
        height = shape[0] // lax.axis_size("dp")
        columns = []
        for _ in range(0, shape[1], D):
            columns.append(scattered[place : place + height])
            place += height
        pieces[name] = {"done": True, "result": jnp.concatenate(columns, axis=1)}


def block_backward(seq, section, block, saved, picks, latent_grad, coefficient, pieces):
    count = latent_grad.shape[0] // P_SIZE
    first, norms = saved["first"], saved["norms"]

    def launch(name, mine, given):
        if name in BY_COLLECTIVE[block] or (block, name) == SPLIT:
            pieces[name] = seq.launch(sum_pair(mine, given))
            return
        order = order_from(SCATTER_ORDERS, block, name)
        pieces[name] = seq.launch(scatter_steps(mine, given, order))

    def scatter_summed():
        rows = []
        for name in BY_COLLECTIVE[block]:
            mine, other = (value.reshape(lax.axis_size("dp"), -1, *value.shape[1:]) for value in pieces[name]["result"])
            total = (mine.astype(F32) + other.astype(F32)).astype(BF)
            rows += [total[:, :, start : start + D] for start in range(0, total.shape[2], D)]
        whole = jnp.concatenate(rows, axis=1)
        return lax.psum_scatter(seq.tie(whole), "dp", scatter_dimension=0, tiled=False)

    through, flow, low_final, head_grad, sums_three = seq.compute(
        lambda grad: head_back(
            coefficient, grad, saved["shrink"], saved["latent"], saved["final"], norms, first, saved["normed_three"]
        ),
        latent_grad,
    )
    launch("down", *seq.compute(down_grads, *saved["actives"], low_final))
    if block == 0:
        seq.turn()
    grad_one, grad_two, *up_grads = seq.compute(
        lambda low: up_back(low, saved["normed_two"], saved["downs"], saved["slopes"]), low_final
    )
    launch("up", *up_grads)
    if block == 1:
        seq.turn()
    wide_middle, low_middle, attended_grad, sums_two = seq.compute(
        lambda one, two: middle_back((one, two), saved["ups"], saved["middle"], norms, flow, first), grad_one, grad_two
    )
    if block == 0:
        seq.turn()
    joint_grad = seq.compute(attend_back, saved["joint"], saved["probs"], attended_grad)
    if block == 1:
        seq.turn()
        pieces["scattered"] = scatter_summed()
    low_hidden, input_grad, sums_one = seq.compute(
        lambda grad: input_back(grad, first, saved["hidden"], norms, wide_middle, through), joint_grad
    )
    places = jnp.tile(jnp.eye(P_SIZE, dtype=BF), (count, 1))
    sources = jnp.concatenate(
        [places, saved["inputs"].astype(BF), jnp.repeat(picks, P_SIZE, axis=0)], axis=1
    )
    sources = jnp.pad(sources, ((0, 0), (0, 128 + -(sources.shape[1] + 128) % 512)))
    launch(
        "first",
        *seq.compute(
            lambda low: first_grads(
                section, saved["normed_one"], saved["attended"], low, joint_grad, low_middle, sources, head_grad,
                (sums_one, sums_two, sums_three),
            ),
            low_hidden,
        ),
    )
    return input_grad


def body(*arguments):
    images, noise_draw, labels, class_drop = arguments[:4]
    weights, moments, squares = arguments[4:12], arguments[12:20], arguments[20:28]
    w_qkv, w_attn, w_up, w_down, w_in, w_head, w_embed, w_norms = (w[0] for w in weights)
    count_dp = lax.axis_size("dp")
    section = lax.axis_index("section")
    is_first = section == 0
    dp_index = lax.axis_index("dp")
    per_chip = images.shape[0]
    per_core = per_chip // 2
    total_images = per_chip * count_dp
    width = w_qkv.shape[0]
    ff_width = w_down.shape[0]
    coefficient = 1.0 / (total_images * P_SIZE * PD * math.log(2.0))
    seq = Sequencer()

    position = jnp.concatenate(two_terms(w_embed[:P_SIZE]), axis=0)
    small = jnp.concatenate(
        [
            position.T,
            w_head.astype(BF),
            jnp.pad(jnp.concatenate(three_terms(w_norms), axis=0), ((0, S_IN - S_NORM - 18), (0, 0))).T,
            jnp.pad(w_in.astype(BF), ((0, S_WIDTH - S_IN - PD), (0, 0))).T,
        ],
        axis=1,
    )
    first = jnp.concatenate([small, w_qkv.astype(BF), w_attn.astype(BF)], axis=1)
    up_units = w_up.astype(BF).reshape(width, count_dp, 2, ff_width // 2)
    own_halves = dict(
        first=(first[:, : FIRST_WIDTH // 2], first[:, FIRST_WIDTH // 2 :]),
        up=tuple(up_units[:, :, half].reshape(width, FF // 2) for half in range(2)),
        down=(w_down[: ff_width // 2].astype(BF), w_down[ff_width // 2 :].astype(BF)),
    )
    label_flight = seq.launch(label_steps(labels))
    starts = [seq.launch(one_step(jnp.where(is_first, right, left), "section")) for left, right in own_halves.values()]
    seq.turn()
    seq.turn()
    parts = ({}, {})
    for (name, (left, right)), start in zip(own_halves.items(), starts):
        taken = start["result"]
        parts[0][name] = jnp.where(is_first, left, taken)
        parts[1][name] = jnp.where(is_first, taken, right)
    flat = jnp.concatenate([parts[1]["first"], parts[1]["up"], down_columns(parts[1]["down"], width)], axis=1)
    gathered = lax.all_gather(seq.tie(flat), "dp", axis=0, tiled=True)
    flights = {
        name: seq.launch(weight_steps(parts[0][name], order_from(GATHER_ORDERS, 0, name))) for name in own_halves
    }
    all_labels = seq.wait(label_flight)
    named = (jnp.arange(CLS)[:, None] == all_labels[None, :]).astype(BF)
    own_classes = [dot_tn(term, named).astype(BF) for term in two_terms(w_embed[P_SIZE:])]
    class_flight = seq.launch(
        class_steps(jnp.concatenate(own_classes, axis=1), is_first, tuple(range(dp_bits())))
    )
    classes = seq.wait(class_flight)
    classes_of = (classes[:, : 2 * total_images], classes[:, 2 * total_images :])

    start = section * per_core
    own_images = lax.dynamic_slice_in_dim(images, start, per_core, 0)
    own_noise = lax.dynamic_slice_in_dim(noise_draw, start, per_core, 0)
    keep = (1 - lax.dynamic_slice_in_dim(class_drop, start, per_core, 0)).astype(F32)
    inputs = (own_images + NOISE_SCALE * own_noise).reshape(per_core * P_SIZE, PD)

    def reverse(rows):
        return rows.reshape(per_core, P_SIZE, PD)[:, ::-1].reshape(per_core * P_SIZE, PD)

    image_ids = dp_index * per_chip + start + jnp.arange(per_core)
    picks = jnp.where(jnp.arange(total_images)[None, :] == image_ids[:, None], keep[:, None], 0.0).astype(BF)
    later = {}

    def split_gathered():
        whole = seq.tie(gathered)
        edge = FIRST_WIDTH // 2
        later["first"] = seq.launch(one_pair(whole[:, :edge]))
        later["up"] = seq.launch(one_pair(whole[:, edge : edge + FF // 2]))
        later["down"] = seq.launch(one_pair(down_rows(whole[:, edge + FF // 2 :], width)))

    saved_zero, sums_zero = block_forward(
        seq, is_first, flights, classes_of[0], inputs, picks, split_gathered
    )
    flights = later
    saved_one, sums_one = block_forward(
        seq, is_first, flights, classes_of[1], reverse(saved_zero["latent"]), picks
    )
    latent_one = saved_one["latent"]
    loss_local = 0.5 * jnp.sum(latent_one * latent_one) + sums_zero[3] + sums_one[3]

    pieces = ({}, {})
    grad_one = block_backward(
        seq, section, 1, saved_one, picks, coefficient * latent_one, coefficient, pieces[1]
    )
    block_backward(seq, section, 0, saved_zero, picks, reverse(grad_one), coefficient, pieces[0])

    while not pieces[0]["first"]["done"]:
        seq.turn()
    both = pieces[0]["first"]["result"]
    half = both[0].shape[1] // 2
    last = [
        seq.launch(
            scatter_both(
                [value[:, part * half : (part + 1) * half] for value in both],
                order_from(SCATTER_ORDERS, 0, ("first", "last")[part]),
            )
        )
        for part in range(2)
    ]
    pieces[0]["first"] = {"done": True, "result": jnp.concatenate(seq.wait(*last), axis=1)}
    part_scattered(pieces[1], 1, seq.tie(pieces[1]["scattered"]))

    own = {}
    for name in ("down", "up", "first"):
        one, zero = seq.wait(pieces[1][name], pieces[0][name])
        kept = jnp.where(is_first, zero, one)
        own[name] = (kept, seq.launch(one_step(jnp.where(is_first, one, zero), "section")))
    for name, (kept, flight) in own.items():
        other = seq.wait(flight)
        own[name] = (jnp.where(is_first, kept, other), jnp.where(is_first, other, kept))
    first = jnp.concatenate(own["first"], axis=1)
    small = first[:, QKV + D :]
    rest = small.shape[1] - 128
    class_at = P_SIZE + PD
    class_rows = lax.dot_general(
        named.astype(F32),
        small[:, class_at : class_at + total_images],
        (((1,), (1,)), ((), ())),
        precision=lax.Precision.HIGHEST,
        preferred_element_type=F32,
    )
    up_grad = jnp.stack([half.reshape(width, count_dp, ff_width // 2) for half in own["up"]], axis=2)
    shards = (
        first[:, :QKV],
        first[:, QKV : QKV + D],
        up_grad.reshape(width, FF),
        jnp.concatenate(own["down"], axis=0),
        small[:, P_SIZE : P_SIZE + PD].T,
        small[:, rest : rest + 2 * PD],
        jnp.concatenate([small[:, :P_SIZE].T, class_rows], axis=0),
        small[:, rest + 2 * PD : rest + 2 * PD + 6].T,
    )
    square_local = sum(jnp.sum(shard * shard) for shard in shards)
    totals = jnp.concatenate([sums_zero[:3], sums_one[:3], jnp.stack([loss_local, square_local])])[None]
    totals = seq.wait(seq.launch(sum_steps(totals)))[0]
    loss_sum = totals[6] + seq.token
    grad_norm = jnp.sqrt(totals[7])
    activity = jnp.sqrt(totals[:6].reshape(2, 3) / (total_images * P_SIZE * D))
    factor = jnp.minimum(1.0, CLIP_NORM / grad_norm)
    new_moments, new_squares, new_weights = ([], [], [])
    for weight, moment, square, shard, rate in zip(weights, moments, squares, shards, LEARN_RATES):
        clipped = shard[None] * factor
        moment_next = BETA_ONE * moment + (1 - BETA_ONE) * clipped
        square_next = BETA_TWO * square + (1 - BETA_TWO) * clipped * clipped
        update = (
            moment_next
            / (1 - BETA_ONE**STEP)
            / (jnp.sqrt(square_next / (1 - BETA_TWO**STEP)) + EPS_ADAM)
        )
        new_moments.append(moment_next)
        new_squares.append(square_next)
        new_weights.append(weight - rate * (update + WEIGHT_DECAY * weight))
    return (*new_moments, *new_squares, *new_weights, loss_sum, grad_norm, activity)


def solution(mesh):
    by_row = P("section", "dp", None)
    by_column = P("section", None, "dp")
    weight_specs = (by_row, by_row, by_row, by_row, by_column, by_row, by_column, by_column)
    return jax.shard_map(
        body,
        mesh=mesh,
        in_specs=(P("dp", None, None), P("dp", None, None), P("dp"), P("dp")) + weight_specs * 3,
        out_specs=weight_specs * 3 + (P(), P(), P()),
        check_vma=False,
    )
```

time: 1890 us -> 714 us (0.38)
  waiting for transfers between devices: 1230 us -> 251 us
  Pallas kernels: 0 us -> 225 us
  matrix products: 227 us -> 2.56 us
  blocking collectives: 162 us -> 0 us
  local copies, waits for them, and re-layouts: 121 us -> 70.7 us
  starting transfers between devices: 7.18 us -> 57.1 us
  other arithmetic: 106 us -> 68.6 us
    reduce_scatter x5 -> x1, waiting for transfers between devices: 757 us -> 0.01 us  [scatter_summed(): lax.psum_scatter(seq.tie(whole), 'dp', scatter_dimension=0, tiled=False)]
    unnamed x16 -> x2, waiting for transfers between devices: 304 us -> 0.03 us
    ppermute x4 -> x64, waiting for transfers between devices: 1.1 us -> 251 us  [exchange(): return lax.ppermute(value, axis, swap_pairs(lax.axis_size(axis), bit))]
    pallas_call x0 -> x24, Pallas kernels: none -> 225 us  [the longest x2 27.9 us: first_grads(): call(lambda *refs: first_grad_kernel(steps, *refs), 'first_weight_grad',...]
    dot_general x71 -> x5, matrix products: 227 us -> 2.56 us  [the longest x2 1.63 us: dot_nt(): lax.dot_general(left, right, (((1,), (1,)), ((), ())), preferred_element_...]
    all_gather x5 -> x1, waiting for transfers between devices: 169 us -> 0.01 us  [body(): gathered = lax.all_gather(seq.tie(flat), 'dp', axis=0, tiled=True)]
    all_gather x3 -> x0, blocking collectives: 123 us -> none  [the longest x1 45.1 us: body(): lax.all_gather(w_in[0].astype(jnp.bfloat16), 'dp', axis=1, tiled=True)]
    ppermute x4 -> x64, starting transfers between devices: 6.25 us -> 57 us  [exchange(): return lax.ppermute(value, axis, swap_pairs(lax.axis_size(axis), bit))]
  transfers between devices with their start and end apart: 17 -> 66, of which waited for: 13 -> 37; matrix products, arithmetic and copies ran while one was open for 9% -> 8% of each run, Pallas kernels for 0% -> 17%
where the time goes in v1:
time: 714 us; the launch traced here: 701 us
  waiting for transfers between devices  251 us (35%)
  Pallas kernels  225 us (32%)
  local copies, waits for them, and re-layouts  70.7 us (10%)
  other arithmetic  68.6 us (10%)
  starting transfers between devices  57.1 us (8%)
  between operations  26.7 us (4%)
    ppermute x64, waiting for transfers between devices, exchange(): return lax.ppermute(value, axis, swap_pairs(lax.axis_size(axis), bit))  251 us
    ppermute x64, starting transfers between devices, exchange(): return lax.ppermute(value, axis, swap_pairs(lax.axis_size(axis), bit))  57 us
    pallas_call x2, Pallas kernels, first_grads(): call(lambda *refs: first_grad_kernel(steps, *refs), 'first_weight_grad',...  27.9 us
    pallas_call x2, Pallas kernels, attend_back(): pl.pallas_call(attend_back_kernel, grid=(count, PAIRS), in_specs=part + [...  25.7 us
    pallas_call x2, Pallas kernels, up_back(): call(lambda *refs: up_back_kernel(count, *refs), 'up_back', 8 * rows * D...  23.7 us
    pallas_call x2, Pallas kernels, up_halves(): call(lambda *refs: up_kernel(count, *refs), 'up_gelu', 4 * rows * D * col...  23 us
    pallas_call x2, Pallas kernels, attend(): pl.pallas_call(attend_kernel, grid=(count, PAIRS), in_specs=part, out_spe...  21.6 us
    pallas_call x2, Pallas kernels, middle_back(): call(middle_back_kernel, 'middle_back', 4 * rows * D * columns, grid=(row...  20.7 us
  transfers between devices with their start and end apart: 66, of which 37 were waited for; matrix products, arithmetic and copies ran while one was open for 8% of the time, Pallas kernels for 17%

profile of v1, /device:TPU:0, one launch (start us, length us, event | category | flops | bytes accessed | tf_op | source)
XLA Modules:
  0.0 701.4 jit_solution(15916403205674602804)
XLA Ops:
  73.2 21.1 %collective-permute-done.14 = bf16[2,2,48,1536]{3,2,1,0:T(8,128)(2,1)} collective-permute-done((bf16[2,2,48,1536]{3,2,1,0:T(8,128)(2,1)}, bf16[2,2,48,1536]{3,2,1,0:T(8,128)(2,1)}, u32[]{:S(2)}, u32[]{:S(2)}) %collective-permute-start.14) | collective-permute-done | bytes 589856 | tf_op jit(solution)/shard_map/ppermute | solution.py:48
  101.5 22.8 %collective-permute-done.17 = bf16[2,2,2,48,1536]{4,3,2,0,1:T(8,128)(2,1)S(1)} collective-permute-done((bf16[2,2,2,48,1536]{4,3,2,0,1:T(8,128)(2,1)S(1)}, bf16[2,2,2,48,1536]{4,3,2,0,1:T(8,128)(2,1)S(1)}, u32[]{:S(2)}, u32[]{:S(2)}) %collective-permute-start.17) | collective-permute-done | bytes 1179680 | tf_op jit(solution)/shard_map/ppermute | solution.py:48
  124.3 29.8 %collective-permute-done.18 = bf16[2,2,2,96,768]{4,3,0,1,2:T(8,128)(2,1)S(1)} collective-permute-done((bf16[2,2,2,96,768]{4,3,0,1,2:T(8,128)(2,1)S(1)}, bf16[2,2,2,96,768]{4,3,0,1,2:T(8,128)(2,1)S(1)}, u32[]{:S(2)}, u32[]{:S(2)}) %collective-permute-start.18) | collective-permute-done | bytes 1179680 | tf_op jit(solution)/shard_map/ppermute | solution.py:48
  202.2 10.8 %attention.2 = (bf16[512,768]{1,0:T(8,128)(2,1)}, bf16[2,12,256,256]{3,2,1,0:T(8,128)(2,1)}) custom-call(bf16[512,2304]{1,0:T(8,128)(2,1)} %get-tuple-element.831.q_ref.k_ref.v_ref, bf16[512,2304]{1,0:T(8,128)(2,1)} %get-tuple-element.831.q_ref.k_ref.v_ref, bf16[512,2304]{1,0:T(8,128)(2,1)} %get-tuple-element.831.q_ref.k_ref.v_ref), custom_call_target="tpu_custom_call" | custom-call | flops 805306368 | bytes 6291456 | tf_op jit(solution)/shard_map/attention/pallas_call | solution.py:729
  217.2 11.4 %up_gelu.2 = (bf16[512,1536]{1,0:T(8,128)(2,1)}, bf16[512,1536]{1,0:T(8,128)(2,1)}, bf16[512,1536]{1,0:T(8,128)(2,1)}, bf16[512,1536]{1,0:T(8,128)(2,1)}) custom-call(bf16[512,768]{1,0:T(8,128)(2,1)} %get-tuple-element.597.refs_0_.refs_1_, bf16[768,1536]{1,0:T(8,128)(2,1)} %bitcast.47.refs_1_.up_one, bf16[768,1536]{1,0:T(8,128)(2,1)} %collective-permute-done.21.refs_2_.up_two), custom_call_target="tpu_custom_call" | custom-call | flops 2415919104 | bytes 9437184 | tf_op jit(solution)/shard_map/up_gelu/pallas_call | solution.py:406
  246.3 9.0 %down_norm_head.2 = (f32[512,768]{1,0:T(8,128)}, bf16[512,768]{1,0:T(8,128)(2,1)}, f32[512,48]{1,0:T(8,128)}, f32[512,48]{1,0:T(8,128)}, f32[8,768]{1,0:T(8,128)}) custom-call(bf16[512,1536]{1,0:T(8,128)(2,1)} %get-tuple-element.790.active_one.refs_0_, bf16[512,1536]{1,0:T(8,128)(2,1)} %get-tuple-element.791.active_two.refs_1_, ...), custom_call_target="tpu_custom_call" | custom-call | flops 2415919104 | bytes 9437184 | tf_op jit(solution)/shard_map/down_norm_head/pallas_call | solution.py:444
  270.9 10.8 %attention.3 = (bf16[512,768]{1,0:T(8,128)(2,1)}, bf16[2,12,256,256]{3,2,1,0:T(8,128)(2,1)}) custom-call(bf16[512,2304]{1,0:T(8,128)(2,1)} %get-tuple-element.743.q_ref.k_ref.v_ref, bf16[512,2304]{1,0:T(8,128)(2,1)} %get-tuple-element.743.q_ref.k_ref.v_ref, bf16[512,2304]{1,0:T(8,128)(2,1)} %get-tuple-element.743.q_ref.k_ref.v_ref), custom_call_target="tpu_custom_call" | custom-call | flops 805306368 | bytes 6291456 | tf_op jit(solution)/shard_map/attention/pallas_call | solution.py:729
  286.3 11.5 %up_gelu.3 = (bf16[512,1536]{1,0:T(8,128)(2,1)}, bf16[512,1536]{1,0:T(8,128)(2,1)}, bf16[512,1536]{1,0:T(8,128)(2,1)}, bf16[512,1536]{1,0:T(8,128)(2,1)}) custom-call(bf16[512,768]{1,0:T(8,128)(2,1)} %get-tuple-element.670.refs_0_.refs_1_, bf16[768,1536]{1,0:T(8,128)(2,1)} %get-tuple-element.671.refs_1_.up_one, ...), custom_call_target="tpu_custom_call" | custom-call | flops 2415919104 | bytes 9437184 | tf_op jit(solution)/shard_map/up_gelu/pallas_call | solution.py:406
  297.8 9.0 %down_norm_head.3 = (f32[512,768]{1,0:T(8,128)}, bf16[512,768]{1,0:T(8,128)(2,1)}, f32[512,48]{1,0:T(8,128)}, f32[512,48]{1,0:T(8,128)}, f32[8,768]{1,0:T(8,128)}) custom-call(bf16[512,1536]{1,0:T(8,128)(2,1)} %get-tuple-element.711.active_one.refs_0_, bf16[512,1536]{1,0:T(8,128)(2,1)} %get-tuple-element.712.active_two.refs_1_, ...), custom_call_target="tpu_custom_call" | custom-call | flops 2415919104 | bytes 9437184 | tf_op jit(solution)/shard_map/down_norm_head/pallas_call | solution.py:444
  322.0 11.9 %up_back.2 = (bf16[512,1536]{1,0:T(8,128)(2,1)}, bf16[512,1536]{1,0:T(8,128)(2,1)}, bf16[768,1536]{1,0:T(8,128)(2,1)}, bf16[768,1536]{1,0:T(8,128)(2,1)}) custom-call(bf16[512,768]{1,0:T(8,128)(2,1)} %get-tuple-element.718.refs_2_.refs_0_, bf16[512,768]{1,0:T(8,128)(2,1)} %get-tuple-element.670.refs_0_.refs_1_, bf16[1536,768]{1,0:T(8,128)(2,1)} %bitcast.62.down_one.refs_2_, ...), custom_call_target="tpu_custom_call" | custom-call | flops 4831838208 | bytes 18874368 | tf_op jit(solution)/shard_map/up_back/pallas_call | solution.py:553
  335.6 10.3 %middle_back.2 = (f32[512,768]{1,0:T(8,128)}, bf16[512,768]{1,0:T(8,128)(2,1)}, bf16[512,768]{1,0:T(8,128)(2,1)}, f32[8,768]{1,0:T(8,128)}) custom-call(bf16[512,1536]{1,0:T(8,128)(2,1)} %get-tuple-element.732.one_ref, bf16[512,1536]{1,0:T(8,128)(2,1)} %get-tuple-element.733.two_ref, bf16[768,1536]{1,0:T(8,128)(2,1)} %get-tuple-element.671.refs_1_.up_one, ...), custom_call_target="tpu_custom_call" | custom-call | flops 2415919104 | bytes 9437184 | tf_op jit(solution)/shard_map/middle_back/pallas_call | solution.py:580
  346.0 13.0 %attention_back.2.joint_ref.refs_4_ = bf16[512,2304]{1,0:T(8,128)(2,1)} custom-call(bf16[512,2304]{1,0:T(8,128)(2,1)} %get-tuple-element.743.q_ref.k_ref.v_ref, bf16[512,2304]{1,0:T(8,128)(2,1)} %get-tuple-element.743.q_ref.k_ref.v_ref, bf16[512,2304]{1,0:T(8,128)(2,1)} %get-tuple-element.743.q_ref.k_ref.v_ref, ...), custom_call_target="tpu_custom_call" | custom-call | flops 1610612736 | bytes 8650752 | tf_op jit(solution)/shard_map/attention_back/pallas_call | solution.py:776
  371.6 13.8 %first_weight_grad.2 = (bf16[768,1792]{1,0:T(8,128)(2,1)}, bf16[768,1792]{1,0:T(8,128)(2,1)}) custom-call(s32[1]{0:T(128)} %bitcast.67.refs_0_, bf16[512,768]{1,0:T(8,128)(2,1)} %get-tuple-element.766.refs_1_, bf16[512,768]{1,0:T(8,128)(2,1)} %get-tuple-element.659.attended_ref.refs_2_, bf16[512,768]{1,0:T(8,128)(2,1)} %get-tuple-element.767.refs_3_, ...), custom_call_target="tpu_custom_call" | custom-call | flops 2818572288 | bytes 11010048 | tf_op jit(solution)/shard_map/first_weight_grad/pallas_call | solution.py:675
  400.2 11.8 %up_back.3 = (bf16[512,1536]{1,0:T(8,128)(2,1)}, bf16[512,1536]{1,0:T(8,128)(2,1)}, bf16[768,1536]{1,0:T(8,128)(2,1)}, bf16[768,1536]{1,0:T(8,128)(2,1)}) custom-call(bf16[512,768]{1,0:T(8,128)(2,1)} %get-tuple-element.800.refs_2_.refs_0_, bf16[512,768]{1,0:T(8,128)(2,1)} %get-tuple-element.597.refs_0_.refs_1_, bf16[1536,768]{1,0:T(8,128)(2,1)} %bitcast.50.down_one.refs_2_, ...), custom_call_target="tpu_custom_call" | custom-call | flops 4831838208 | bytes 18874368 | tf_op jit(solution)/shard_map/up_back/pallas_call | solution.py:553
  412.0 10.4 %middle_back.3 = (f32[512,768]{1,0:T(8,128)}, bf16[512,768]{1,0:T(8,128)(2,1)}, bf16[512,768]{1,0:T(8,128)(2,1)}, f32[8,768]{1,0:T(8,128)}) custom-call(bf16[512,1536]{1,0:T(8,128)(2,1)} %get-tuple-element.811.one_ref, bf16[512,1536]{1,0:T(8,128)(2,1)} %get-tuple-element.812.two_ref, bf16[768,1536]{1,0:T(8,128)(2,1)} %bitcast.47.refs_1_.up_one, ...), custom_call_target="tpu_custom_call" | custom-call | flops 2415919104 | bytes 9437184 | tf_op jit(solution)/shard_map/middle_back/pallas_call | solution.py:580
  436.6 12.7 %attention_back.3.joint_ref.refs_4_ = bf16[512,2304]{1,0:T(8,128)(2,1)} custom-call(bf16[512,2304]{1,0:T(8,128)(2,1)} %get-tuple-element.831.q_ref.k_ref.v_ref, bf16[512,2304]{1,0:T(8,128)(2,1)} %get-tuple-element.831.q_ref.k_ref.v_ref, bf16[512,2304]{1,0:T(8,128)(2,1)} %get-tuple-element.831.q_ref.k_ref.v_ref, ...), custom_call_target="tpu_custom_call" | custom-call | flops 1610612736 | bytes 8650752 | tf_op jit(solution)/shard_map/attention_back/pallas_call | solution.py:776
  458.0 14.1 %first_weight_grad.3 = (bf16[768,1792]{1,0:T(8,128)(2,1)}, bf16[768,1792]{1,0:T(8,128)(2,1)}) custom-call(s32[1]{0:T(128)} %bitcast.67.refs_0_, bf16[512,768]{1,0:T(8,128)(2,1)} %get-tuple-element.843.refs_1_, bf16[512,768]{1,0:T(8,128)(2,1)} %get-tuple-element.586.attended_ref.refs_2_, bf16[512,768]{1,0:T(8,128)(2,1)} %get-tuple-element.844.refs_3_, ...), custom_call_target="tpu_custom_call" | custom-call | flops 2818572288 | bytes 11010048 | tf_op jit(solution)/shard_map/first_weight_grad/pallas_call | solution.py:675
  472.4 10.1 %collective-permute-done.35 = bf16[2,2,2,96,768]{4,3,0,2,1:T(8,128)(2,1)} collective-permute-done((bf16[2,2,2,96,768]{4,3,0,2,1:T(8,128)(2,1)}, bf16[2,2,2,96,768]{4,3,0,2,1:T(8,128)(2,1)}, u32[]{:S(2)}, u32[]{:S(2)}) %collective-permute-start.35) | collective-permute-done | bytes 1179680 | tf_op jit(solution)/shard_map/ppermute | solution.py:48
  482.5 11.8 %collective-permute-done.34 = bf16[2,2,2,48,1792]{4,3,1,2,0:T(8,128)(2,1)} collective-permute-done((bf16[2,2,2,48,1792]{4,3,1,2,0:T(8,128)(2,1)}, bf16[2,2,2,48,1792]{4,3,1,2,0:T(8,128)(2,1)}, u32[]{:S(2)}, u32[]{:S(2)}) %collective-permute-start.34) | collective-permute-done | bytes 1376288 | tf_op jit(solution)/shard_map/ppermute | solution.py:48
  507.0 14.0 %collective-permute-done.38 = bf16[2,2,96,768]{3,2,1,0:T(8,128)(2,1)S(1)} collective-permute-done((bf16[2,2,96,768]{3,2,1,0:T(8,128)(2,1)S(1)}, bf16[2,2,96,768]{3,2,1,0:T(8,128)(2,1)S(1)}, u32[]{:S(2)}, u32[]{:S(2)}) %collective-permute-start.38) | collective-permute-done | bytes 589856 | tf_op jit(solution)/shard_map/ppermute | solution.py:48
  525.5 10.4 %collective-permute-done.39 = bf16[2,2,2,48,1536]{4,3,0,2,1:T(8,128)(2,1)S(1)} collective-permute-done((bf16[2,2,2,48,1536]{4,3,0,2,1:T(8,128)(2,1)}, bf16[2,2,2,48,1536]{4,3,0,2,1:T(8,128)(2,1)S(1)}, u32[]{:S(2)}, u32[]{:S(2)}) %collective-permute-start.39) | collective-permute-done | bytes 1179680 | tf_op jit(solution)/shard_map/ppermute | solution.py:48
  542.8 10.3 %collective-permute-done.42 = bf16[2,96,768]{2,1,0:T(8,128)(2,1)S(1)} collective-permute-done((bf16[2,96,768]{2,1,0:T(8,128)(2,1)S(1)}, bf16[2,96,768]{2,1,0:T(8,128)(2,1)S(1)}, u32[]{:S(2)}, u32[]{:S(2)}) %collective-permute-start.42) | collective-permute-done | bytes 294944 | tf_op jit(solution)/shard_map/ppermute | solution.py:48
  553.1 13.5 %collective-permute-done.41 = bf16[2,48,1792]{2,1,0:T(8,128)(2,1)S(1)} collective-permute-done((bf16[2,48,1792]{2,1,0:T(8,128)(2,1)S(1)}, bf16[2,48,1792]{2,1,0:T(8,128)(2,1)S(1)}, u32[]{:S(2)}, u32[]{:S(2)}) %collective-permute-start.41) | collective-permute-done | bytes 344096 | tf_op jit(solution)/shard_map/ppermute | solution.py:48
  578.5 12.5 %collective-permute-done.45 = bf16[96,768]{1,0:T(8,128)(2,1)S(1)} collective-permute-done((bf16[96,768]{1,0:T(8,128)(2,1)S(1)}, bf16[96,768]{1,0:T(8,128)(2,1)S(1)}, u32[]{:S(2)}, u32[]{:S(2)}) %collective-permute-start.45) | collective-permute-done | bytes 147488 | tf_op jit(solution)/shard_map/ppermute | solution.py:48
  (471 shorter events, 357.8 us)
Async XLA Ops:
  7.2 221.4 %all-gather.2.cloned.1.call-start = ((), (), s32[]{:S(2)}) async-start(), calls=%async_computation.1 | async-start | bytes 8146944 | tf_op jit(solution)/shard_map/all_gather | solution.py:945
  52.6 573.6 %reduce-scatter.2.cloned.1.call-start = ((), (), s32[]{:S(2)}) async-start(), calls=%async_computation.2 | async-start | bytes 5013504 | tf_op jit(solution)/shard_map/reduce_scatter | solution.py:855
  66.0 28.3 %collective-permute-start.13 = (bf16[2,2,48,1920]{3,2,0,1:T(8,128)(2,1)}, bf16[2,2,48,1920]{3,2,0,1:T(8,128)(2,1)S(1)}, u32[]{:S(2)}, u32[]{:S(2)}) collective-permute-start(bf16[2,2,48,1920]{3,2,0,1:T(8,128)(2,1)} %pad_maximum_fusion.9), channel_id=1, source_target_pairs={{0,4},{2,6},{4,0},{6,2},{8,12},{10,14},{12,8},{14,10},{16,20},{18,... | collective-permute-start | bytes 2211848 | tf_op jit(solution)/shard_map/ppermute | solution.py:48
  67.3 26.9 %collective-permute-start.14 = (bf16[2,2,48,1536]{3,2,1,0:T(8,128)(2,1)}, bf16[2,2,48,1536]{3,2,1,0:T(8,128)(2,1)}, u32[]{:S(2)}, u32[]{:S(2)}) collective-permute-start(bf16[2,2,48,1536]{3,2,1,0:T(8,128)(2,1)} %pad_maximum_fusion.10), channel_id=1, source_target_pairs={{0,8},{2,10},{4,12},{6,14},{8,0},{10,2},{12,4},{14,6},{16,24},{18,... | collective-permute-start | bytes 1769480 | tf_op jit(solution)/shard_map/ppermute | solution.py:48
  71.0 23.3 %collective-permute-start.15 = (bf16[2,2,96,768]{3,2,0,1:T(8,128)(2,1)}, bf16[2,2,96,768]{3,2,0,1:T(8,128)(2,1)}, u32[]{:S(2)}, u32[]{:S(2)}) collective-permute-start(bf16[2,2,96,768]{3,2,0,1:T(8,128)(2,1)} %pad_maximum_fusion.11), channel_id=1, source_target_pairs={{0,2},{2,0},{4,6},{6,4},{8,10},{10,8},{12,14},{14,12},{16,18},{18,... | collective-permute-start | bytes 1769480 | tf_op jit(solution)/shard_map/ppermute | solution.py:48
  97.2 56.9 %collective-permute-start.16 = (bf16[2,2,2,48,1920]{4,3,0,1,2:T(8,128)(2,1)S(1)}, bf16[2,2,2,48,1920]{4,3,0,1,2:T(8,128)(2,1)S(1)}, u32[]{:S(2)}, u32[]{:S(2)}) collective-permute-start(bf16[2,2,2,48,1920]{4,3,0,1,2:T(8,128)(2,1)S(1)} %pad_maximum_fusion.6), channel_id=1, source_target_pairs={{0,2},{2,0},{4,6},{6,4},{8,10},{10,8},{12,14},{14,12},{16,18},{18,... | collective-permute-start | bytes 4423688 | tf_op jit(solution)/shard_map/ppermute | solution.py:48
  98.7 25.6 %collective-permute-start.17 = (bf16[2,2,2,48,1536]{4,3,2,0,1:T(8,128)(2,1)S(1)}, bf16[2,2,2,48,1536]{4,3,2,0,1:T(8,128)(2,1)S(1)}, u32[]{:S(2)}, u32[]{:S(2)}) collective-permute-start(bf16[2,2,2,48,1536]{4,3,2,0,1:T(8,128)(2,1)S(1)} %pad_maximum_fusion.7), channel_id=1, source_target_pairs={{0,4},{2,6},{4,0},{6,2},{8,12},{10,14},{12,8},{14,10},{16,20},{18,... | collective-permute-start | bytes 3538952 | tf_op jit(solution)/shard_map/ppermute | solution.py:48
  100.3 53.8 %collective-permute-start.18 = (bf16[2,2,2,96,768]{4,3,0,1,2:T(8,128)(2,1)S(1)}, bf16[2,2,2,96,768]{4,3,0,1,2:T(8,128)(2,1)S(1)}, u32[]{:S(2)}, u32[]{:S(2)}) collective-permute-start(bf16[2,2,2,96,768]{4,3,0,1,2:T(8,128)(2,1)S(1)} %pad_maximum_fusion.8), channel_id=1, source_target_pairs={{0,8},{2,10},{4,12},{6,14},{8,0},{10,2},{12,4},{14,6},{16,24},{18,... | collective-permute-start | bytes 3538952 | tf_op jit(solution)/shard_map/ppermute | solution.py:48
  333.9 25.0 %collective-permute-start.30 = (bf16[1536,768]{1,0:T(8,128)(2,1)}, bf16[1536,768]{1,0:T(8,128)(2,1)S(1)}, u32[]{:S(2)}, u32[]{:S(2)}) collective-permute-start(bf16[1536,768]{1,0:T(8,128)(2,1)} %get-tuple-element.747), channel_id=1, source_target_pairs={{0,1},{1,0},{2,3},{3,2},{4,5},{5,4},{6,7},{7,6},{8,9},{9,8},{10,11... | collective-permute-start | bytes 7077896 | tf_op jit(solution)/shard_map/ppermute | solution.py:48
  334.4 24.5 %collective-permute-start.31 = (bf16[768,1536]{1,0:T(8,128)(2,1)}, bf16[768,1536]{1,0:T(8,128)(2,1)S(1)}, u32[]{:S(2)}, u32[]{:S(2)}) collective-permute-start(bf16[768,1536]{1,0:T(8,128)(2,1)} %get-tuple-element.748), channel_id=1, source_target_pairs={{0,1},{1,0},{2,3},{3,2},{4,5},{5,4},{6,7},{7,6},{8,9},{9,8},{10,11... | collective-permute-start | bytes 7077896 | tf_op jit(solution)/shard_map/ppermute | solution.py:48
  399.6 25.1 %collective-permute-start.32 = (bf16[768,1792]{1,0:T(8,128)(2,1)}, bf16[768,1792]{1,0:T(8,128)(2,1)}, u32[]{:S(2)}, u32[]{:S(2)}) collective-permute-start(bf16[768,1792]{1,0:T(8,128)(2,1)} %get-tuple-element.819), channel_id=1, source_target_pairs={{0,1},{1,0},{2,3},{3,2},{4,5},{5,4},{6,7},{7,6},{8,9},{9,8},{10,11... | collective-permute-start | bytes 8257544 | tf_op jit(solution)/shard_map/ppermute | solution.py:48
  400.2 24.6 %collective-permute-start.33 = (bf16[1536,768]{1,0:T(8,128)(2,1)}, bf16[1536,768]{1,0:T(8,128)(2,1)}, u32[]{:S(2)}, u32[]{:S(2)}) collective-permute-start(bf16[1536,768]{1,0:T(8,128)(2,1)} %get-tuple-element.820), channel_id=1, source_target_pairs={{0,1},{1,0},{2,3},{3,2},{4,5},{5,4},{6,7},{7,6},{8,9},{9,8},{10,11... | collective-permute-start | bytes 7077896 | tf_op jit(solution)/shard_map/ppermute | solution.py:48
  432.3 62.0 %collective-permute-start.36 = (bf16[768,1536]{1,0:T(8,128)(2,1)}, bf16[768,1536]{1,0:T(8,128)(2,1)}, u32[]{:S(2)}, u32[]{:S(2)}) collective-permute-start(bf16[768,1536]{1,0:T(8,128)(2,1)} %get-tuple-element.857), channel_id=1, source_target_pairs={{0,1},{1,0},{2,3},{3,2},{4,5},{5,4},{6,7},{7,6},{8,9},{9,8},{10,11... | collective-permute-start | bytes 7077896 | tf_op jit(solution)/shard_map/ppermute | solution.py:48
  436.6 57.7 %collective-permute-start.34 = (bf16[2,2,2,48,1792]{4,3,1,2,0:T(8,128)(2,1)}, bf16[2,2,2,48,1792]{4,3,1,2,0:T(8,128)(2,1)}, u32[]{:S(2)}, u32[]{:S(2)}) collective-permute-start(bf16[2,2,2,48,1792]{4,3,1,2,0:T(8,128)(2,1)} %fusion), channel_id=1, source_target_pairs={{0,8},{2,10},{4,12},{6,14},{8,0},{10,2},{12,4},{14,6},{16,24},{18,... | collective-permute-start | bytes 4128776 | tf_op jit(solution)/shard_map/ppermute | solution.py:48
  449.3 33.2 %collective-permute-start.35 = (bf16[2,2,2,96,768]{4,3,0,2,1:T(8,128)(2,1)}, bf16[2,2,2,96,768]{4,3,0,2,1:T(8,128)(2,1)}, u32[]{:S(2)}, u32[]{:S(2)}) collective-permute-start(bf16[2,2,2,96,768]{4,3,0,2,1:T(8,128)(2,1)} %fusion.3), channel_id=1, source_target_pairs={{0,2},{2,0},{4,6},{6,4},{8,10},{10,8},{12,14},{14,12},{16,18},{18,... | collective-permute-start | bytes 3538952 | tf_op jit(solution)/shard_map/ppermute | solution.py:48
  501.5 34.4 %collective-permute-start.40 = (bf16[768,1792]{1,0:T(8,128)(2,1)}, bf16[768,1792]{1,0:T(8,128)(2,1)}, u32[]{:S(2)}, u32[]{:S(2)}) collective-permute-start(bf16[768,1792]{1,0:T(8,128)(2,1)} %get-tuple-element.868), channel_id=1, source_target_pairs={{0,1},{1,0},{2,3},{3,2},{4,5},{5,4},{6,7},{7,6},{8,9},{9,8},{10,11... | collective-permute-start | bytes 8257544 | tf_op jit(solution)/shard_map/ppermute | solution.py:48
  501.5 34.4 %collective-permute-start.39 = (bf16[2,2,2,48,1536]{4,3,0,2,1:T(8,128)(2,1)}, bf16[2,2,2,48,1536]{4,3,0,2,1:T(8,128)(2,1)S(1)}, u32[]{:S(2)}, u32[]{:S(2)}) collective-permute-start(bf16[2,2,2,48,1536]{4,3,0,2,1:T(8,128)(2,1)} %fusion.4), channel_id=1, source_target_pairs={{0,4},{2,6},{4,0},{6,2},{8,12},{10,14},{12,8},{14,10},{16,20},{18,... | collective-permute-start | bytes 3538952 | tf_op jit(solution)/shard_map/ppermute | solution.py:48
  504.6 20.8 %collective-permute-start.37 = (bf16[2,2,48,1792]{3,2,1,0:T(8,128)(2,1)S(1)}, bf16[2,2,48,1792]{3,2,1,0:T(8,128)(2,1)S(1)}, u32[]{:S(2)}, u32[]{:S(2)}) collective-permute-start(bf16[2,2,48,1792]{3,2,1,0:T(8,128)(2,1)S(1)} %copy-done.16), channel_id=1, source_target_pairs={{0,2},{2,0},{4,6},{6,4},{8,10},{10,8},{12,14},{14,12},{16,18},{18,... | collective-permute-start | bytes 2064392 | tf_op jit(solution)/shard_map/ppermute | solution.py:48
  536.6 30.1 %collective-permute-start.41 = (bf16[2,48,1792]{2,1,0:T(8,128)(2,1)S(1)}, bf16[2,48,1792]{2,1,0:T(8,128)(2,1)S(1)}, u32[]{:S(2)}, u32[]{:S(2)}) collective-permute-start(bf16[2,48,1792]{2,1,0:T(8,128)(2,1)S(1)} %get-tuple-element.875), channel_id=1, source_target_pairs={{0,16},{2,18},{4,20},{6,22},{8,24},{10,26},{12,28},{14,30},{16,0},... | collective-permute-start | bytes 1032200 | tf_op jit(solution)/shard_map/ppermute | solution.py:48
  539.2 34.2 %collective-permute-start.43 = (bf16[2,2,48,1536]{3,2,1,0:T(8,128)(2,1)S(1)}, bf16[2,2,48,1536]{3,2,1,0:T(8,128)(2,1)S(1)}, u32[]{:S(2)}, u32[]{:S(2)}) collective-permute-start(bf16[2,2,48,1536]{3,2,1,0:T(8,128)(2,1)S(1)} %copy.150), channel_id=1, source_target_pairs={{0,8},{2,10},{4,12},{6,14},{8,0},{10,2},{12,4},{14,6},{16,24},{18,... | collective-permute-start | bytes 1769480 | tf_op jit(solution)/shard_map/ppermute | solution.py:48
  573.6 25.2 %collective-permute-start.47 = (bf16[2,2,2,48,896]{4,3,0,2,1:T(8,128)(2,1)S(1)}, bf16[2,2,2,48,896]{4,3,0,2,1:T(8,128)(2,1)S(1)}, u32[]{:S(2)}, u32[]{:S(2)}) collective-permute-start(bf16[2,2,2,48,896]{4,3,0,2,1:T(8,128)(2,1)S(1)} %fusion.10), channel_id=1, source_target_pairs={{0,2},{2,0},{4,6},{6,4},{8,10},{10,8},{12,14},{14,12},{16,18},{18,... | collective-permute-start | bytes 2064392 | tf_op jit(solution)/shard_map/ppermute | solution.py:48
  575.4 23.5 %collective-permute-start.48 = (bf16[2,2,2,48,896]{4,3,0,2,1:T(8,128)(2,1)S(1)}, bf16[2,2,2,48,896]{4,3,0,2,1:T(8,128)(2,1)S(1)}, u32[]{:S(2)}, u32[]{:S(2)}) collective-permute-start(bf16[2,2,2,48,896]{4,3,0,2,1:T(8,128)(2,1)S(1)} %fusion.11), channel_id=1, source_target_pairs={{0,4},{2,6},{4,0},{6,2},{8,12},{10,14},{12,8},{14,10},{16,20},{18,... | collective-permute-start | bytes 2064392 | tf_op jit(solution)/shard_map/ppermute | solution.py:48
  576.3 22.5 %collective-permute-start.46 = (bf16[2,48,1536]{2,1,0:T(8,128)(2,1)S(1)}, bf16[2,48,1536]{2,1,0:T(8,128)(2,1)S(1)}, u32[]{:S(2)}, u32[]{:S(2)}) collective-permute-start(bf16[2,48,1536]{2,1,0:T(8,128)(2,1)S(1)} %get-tuple-element.885), channel_id=1, source_target_pairs={{0,2},{2,0},{4,6},{6,4},{8,10},{10,8},{12,14},{14,12},{16,18},{18,... | collective-permute-start | bytes 884744 | tf_op jit(solution)/shard_map/ppermute | solution.py:48
  577.3 20.2 %collective-permute-start.44 = (bf16[48,1792]{1,0:T(8,128)(2,1)S(1)}, bf16[48,1792]{1,0:T(8,128)(2,1)S(1)}, u32[]{:S(2)}, u32[]{:S(2)}) collective-permute-start(bf16[48,1792]{1,0:T(8,128)(2,1)S(1)} %fusion.63), channel_id=1, source_target_pairs={{0,4},{2,6},{4,0},{6,2},{8,12},{10,14},{12,8},{14,10},{16,20},{18,... | collective-permute-start | bytes 516104 | tf_op jit(solution)/shard_map/ppermute | solution.py:48
  (102 other events, 738.4 us)
Sparse Core Ops, SparseCore 0:
  52.8 123.5 all-gather.1
  433.8 159.8 reduce-scatter.1

commit v2 on v1

--- a/solution.py
+++ b/solution.py
@@ -36,12 +36,14 @@
 FIRST_WIDTH = S_WIDTH + QKV + D
 PAIR = 2 * HD
 PAIRS = H // 2
-TILE = 512
-VMEM_BYTES = 56 << 20
+TILE = D
+FF_HALF = FF // 2
+VMEM_BYTES = 30 << 20
 
 
 def swap_pairs(count, bit):
-    return [(source, source ^ (1 << bit)) for source in range(count)]
+    mask = bit[0] if isinstance(bit, tuple) else 1 << bit
+    return [(source, source ^ mask) for source in range(count)]
 
 
 def exchange(value, axis, bit=0):
@@ -58,12 +60,11 @@
 
 GATHER_ORDERS = ({"first": (0, 1, 2, 3), "up": (1, 2, 3, 0), "down": (2, 0, 1, 3)},)
 SCATTER_ORDERS = (
-    {"down": (0, 2, 1, 3), "up": (1, 2, 0, 3), "first": (0, 1, 2, 3), "last": (1, 2, 0, 3)},
-    {"first": (2, 0, 3, 1)},
+    {"down": (2, 0, 1, 3), "up": (1, 2, 0, 3), "first": (0, 1, 2, 3), "last": (1, 2, 0, 3)},
+    {"down": (0, 2, 1, 3), "up": (1, 0, 2, 3), "first": (0, 1, 2, 3)},
 )
 
 
-BY_COLLECTIVE = ((), ("down", "up"))
 SPLIT = (0, "first")
 
 
@@ -187,29 +188,22 @@
     return got
 
 
-def one_pair(mine):
-    other = yield (mine, "section", 0)
-    return mine, other
-
-
 def sum_pair(mine, given):
     other = yield (given, "section", 0)
     return mine, other
 
 
-def down_columns(rows, width):
-    count = rows.shape[0] // width
-    return rows.reshape(count, width, D).transpose(1, 0, 2).reshape(width, count * D)
-
-
-def down_rows(columns, width):
-    count = columns.shape[1] // D
-    return columns.reshape(-1, width, count, D).transpose(0, 2, 1, 3).reshape(-1, D)
-
-
-def label_steps(labels):
-    gathered = yield from gather_steps(labels[None], tuple(range(dp_bits())))
-    return gathered.reshape(-1)
+def label_steps(nearby):
+    high = dp_bits() - 2
+    own = lax.axis_index("dp") >> high
+    rows = [sum(jnp.where((own ^ step) == at, value, 0) for step, value in enumerate(nearby)) for at in range(4)]
+    held = jnp.stack(rows)
+    for bit in range(high - 1, -1, -1):
+        other = yield (held, "dp", bit)
+        swap = parity_of(bit) == 1
+        place = high - bit
+        held = jnp.stack([jnp.where(swap, other, held), jnp.where(swap, held, other)], axis=place)
+    return held.reshape(-1)
 
 
 def class_steps(own, is_first, order):
@@ -217,6 +211,13 @@
     both = jnp.concatenate([jnp.where(is_first, own, other), jnp.where(is_first, other, own)], axis=1)
     whole = yield from gather_steps(both, order)
     return whole
+
+
+def class_rows_of(named, columns):
+    return lax.dot_general(
+        named.astype(F32), columns, (((1,), (1,)), ((), ())),
+        precision=lax.Precision.HIGHEST, preferred_element_type=F32,
+    )
 
 
 def sum_steps(values):
@@ -264,6 +265,10 @@
 
 HEAD_SPEC = pl.BlockSpec((D, 128), lambda *_: (0, S_HEAD // 128))
 IN_SPEC = pl.BlockSpec((D, 128), lambda *_: (0, S_IN // 128))
+
+
+def half_spec(part):
+    return pl.BlockSpec((D, FF_HALF), lambda *_: (0, part[1] // STEPS))
 
 
 def shape_of(rows, columns, kind=F32):
@@ -320,6 +325,16 @@
 
     for index, row in enumerate(rows):
         sums_ref[index : index + 1, :] += row
+
+
+def reversed_rows(values):
+    row, column = iotas(P_SIZE, P_SIZE)
+    turn = where_ones(row + column == P_SIZE - 1)
+    high = values.astype(BF)
+    rest = values - high.astype(F32)
+    middle = rest.astype(BF)
+    low = (rest - middle.astype(F32)).astype(BF)
+    return dot(turn, high) + dot(turn, middle) + dot(turn, low)
 
 
 def begin_kernel(x_ref, class_ref, small_ref, q_ref, k_ref, v_ref, hidden_ref, normed_ref, joint_ref, norms_ref):
@@ -374,12 +389,25 @@
     )(attended, first, hidden, norms)
 
 
-def half_steps(columns):
-    count = columns // TILE
-    return 2 * count, lambda j: jnp.minimum(j, count - 1), lambda j: jnp.maximum(j - count, 0), count
-
-
-def up_kernel(count, x_ref, one_ref, two_ref, active_one, active_two, slope_one, slope_two):
+STEPS = FF_HALF // TILE
+
+
+def at_one(j):
+    return jnp.minimum(j, STEPS - 1)
+
+
+def at_two(j):
+    return jnp.maximum(j - STEPS, 0)
+
+
+def tile_specs(rows, starts=(0, 0)):
+    return [
+        pl.BlockSpec((rows, TILE), lambda j: (0, starts[0] + at_one(j))),
+        pl.BlockSpec((rows, TILE), lambda j: (0, starts[1] + at_two(j))),
+    ]
+
+
+def up_kernel(x_ref, one_ref, two_ref, active_one, active_two, slope_one, slope_two):
     def half(weight_ref, active_ref, slope_ref):
         u = dot(x_ref[...], weight_ref[...])
         t = pl.reciprocal(1.0 + (0.3275911 / math.sqrt(2.0)) * jnp.abs(u), approx=True)
@@ -390,35 +418,37 @@
         active_ref[...] = (u * share).astype(BF)
         slope_ref[...] = (share + u * bell * (1.0 / math.sqrt(2.0 * math.pi))).astype(BF)
 
-    @pl.when(pl.program_id(0) < count)
+    @pl.when(pl.program_id(0) < STEPS)
     def _():
         half(one_ref, active_one, slope_one)
 
-    @pl.when(pl.program_id(0) >= count)
+    @pl.when(pl.program_id(0) >= STEPS)
     def _():
         half(two_ref, active_two, slope_two)
 
 
 def up_halves(normed, one, two):
-    rows, columns = normed.shape[0], one.shape[1]
-    steps, at_one, at_two, count = half_steps(columns)
-    tiles = [lambda j: (0, at_one(j)), lambda j: (0, at_two(j))]
+    rows = normed.shape[0]
     return call(
-        lambda *refs: up_kernel(count, *refs),
+        up_kernel,
         "up_gelu",
-        4 * rows * D * columns,
-        grid=(steps,),
-        in_specs=[whole_spec(rows, D)] + [pl.BlockSpec((D, TILE), tile) for tile in tiles],
-        out_specs=[pl.BlockSpec((rows, TILE), tile) for tile in tiles * 2],
-        out_shape=[shape_of(rows, columns, BF)] * 4,
-    )(normed, one, two)
+        4 * rows * D * FF_HALF,
+        grid=(2 * STEPS,),
+        in_specs=[whole_spec(rows, D)] + tile_specs(D, (one[1], two[1])),
+        out_specs=tile_specs(rows) * 2,
+        out_shape=[shape_of(rows, FF_HALF, BF)] * 4,
+    )(normed, one[0], two[0])
 
 
 def end_kernel(
     active_one, active_two, down_one, down_two, middle_ref, norms_ref, head_ref, x_ref,
-    final_ref, normed_ref, shrink_ref, latent_ref, sums_ref,
+    final_ref, normed_ref, shrink_ref, latent_ref, turned_ref, sums_ref,
 ):
-    branch = dot(active_one[...], down_one[...]) + dot(active_two[...], down_two[...])
+    branch = sum(
+        dot(active_ref[:, part * D : (part + 1) * D], down_ref[:, part * D : (part + 1) * D])
+        for active_ref, down_ref in ((active_one, down_one), (active_two, down_two))
+        for part in range(STEPS)
+    )
     final = middle_ref[...] + branch
     final_ref[...] = final
     normed = norm_rows(final, norms_ref[...], 2)
@@ -429,38 +459,38 @@
     log_scale = moved[:, PD : 2 * PD]
     shrink = jnp.exp(-log_scale)
     shrink_ref[...] = shrink
-    latent_ref[...] = (x_ref[...] - moved[:, :PD]) * shrink
+    latent = (x_ref[...] - moved[:, :PD]) * shrink
+    latent_ref[...] = latent
+    turned_ref[...] = reversed_rows(latent)
     _, lane = iotas(1, D)
     add_sums(
         sums_ref,
         jnp.sum(final * final, axis=0, keepdims=True),
         jnp.sum(branch * branch, axis=0, keepdims=True),
-        jnp.where(lane == 0, jnp.sum(log_scale), 0.0),
+        jnp.where(lane == 0, jnp.sum(log_scale), 0.0) + jnp.where(lane == 1, 0.5 * jnp.sum(latent * latent), 0.0),
     )
 
 
 def end(actives, downs, middle, norms, first, inputs):
-    rows, columns = actives[0].shape
+    rows = middle.shape[0]
     return call(
         end_kernel,
         "down_norm_head",
-        4 * rows * D * columns,
+        4 * rows * D * FF_HALF,
         grid=(rows // P_SIZE,),
-        in_specs=[row_spec(columns)] * 2
-        + [whole_spec(columns, D)] * 2
+        in_specs=[row_spec(FF_HALF)] * 2
+        + [half_spec(down) for down in downs]
         + [row_spec(D), whole_spec(8, D), HEAD_SPEC, row_spec(PD)],
-        out_specs=[row_spec(D), row_spec(D), row_spec(PD), row_spec(PD), whole_spec(8, D)],
-        out_shape=[
-            shape_of(rows, D), shape_of(rows, D, BF), shape_of(rows, PD), shape_of(rows, PD), shape_of(8, D)
-        ],
-    )(*actives, *downs, middle, norms, first, inputs)
+        out_specs=[row_spec(D), row_spec(D)] + [row_spec(PD)] * 3 + [whole_spec(8, D)],
+        out_shape=[shape_of(rows, D), shape_of(rows, D, BF)] + [shape_of(rows, PD)] * 3 + [shape_of(8, D)],
+    )(*actives, *(down for down, _ in downs), middle, norms, first, inputs)
 
 
 def head_back_kernel(
-    coefficient, latent_grad_ref, shrink_ref, latent_ref, final_ref, norms_ref, head_ref, normed_ref,
+    coefficient, last, latent_grad_ref, shrink_ref, latent_ref, final_ref, norms_ref, head_ref, normed_ref,
     through_ref, flow_ref, low_ref, weight_ref, sums_ref,
 ):
-    latent_grad = latent_grad_ref[...]
+    latent_grad = coefficient * latent_ref[...] if last else latent_grad_ref[...]
     through = latent_grad * shrink_ref[...]
     through_ref[...] = through
     scale_grad = coefficient - latent_grad * latent_ref[...]
@@ -483,10 +513,10 @@
     add_sums(sums_ref, gain_grad, offset_grad)
 
 
-def head_back(coefficient, latent_grad, shrink, latent, final, norms, first, normed):
+def head_back(coefficient, last, latent_grad, shrink, latent, final, norms, first, normed):
     rows = final.shape[0]
     return call(
-        lambda *refs: head_back_kernel(coefficient, *refs),
+        lambda *refs: head_back_kernel(coefficient, last, *refs),
         "head_back",
         4 * rows * D * 128,
         grid=(rows // P_SIZE,),
@@ -498,67 +528,62 @@
     )(latent_grad, shrink, latent, final, norms, first, normed)
 
 
-def down_grad_kernel(count, one_ref, two_ref, low_ref, out_one, out_two):
-    @pl.when(pl.program_id(0) < count)
+def down_grad_kernel(one_ref, two_ref, low_ref, out_one, out_two):
+    @pl.when(pl.program_id(0) < STEPS)
     def _():
         out_one[...] = dot_tn(one_ref[...], low_ref[...]).astype(BF)
 
-    @pl.when(pl.program_id(0) >= count)
+    @pl.when(pl.program_id(0) >= STEPS)
     def _():
         out_two[...] = dot_tn(two_ref[...], low_ref[...]).astype(BF)
 
 
 def down_grads(one, two, low):
-    rows, columns = one.shape
-    steps, at_one, at_two, count = half_steps(columns)
+    rows = low.shape[0]
     return call(
-        lambda *refs: down_grad_kernel(count, *refs),
+        down_grad_kernel,
         "down_weight_grad",
-        4 * rows * D * columns,
-        grid=(steps,),
-        in_specs=[
-            pl.BlockSpec((rows, TILE), lambda j: (0, at_one(j))),
-            pl.BlockSpec((rows, TILE), lambda j: (0, at_two(j))),
-            whole_spec(rows, D),
-        ],
-        out_specs=[
-            pl.BlockSpec((TILE, D), lambda j: (at_one(j), 0)),
-            pl.BlockSpec((TILE, D), lambda j: (at_two(j), 0)),
-        ],
-        out_shape=[shape_of(columns, D, BF)] * 2,
+        4 * rows * D * FF_HALF,
+        grid=(2 * STEPS,),
+        in_specs=tile_specs(rows) + [whole_spec(rows, D)],
+        out_specs=tile_specs(D),
+        out_shape=[shape_of(D, FF_HALF, BF)] * 2,
     )(one, two, low)
 
 
-def up_back_kernel(count, low_ref, normed_ref, *refs):
+def up_back_kernel(low_ref, normed_ref, *refs):
+    *refs, turned_ref = refs
+
+    @pl.when(pl.program_id(0) == 0)
+    def _():
+        turned_ref[...] = normed_ref[...].T
+
     def half(weight_ref, slope_ref, grad_ref, out_ref):
         grad = (dot_nt(low_ref[...], weight_ref[...]) * slope_ref[...].astype(F32)).astype(BF)
         grad_ref[...] = grad
-        out_ref[...] = dot_tn(normed_ref[...], grad).astype(BF)
-
-    @pl.when(pl.program_id(0) < count)
+        out_ref[...] = dot(turned_ref[...], grad).astype(BF)
+
+    @pl.when(pl.program_id(0) < STEPS)
     def _():
         half(*refs[0::2])
 
-    @pl.when(pl.program_id(0) >= count)
+    @pl.when(pl.program_id(0) >= STEPS)
     def _():
         half(*refs[1::2])
 
 
 def up_back(low, normed, downs, slopes):
-    rows, columns = slopes[0].shape
-    steps, at_one, at_two, count = half_steps(columns)
-    by_column = [lambda j: (0, at_one(j)), lambda j: (0, at_two(j))]
-    by_row = [lambda j: (at_one(j), 0), lambda j: (at_two(j), 0)]
-    tiles = [pl.BlockSpec((rows, TILE), tile) for tile in by_column]
+    rows = low.shape[0]
     return call(
-        lambda *refs: up_back_kernel(count, *refs),
+        up_back_kernel,
         "up_back",
-        8 * rows * D * columns,
-        grid=(steps,),
-        in_specs=[whole_spec(rows, D)] * 2 + [pl.BlockSpec((TILE, D), tile) for tile in by_row] + tiles,
-        out_specs=tiles + [pl.BlockSpec((D, TILE), tile) for tile in by_column],
-        out_shape=[shape_of(rows, columns, BF)] * 2 + [shape_of(D, columns, BF)] * 2,
-    )(low, normed, *downs, *slopes)
+        8 * rows * D * FF_HALF,
+        grid=(2 * STEPS,),
+        in_specs=[whole_spec(rows, D)] * 2 + tile_specs(D, [start for _, start in downs]) + tile_specs(rows),
+        out_specs=tile_specs(rows) + tile_specs(D),
+        out_shape=[shape_of(rows, FF_HALF, BF)] * 2 + [shape_of(D, FF_HALF, BF)] * 2,
+        scratch_shapes=[pltpu.VMEM((D, rows), BF)],
+    )(low, normed, *(down for down, _ in downs), *slopes)
 
 
 def middle_back_kernel(
@@ -576,18 +601,18 @@
 
 
 def middle_back(grads, ups, middle, norms, above, first):
-    rows, columns = grads[0].shape
+    rows = middle.shape[0]
     return call(
         middle_back_kernel,
         "middle_back",
-        4 * rows * D * columns,
+        4 * rows * D * FF_HALF,
         grid=(rows // P_SIZE,),
-        in_specs=[row_spec(columns)] * 2
-        + [whole_spec(D, columns)] * 2
+        in_specs=[row_spec(FF_HALF)] * 2
+        + [half_spec(up) for up in ups]
         + [row_spec(D), whole_spec(8, D), row_spec(D), first_spec(4)],
         out_specs=[row_spec(D), row_spec(D), row_spec(D), whole_spec(8, D)],
         out_shape=[shape_of(rows, D), shape_of(rows, D, BF), shape_of(rows, D, BF), shape_of(8, D)],
-    )(*grads, *ups, middle, norms, above, first)
+    )(*grads, *(up for up, _ in ups), middle, norms, above, first)
 
 
 def input_back_kernel(
@@ -600,7 +625,7 @@
     flow, gain_grad, offset_grad = norm_back_rows(hidden_ref[...], norms_ref[...], 0, back)
     low = (above_ref[...] + flow).astype(BF)
     low_ref[...] = low
-    out_ref[...] = through_ref[...] + dot(low, in_ref[...])[:, :PD]
+    out_ref[...] = reversed_rows(through_ref[...] + dot(low, in_ref[...])[:, :PD])
     add_sums(sums_ref, gain_grad, offset_grad)
 
 
@@ -625,9 +650,15 @@
 
 def first_grad_kernel(
     steps, section_ref, normed_ref, attended_ref, low_ref, joint_ref, middle_ref, source_ref, head_ref,
-    sums_one, sums_two, sums_three, mine_ref, given_ref,
+    sums_one, sums_two, sums_three, mine_ref, given_ref, turned_ref,
 ):
     step = pl.program_id(0)
+    for at, left_ref in ((0, normed_ref), (QKV // COLUMNS, attended_ref), (SOURCE_AT, low_ref)):
+
+        @pl.when(step == at)
+        def _(left_ref=left_ref):
+            turned_ref[...] = left_ref[...].T
+
     to_mine = (step >= steps // 2) == (section_ref[0] == 1)
 
     def put(value):
@@ -641,15 +672,15 @@
 
     @pl.when(step < QKV // COLUMNS)
     def _():
-        put(dot_tn(normed_ref[...], joint_ref[...]).astype(BF))
+        put(dot(turned_ref[...], joint_ref[...]).astype(BF))
 
     @pl.when((step >= QKV // COLUMNS) & (step < SOURCE_AT))
     def _():
-        put(dot_tn(attended_ref[...], middle_ref[...]).astype(BF))
+        put(dot(turned_ref[...], middle_ref[...]).astype(BF))
 
     @pl.when((step >= SOURCE_AT) & (step < steps - 1))
     def _():
-        put(dot_tn(low_ref[...], source_ref[...]).astype(BF))
+        put(dot(turned_ref[...], source_ref[...]).astype(BF))
 
     @pl.when(step == steps - 1)
     def _():
@@ -658,7 +689,7 @@
         for which, sums_ref in enumerate((sums_one, sums_two, sums_three)):
             place = where_ones((row < 2) & (column == row + 2 * PD + 2 * which))
             rest = rest + dot_tn(sums_ref[...].astype(BF), place)
-        source = dot_tn(low_ref[...], source_ref[:, :128])
+        source = dot(turned_ref[...], source_ref[:, :128])
         put(jnp.concatenate([source, rest], axis=1).astype(BF))
 
 
@@ -695,6 +726,7 @@
                 pl.BlockSpec((D, COLUMNS), lambda j, s: (0, jnp.clip(j - half * s[0], 0, half - 1))),
                 pl.BlockSpec((D, COLUMNS), lambda j, s: (0, jnp.clip(j - half * (1 - s[0]), 0, half - 1))),
             ],
+            scratch_shapes=[pltpu.VMEM((D, rows), BF)],
         ),
         out_shape=[shape_of(D, half * COLUMNS, BF)] * 2,
     )(section[None].astype(jnp.int32), normed, attended, low, joint_grad, low_middle, sources, head, *sums)
@@ -793,45 +825,100 @@
     )(joint, joint, joint, probs, grad)
 
 
+def square_kernel(class_at, section_ref, named_ref, *refs):
+    *parts, out_ref = refs
+    images = named_ref.shape[1]
+    first_core = section_ref[0] == 0
+    total = jnp.zeros((1, 1), F32)
+    for index, ref in enumerate(parts):
+        value = ref[...]
+        squares = jnp.sum(jnp.sum(value * value, axis=0, keepdims=True), axis=1, keepdims=True)
+        if index % 3 == 2:
+            columns = ref[:, class_at : class_at + images]
+            high = columns.astype(BF)
+            low = (columns - high.astype(F32)).astype(BF)
+            rows = dot_nt(named_ref[...], high) + dot_nt(named_ref[...], low)
+            joined = jnp.sum(jnp.sum(rows * rows, axis=0, keepdims=True), axis=1, keepdims=True)
+            apart = jnp.sum(jnp.sum(columns * columns, axis=0, keepdims=True), axis=1, keepdims=True)
+            squares = squares + jnp.where(first_core, 0.0, joined - apart)
+        total = total + squares
+    out_ref[...] = jnp.broadcast_to(total, out_ref.shape)
+
+
+def square_sum(section, named, done, small_width):
+    parts = [block[name] for block in done for name in ("down", "up", "first")]
+    class_at = parts[2].shape[1] - small_width + P_SIZE
+    whole = [pl.BlockSpec(value.shape, lambda j: (0, 0)) for value in [named] + parts]
+    return call(
+        lambda *refs: square_kernel(class_at, *refs),
+        "square_sum",
+        0,
+        grid=(1,),
+        in_specs=[pl.BlockSpec(memory_space=pltpu.SMEM)] + whole,
+        out_specs=pl.BlockSpec((8, 128), lambda j: (0, 0)),
+        out_shape=shape_of(8, 128),
+    )(section[None].astype(jnp.int32), named, *parts)[0, 0]
+
+
+def adam_kernel(factor_ref, *refs):
+    count = len(LEARN_RATES)
+    factor = factor_ref[0, 0]
+    for index, rate in enumerate(LEARN_RATES):
+        weight, moment, square, grad = (ref[...] for ref in refs[4 * index : 4 * index + 4])
+        moment_ref, square_ref, weight_ref = refs[4 * count + 3 * index : 4 * count + 3 * index + 3]
+        clipped = grad * factor
+        moment_next = BETA_ONE * moment + (1 - BETA_ONE) * clipped
+        square_next = BETA_TWO * square + (1 - BETA_TWO) * clipped * clipped
+        size = jnp.sqrt(square_next * (1.0 / (1 - BETA_TWO**STEP))) + EPS_ADAM
+        update = moment_next * (1.0 / (1 - BETA_ONE**STEP)) / size
+        moment_ref[...] = moment_next
+        square_ref[...] = square_next
+        weight_ref[...] = weight - rate * (update + WEIGHT_DECAY * weight)
+
+
+def adam(factor, states):
+    return call(
+        adam_kernel,
+        "adam",
+        0,
+        grid=(1,),
+        in_specs=[pl.BlockSpec(memory_space=pltpu.SMEM)] + [whole_spec(*value.shape) for state in states for value in state],
+        out_specs=[whole_spec(*state[0].shape) for state in states for _ in range(3)],
+        out_shape=[shape_of(*state[0].shape) for state in states for _ in range(3)],
+    )(factor.reshape(1, 1), *(value for state in states for value in state))
+
+
 def place_halves(is_first, mine, other):
     return jnp.concatenate(
         [jnp.where(is_first, mine, other), jnp.where(is_first, other, mine)], axis=1
     )
 
 
-def block_forward(seq, is_first, flights, classes, inputs, picks, between=lambda: None):
-    count = inputs.shape[0] // P_SIZE
-    first = seq.compute(place_halves, is_first, *seq.wait(flights["first"]))
+def block_forward(seq, first, mlp_weights, classes, inputs, picks, between=lambda: None):
     own = dot_nt(jnp.concatenate([picks, picks], axis=1), classes)
     hidden, normed_one, joint, norms = seq.compute(begin, inputs, own, first)
     attended, probs = seq.compute(attend, joint)
     middle, normed_two, sums_two = seq.compute(attention_end, attended, first, hidden, norms)
-    ups = seq.wait(flights["up"])
-    *actives, slope_one, slope_two = seq.compute(up_halves, normed_two, *ups)
+    ups, downs = mlp_weights()
+    *actives, slope_one, slope_two = seq.compute(lambda normed: up_halves(normed, *ups), normed_two)
     between()
-    seq.turn()
-    downs = seq.wait(flights["down"])
-    final, normed_three, shrink, latent, sums = seq.compute(end, actives, downs, middle, norms, first, inputs)
+    final, normed_three, shrink, latent, turned, sums = seq.compute(
+        lambda actives, middle: end(actives, downs, middle, norms, first, inputs), actives, middle
+    )
     saved = dict(
         first=first, ups=ups, downs=downs, inputs=inputs, hidden=hidden, normed_one=normed_one, joint=joint,
         norms=norms, attended=attended, probs=probs, middle=middle, normed_two=normed_two, actives=actives,
         slopes=(slope_one, slope_two), final=final, normed_three=normed_three, shrink=shrink, latent=latent,
-    )
-    squares = jnp.stack([jnp.sum(sums[0]), jnp.sum(sums_two[0]), jnp.sum(sums[1]), jnp.sum(sums[2])])
+        turned=turned,
+    )
+    squares = seq.compute(
+        lambda one, two: jnp.concatenate(
+            [jnp.sum(jnp.concatenate([one[:1], two[:1], one[1:2]], axis=0), axis=1), one[2, :2]]
+        ),
+        sums,
+        sums_two,
+    )
     return saved, squares
-
-
-def part_scattered(pieces, block, scattered):
-    scattered = scattered.astype(F32)
-    place = 0
-    for name in BY_COLLECTIVE[block]:
-        shape = pieces[name]["result"][0].shape
-        height = shape[0] // lax.axis_size("dp")
-        columns = []
-        for _ in range(0, shape[1], D):
-            columns.append(scattered[place : place + height])
-            place += height
-        pieces[name] = {"done": True, "result": jnp.concatenate(columns, axis=1)}
 
 
 def block_backward(seq, section, block, saved, picks, latent_grad, coefficient, pieces):
@@ -839,24 +926,15 @@
     first, norms = saved["first"], saved["norms"]
 
     def launch(name, mine, given):
-        if name in BY_COLLECTIVE[block] or (block, name) == SPLIT:
+        if (block, name) == SPLIT:
             pieces[name] = seq.launch(sum_pair(mine, given))
             return
         order = order_from(SCATTER_ORDERS, block, name)
         pieces[name] = seq.launch(scatter_steps(mine, given, order))
 
-    def scatter_summed():
-        rows = []
-        for name in BY_COLLECTIVE[block]:
-            mine, other = (value.reshape(lax.axis_size("dp"), -1, *value.shape[1:]) for value in pieces[name]["result"])
-            total = (mine.astype(F32) + other.astype(F32)).astype(BF)
-            rows += [total[:, :, start : start + D] for start in range(0, total.shape[2], D)]
-        whole = jnp.concatenate(rows, axis=1)
-        return lax.psum_scatter(seq.tie(whole), "dp", scatter_dimension=0, tiled=False)
-
     through, flow, low_final, head_grad, sums_three = seq.compute(
         lambda grad: head_back(
-            coefficient, grad, saved["shrink"], saved["latent"], saved["final"], norms, first, saved["normed_three"]
+            coefficient, block == 1, grad, saved["shrink"], saved["latent"], saved["final"], norms, first, saved["normed_three"]
         ),
         latent_grad,
     )
@@ -877,13 +955,14 @@
     joint_grad = seq.compute(attend_back, saved["joint"], saved["probs"], attended_grad)
     if block == 1:
         seq.turn()
-        pieces["scattered"] = scatter_summed()
     low_hidden, input_grad, sums_one = seq.compute(
         lambda grad: input_back(grad, first, saved["hidden"], norms, wide_middle, through), joint_grad
     )
+    if block == 0:
+        seq.turn()
     places = jnp.tile(jnp.eye(P_SIZE, dtype=BF), (count, 1))
     sources = jnp.concatenate(
-        [places, saved["inputs"].astype(BF), jnp.repeat(picks, P_SIZE, axis=0)], axis=1
+        [places, jnp.repeat(picks, P_SIZE, axis=0), saved["inputs"].astype(BF)], axis=1
     )
     sources = jnp.pad(sources, ((0, 0), (0, 128 + -(sources.shape[1] + 128) % 512)))
     launch(
@@ -926,13 +1005,18 @@
         axis=1,
     )
     first = jnp.concatenate([small, w_qkv.astype(BF), w_attn.astype(BF)], axis=1)
-    up_units = w_up.astype(BF).reshape(width, count_dp, 2, ff_width // 2)
+    up_units = w_up.astype(BF).reshape(width, count_dp, 2, 2, width).transpose(2, 0, 3, 1, 4).reshape(2, width, FF_HALF)
+    down_units = w_down.astype(BF).reshape(2, 2, width, D).transpose(0, 2, 1, 3).reshape(2, width, FF_HALF)
     own_halves = dict(
+        up=(up_units[0], up_units[1]),
+        down=(down_units[0], down_units[1]),
         first=(first[:, : FIRST_WIDTH // 2], first[:, FIRST_WIDTH // 2 :]),
-        up=tuple(up_units[:, :, half].reshape(width, FF // 2) for half in range(2)),
-        down=(w_down[: ff_width // 2].astype(BF), w_down[ff_width // 2 :].astype(BF)),
-    )
-    label_flight = seq.launch(label_steps(labels))
+    )
+    nearby = [seq.launch(one_step(labels, "dp", (step << (dp_bits() - 2), ))) for step in range(1, 4)]
+    seq.turn()
+    seq.turn()
+    label_flight = seq.launch(label_steps([labels] + [flight["result"] for flight in nearby]))
+    seq.turn()
     starts = [seq.launch(one_step(jnp.where(is_first, right, left), "section")) for left, right in own_halves.values()]
     seq.turn()
     seq.turn()
@@ -941,18 +1025,25 @@
         taken = start["result"]
         parts[0][name] = jnp.where(is_first, left, taken)
         parts[1][name] = jnp.where(is_first, taken, right)
-    flat = jnp.concatenate([parts[1]["first"], parts[1]["up"], down_columns(parts[1]["down"], width)], axis=1)
+    flat = jnp.concatenate([parts[1][name] for name in own_halves], axis=1)
     gathered = lax.all_gather(seq.tie(flat), "dp", axis=0, tiled=True)
     flights = {
-        name: seq.launch(weight_steps(parts[0][name], order_from(GATHER_ORDERS, 0, name))) for name in own_halves
+        name: seq.launch(steps(parts[0][name], order_from(GATHER_ORDERS, 0, name)))
+        for name, steps in (("first", weight_steps), ("up", gather_steps), ("down", gather_steps))
     }
+    seq.turn()
     all_labels = seq.wait(label_flight)
     named = (jnp.arange(CLS)[:, None] == all_labels[None, :]).astype(BF)
     own_classes = [dot_tn(term, named).astype(BF) for term in two_terms(w_embed[P_SIZE:])]
     class_flight = seq.launch(
         class_steps(jnp.concatenate(own_classes, axis=1), is_first, tuple(range(dp_bits())))
     )
+    mine_of = {name: seq.wait(flights[name]) for name in ("up", "down")}
+    first_halves = seq.wait(flights["first"])
+    later = {name: seq.launch(one_step(mine, "section")) for name, mine in mine_of.items()}
     classes = seq.wait(class_flight)
+    seq.turn()
+    first = seq.compute(place_halves, is_first, *first_halves)
     classes_of = (classes[:, : 2 * total_images], classes[:, 2 * total_images :])
 
     start = section * per_core
@@ -961,36 +1052,37 @@
     keep = (1 - lax.dynamic_slice_in_dim(class_drop, start, per_core, 0)).astype(F32)
     inputs = (own_images + NOISE_SCALE * own_noise).reshape(per_core * P_SIZE, PD)
 
-    def reverse(rows):
-        return rows.reshape(per_core, P_SIZE, PD)[:, ::-1].reshape(per_core * P_SIZE, PD)
-
     image_ids = dp_index * per_chip + start + jnp.arange(per_core)
     picks = jnp.where(jnp.arange(total_images)[None, :] == image_ids[:, None], keep[:, None], 0.0).astype(BF)
-    later = {}
-
-    def split_gathered():
-        whole = seq.tie(gathered)
-        edge = FIRST_WIDTH // 2
-        later["first"] = seq.launch(one_pair(whole[:, :edge]))
-        later["up"] = seq.launch(one_pair(whole[:, edge : edge + FF // 2]))
-        later["down"] = seq.launch(one_pair(down_rows(whole[:, edge + FF // 2 :], width)))
-
-    saved_zero, sums_zero = block_forward(
-        seq, is_first, flights, classes_of[0], inputs, picks, split_gathered
-    )
-    flights = later
+    swapped = []
+
+    def swap_gathered():
+        mine = seq.tie(gathered)
+        swapped.append((mine, seq.launch(one_step(mine, "section"))))
+        seq.turn()
+
+    def mlp_zero():
+        return [[(half, 0) for half in (mine_of[name], seq.wait(later[name]))] for name in ("up", "down")]
+
+    saved_zero, sums_zero = block_forward(seq, first, mlp_zero, classes_of[0], inputs, picks, swap_gathered)
+    mine, flight = swapped[0]
+    both = (mine, seq.wait(flight))
+    first = seq.compute(lambda one, two: place_halves(is_first, one[:, FF:], two[:, FF:]), *both)
     saved_one, sums_one = block_forward(
-        seq, is_first, flights, classes_of[1], reverse(saved_zero["latent"]), picks
-    )
-    latent_one = saved_one["latent"]
-    loss_local = 0.5 * jnp.sum(latent_one * latent_one) + sums_zero[3] + sums_one[3]
+        seq, first, lambda: [[(half, start) for half in both] for start in (0, STEPS)], classes_of[1], saved_zero["turned"], picks
+    )
+    loss_local = sums_one[4] + sums_zero[3] + sums_one[3]
+    totals = seq.tie(jnp.concatenate([sums_zero[:3], sums_one[:3], loss_local[None], jnp.zeros((1,), F32)]))
 
     pieces = ({}, {})
     grad_one = block_backward(
-        seq, section, 1, saved_one, picks, coefficient * latent_one, coefficient, pieces[1]
-    )
-    block_backward(seq, section, 0, saved_zero, picks, reverse(grad_one), coefficient, pieces[0])
-
+        seq, section, 1, saved_one, picks, saved_one["latent"], coefficient, pieces[1]
+    )
+    seq.turn()
+    block_backward(seq, section, 0, saved_zero, picks, grad_one, coefficient, pieces[0])
+
+    small_width = 128 + P_SIZE + PD + total_images
+    small_width += -small_width % 512
     while not pieces[0]["first"]["done"]:
         seq.turn()
     both = pieces[0]["first"]["result"]
@@ -1005,41 +1097,38 @@
         for part in range(2)
     ]
     pieces[0]["first"] = {"done": True, "result": jnp.concatenate(seq.wait(*last), axis=1)}
-    part_scattered(pieces[1], 1, seq.tie(pieces[1]["scattered"]))
+
+    done = [{name: seq.wait(pieces[block][name]) for name in ("down", "up", "first")} for block in range(2)]
+
+    done = seq.tie(done)
+    square_local = square_sum(section, named, done, small_width)
 
     own = {}
     for name in ("down", "up", "first"):
-        one, zero = seq.wait(pieces[1][name], pieces[0][name])
-        kept = jnp.where(is_first, zero, one)
-        own[name] = (kept, seq.launch(one_step(jnp.where(is_first, one, zero), "section")))
+        zero, one = done[0][name], done[1][name]
+        own[name] = (jnp.where(is_first, zero, one), seq.launch(one_step(jnp.where(is_first, one, zero), "section")))
+    totals_flight = seq.launch(sum_steps(jnp.where(jnp.arange(8) == 7, square_local, totals)[None]))
     for name, (kept, flight) in own.items():
         other = seq.wait(flight)
         own[name] = (jnp.where(is_first, kept, other), jnp.where(is_first, other, kept))
     first = jnp.concatenate(own["first"], axis=1)
     small = first[:, QKV + D :]
     rest = small.shape[1] - 128
-    class_at = P_SIZE + PD
-    class_rows = lax.dot_general(
-        named.astype(F32),
-        small[:, class_at : class_at + total_images],
-        (((1,), (1,)), ((), ())),
-        precision=lax.Precision.HIGHEST,
-        preferred_element_type=F32,
-    )
-    up_grad = jnp.stack([half.reshape(width, count_dp, ff_width // 2) for half in own["up"]], axis=2)
+    class_rows = class_rows_of(named, small[:, P_SIZE : P_SIZE + total_images])
+    up_grad = jnp.stack([half.reshape(width, 2, count_dp, width) for half in own["up"]], axis=1)
+    up_grad = up_grad.transpose(0, 3, 1, 2, 4)
+    down_grad = jnp.stack([half.reshape(width, 2, D).transpose(1, 0, 2) for half in own["down"]])
     shards = (
         first[:, :QKV],
         first[:, QKV : QKV + D],
         up_grad.reshape(width, FF),
-        jnp.concatenate(own["down"], axis=0),
-        small[:, P_SIZE : P_SIZE + PD].T,
+        down_grad.reshape(ff_width, D),
+        small[:, P_SIZE + total_images : P_SIZE + total_images + PD].T,
         small[:, rest : rest + 2 * PD],
         jnp.concatenate([small[:, :P_SIZE].T, class_rows], axis=0),
         small[:, rest + 2 * PD : rest + 2 * PD + 6].T,
     )
-    square_local = sum(jnp.sum(shard * shard) for shard in shards)
-    totals = jnp.concatenate([sums_zero[:3], sums_one[:3], jnp.stack([loss_local, square_local])])[None]
-    totals = seq.wait(seq.launch(sum_steps(totals)))[0]
+    totals = seq.wait(totals_flight)[0]
     loss_sum = totals[6] + seq.token
     grad_norm = jnp.sqrt(totals[7])
     activity = jnp.sqrt(totals[:6].reshape(2, 3) / (total_images * P_SIZE * D))

time: 714 us -> 637 us (0.89)
  Pallas kernels: 225 us -> 158 us
  waiting for transfers between devices: 251 us -> 222 us
  starting transfers between devices: 57.1 us -> 80.8 us
  local copies, waits for them, and re-layouts: 70.7 us -> 93.4 us
  other arithmetic: 68.6 us -> 47.7 us
    unnamed x132 -> x334, local copies, waits for them, and re-layouts: 13.2 us -> 63.3 us
    ppermute x64 -> x71, waiting for transfers between devices: 251 us -> 222 us  [exchange(): return lax.ppermute(value, axis, swap_pairs(lax.axis_size(axis), bit))]
    pallas_call x12 -> x13, Pallas kernels: 111 us -> 82 us  [the longest x2 19.8 us: up_back(): call(up_back_kernel, 'up_back', 8 * rows * D * FF_HALF, grid=(2 * STEPS,)...]
    ppermute x64 -> x71, starting transfers between devices: 57 us -> 80.8 us  [exchange(): return lax.ppermute(value, axis, swap_pairs(lax.axis_size(axis), bit))]
    reduce_sum x13 -> x2, other arithmetic: 13.4 us -> 0.25 us  [block_forward(): jnp.sum(jnp.concatenate([one[:1], two[:1], one[1:2]], axis=0), axis=1)]
    pallas_call x2, Pallas kernels: 27.9 us -> 18.9 us  [first_grads(): call(lambda *refs: first_grad_kernel(steps, *refs), 'first_weight_grad',...]
    slice x5 -> x9, local copies, waits for them, and re-layouts: 10.2 us -> 2.27 us  [the longest x2 1.43 us: body(): loss_local = sums_one[4] + sums_zero[3] + sums_one[3]]
  transfers between devices with their start and end apart: 66 -> 72, of which waited for: 37 -> 43; matrix products, arithmetic and copies ran while one was open for 8% -> 6% of each run, Pallas kernels for 17% -> 17%
where the time goes in v2:
time: 637 us; the launch traced here: 627 us
  waiting for transfers between devices  222 us (35%)
  Pallas kernels  158 us (25%)
  local copies, waits for them, and re-layouts  93.4 us (15%)
  starting transfers between devices  80.8 us (13%)
  other arithmetic  47.7 us (7%)
  between operations  22.5 us (4%)
    ppermute x71, waiting for transfers between devices, exchange(): return lax.ppermute(value, axis, swap_pairs(lax.axis_size(axis), bit))  222 us
    ppermute x71, starting transfers between devices, exchange(): return lax.ppermute(value, axis, swap_pairs(lax.axis_size(axis), bit))  80.8 us
    unnamed x334, local copies, waits for them, and re-layouts  63.3 us
    pallas_call x2, Pallas kernels, up_back(): call(up_back_kernel, 'up_back', 8 * rows * D * FF_HALF, grid=(2 * STEPS,)...  19.8 us
    pallas_call x2, Pallas kernels, first_grads(): call(lambda *refs: first_grad_kernel(steps, *refs), 'first_weight_grad',...  18.9 us
    pallas_call x2, Pallas kernels, attend_back(): pl.pallas_call(attend_back_kernel, grid=(count, PAIRS), in_specs=part + [...  18.7 us
    pallas_call x2, Pallas kernels, up_halves(): call(up_kernel, 'up_gelu', 4 * rows * D * FF_HALF, grid=(2 * STEPS,), in_...  17.6 us
    pallas_call x2, Pallas kernels, attend(): pl.pallas_call(attend_kernel, grid=(count, PAIRS), in_specs=part, out_spe...  16.9 us
  transfers between devices with their start and end apart: 72, of which 43 were waited for; matrix products, arithmetic and copies ran while one was open for 6% of the time, Pallas kernels for 17%

profile of v2, /device:TPU:0, one launch (start us, length us, event | category | flops | bytes accessed | tf_op | source)
XLA Modules:
  0.0 627.2 jit_solution(4280605765819949453)
XLA Ops:
  34.3 10.2 %collective-permute-done.10 = bf16[48,1536]{1,0:T(8,128)(2,1)S(1)} collective-permute-done((bf16[48,1536]{1,0:T(8,128)(2,1)S(1)}, bf16[48,1536]{1,0:T(8,128)(2,1)S(1)}, u32[]{:S(2)}, u32[]{:S(2)}) %collective-permute-start.10) | collective-permute-done | bytes 147488 | tf_op jit(solution)/shard_map/ppermute | solution.py:50
  50.6 11.2 %collective-permute-done.12 = bf16[2,48,1536]{2,1,0:T(8,128)(2,1)S(1)} collective-permute-done((bf16[2,48,1536]{2,1,0:T(8,128)(2,1)S(1)}, bf16[2,48,1536]{2,1,0:T(8,128)(2,1)S(1)}, u32[]{:S(2)}, u32[]{:S(2)}) %collective-permute-start.12) | collective-permute-done | bytes 294944 | tf_op jit(solution)/shard_map/ppermute | solution.py:50
  68.5 7.4 %collective-permute-start.18 = (bf16[48,256]{1,0:T(8,128)(2,1)S(1)}, bf16[48,256]{1,0:T(8,128)(2,1)S(1)}, u32[]{:S(2)}, u32[]{:S(2)}) collective-permute-start(bf16[48,256]{1,0:T(8,128)(2,1)S(1)} %pad_maximum_fusion.25), channel_id=1, source_target_pairs={{0,16},{2,18},{4,20},{6,22},{8,24},{10,26},{12,28},{14,30},{16,0},... | collective-permute-start | bytes 73736 | tf_op jit(solution)/shard_map/ppermute | solution.py:50
  75.8 10.7 %collective-permute-done.18 = bf16[48,256]{1,0:T(8,128)(2,1)S(1)} collective-permute-done((bf16[48,256]{1,0:T(8,128)(2,1)S(1)}, bf16[48,256]{1,0:T(8,128)(2,1)S(1)}, u32[]{:S(2)}, u32[]{:S(2)}) %collective-permute-start.18) | collective-permute-done | bytes 24608 | tf_op jit(solution)/shard_map/ppermute | solution.py:50
  94.3 45.6 %collective-permute-done.22 = bf16[2,48,256]{2,1,0:T(8,128)(2,1)S(1)} collective-permute-done((bf16[2,48,256]{2,1,0:T(8,128)(2,1)S(1)}, bf16[2,48,256]{2,1,0:T(8,128)(2,1)S(1)}, u32[]{:S(2)}, u32[]{:S(2)}) %collective-permute-start.22) | collective-permute-done | bytes 49184 | tf_op jit(solution)/shard_map/ppermute | solution.py:50
  152.0 8.3 %collective-permute-done.25 = bf16[2,2,2,48,256]{4,3,0,1,2:T(8,128)(2,1)S(1)} collective-permute-done((bf16[2,2,2,48,256]{4,3,0,1,2:T(8,128)(2,1)S(1)}, bf16[2,2,2,48,256]{4,3,0,1,2:T(8,128)(2,1)S(1)}, u32[]{:S(2)}, u32[]{:S(2)}) %collective-permute-start.25) | collective-permute-done | bytes 196640 | tf_op jit(solution)/shard_map/ppermute | solution.py:50
  180.1 8.5 %attention.2 = (bf16[512,768]{1,0:T(8,128)(2,1)S(1)}, bf16[2,12,256,256]{3,2,1,0:T(8,128)(2,1)S(1)}) custom-call(bf16[512,2304]{1,0:T(8,128)(2,1)S(1)} %get-tuple-element.868.q_ref.k_ref.v_ref, bf16[512,2304]{1,0:T(8,128)(2,1)S(1)} %get-tuple-element.868.q_ref.k_ref.v_ref, bf16[512,2304]{1,0:T(8,128)(2,1)S(1)} %get-tuple-element.868.q_ref.k_ref.v_ref), custom_call_target="tpu_custom_call" | custom-call | flops 805306368 | bytes 6291456 | tf_op jit(solution)/shard_map/attention/pallas_call | solution.py:761
  191.6 9.4 %up_gelu.2 = (bf16[512,1536]{1,0:T(8,128)(2,1)S(1)}, bf16[512,1536]{1,0:T(8,128)(2,1)S(1)}, bf16[512,1536]{1,0:T(8,128)(2,1)S(1)}, bf16[512,1536]{1,0:T(8,128)(2,1)S(1)}) custom-call(bf16[512,768]{1,0:T(8,128)(2,1)S(1)} %get-tuple-element.618.x_ref.normed_ref, bf16[768,1536]{1,0:T(8,128)(2,1)S(1)} %bitcast.514, ...), custom_call_target="tpu_custom_call" | custom-call | flops 2415919104 | bytes 9437184 | tf_op jit(solution)/shard_map/up_gelu/pallas_call | solution.py:432
  213.9 7.4 %down_norm_head.2 = (f32[512,768]{1,0:T(8,128)S(1)}, bf16[512,768]{1,0:T(8,128)(2,1)S(1)}, f32[512,48]{1,0:T(8,128)S(1)}, f32[512,48]{1,0:T(8,128)S(1)}, f32[512,48]{1,0:T(8,128)S(1)}, /*index=5*/f32[8,768]{1,0:T(8,128)S(1)}) custom-call(bf16[512,1536]{1,0:T(8,128)(2,1)S(1)} %copy-done.36, bf16[512,1536]{1,0:T(8,128)(2,1)S(1)} %copy-done.39, ...), custom_call_target="tpu_custom_call" | custom-call | flops 2415919104 | bytes 9437184 | tf_op jit(solution)/shard_map/down_norm_head/pallas_call | solution.py:476
  231.8 8.5 %attention.3 = (bf16[512,768]{1,0:T(8,128)(2,1)S(1)}, bf16[2,12,256,256]{3,2,1,0:T(8,128)(2,1)S(1)}) custom-call(bf16[512,2304]{1,0:T(8,128)(2,1)S(1)} %get-tuple-element.762.q_ref.k_ref.v_ref, bf16[512,2304]{1,0:T(8,128)(2,1)S(1)} %get-tuple-element.762.q_ref.k_ref.v_ref, bf16[512,2304]{1,0:T(8,128)(2,1)S(1)} %get-tuple-element.762.q_ref.k_ref.v_ref), custom_call_target="tpu_custom_call" | custom-call | flops 805306368 | bytes 6291456 | tf_op jit(solution)/shard_map/attention/pallas_call | solution.py:761
  247.5 8.2 %up_gelu.3 = (bf16[512,1536]{1,0:T(8,128)(2,1)S(1)}, bf16[512,1536]{1,0:T(8,128)(2,1)S(1)}, bf16[512,1536]{1,0:T(8,128)(2,1)S(1)}, bf16[512,1536]{1,0:T(8,128)(2,1)S(1)}) custom-call(bf16[512,768]{1,0:T(8,128)(2,1)S(1)} %get-tuple-element.688.x_ref.normed_ref, bf16[768,4992]{1,0:T(8,128)(2,1)S(1)} %bitcast.510, bf16[768,4992]{1,0:T(8,128)(2,1)S(1)} %copy-done.7), custom_call_target="tpu_custom_call" | custom-call | flops 2415919104 | bytes 9437184 | tf_op jit(solution)/shard_map/up_gelu/pallas_call | solution.py:432
  264.6 7.7 %down_norm_head.3 = (f32[512,768]{1,0:T(8,128)S(1)}, bf16[512,768]{1,0:T(8,128)(2,1)S(1)}, f32[512,48]{1,0:T(8,128)S(1)}, f32[512,48]{1,0:T(8,128)S(1)}, f32[512,48]{1,0:T(8,128)}, /*index=5*/f32[8,768]{1,0:T(8,128)S(1)}) custom-call(bf16[512,1536]{1,0:T(8,128)(2,1)S(1)} %copy-done.56, bf16[512,1536]{1,0:T(8,128)(2,1)S(1)} %get-tuple-element.731.active_two.two_ref, ...), custom_call_target="tpu_custom_call" | custom-call | flops 2415919104 | bytes 9437184 | tf_op jit(solution)/shard_map/down_norm_head/pallas_call | solution.py:476
  283.8 10.0 %up_back.2 = (bf16[512,1536]{1,0:T(8,128)(2,1)S(1)}, bf16[512,1536]{1,0:T(8,128)(2,1)S(1)}, bf16[768,1536]{1,0:T(8,128)(2,1)S(1)}, bf16[768,1536]{1,0:T(8,128)(2,1)}) custom-call(bf16[512,768]{1,0:T(8,128)(2,1)S(1)} %get-tuple-element.737.low_ref, bf16[512,768]{1,0:T(8,128)(2,1)S(1)} %get-tuple-element.688.x_ref.normed_ref, bf16[768,4992]{1,0:T(8,128)(2,1)S(1)} %bitcast.512, ...), custom_call_target="tpu_custom_call" | custom-call | flops 4831838208 | bytes 18874368 | tf_op jit(solution)/shard_map/up_back/pallas_call | solution.py:577
  310.1 7.2 %middle_back.2 = (f32[512,768]{1,0:T(8,128)S(1)}, bf16[512,768]{1,0:T(8,128)(2,1)S(1)}, bf16[512,768]{1,0:T(8,128)(2,1)S(1)}, f32[8,768]{1,0:T(8,128)S(1)}) custom-call(bf16[512,1536]{1,0:T(8,128)(2,1)S(1)} %copy-done.48, bf16[512,1536]{1,0:T(8,128)(2,1)S(1)} %copy-done.50, bf16[768,4992]{1,0:T(8,128)(2,1)S(1)} %copy-done.5, bf16[768,4992]{1,0:T(8,128)(2,1)} %copy-done.6, ...), custom_call_target="tpu_custom_call" | custom-call | flops 2415919104 | bytes 9437184 | tf_op jit(solution)/shard_map/middle_back/pallas_call | solution.py:605
  317.3 9.4 %attention_back.2.joint_ref.refs_4_ = bf16[512,2304]{1,0:T(8,128)(2,1)S(1)} custom-call(bf16[512,2304]{1,0:T(8,128)(2,1)S(1)} %copy-done.11, bf16[512,2304]{1,0:T(8,128)(2,1)S(1)} %copy-done.11, bf16[512,2304]{1,0:T(8,128)(2,1)S(1)} %copy-done.11, bf16[2,12,256,256]{3,2,1,0:T(8,128)(2,1)S(1)} %copy-done.27, bf16[512,768]{1,0:T(8,128)(2,1)S(1)} %get-tuple-element.764.grad_ref), custom_call_target="tpu_custom_call" | custom-call | flops 1610612736 | bytes 8650752 | tf_op jit(solution)/shard_map/attention_back/pallas_call | solution.py:808
  340.6 8.8 %first_weight_grad.2 = (bf16[768,1792]{1,0:T(8,128)(2,1)S(1)}, bf16[768,1792]{1,0:T(8,128)(2,1)S(1)}) custom-call(s32[1]{0:T(128)} %bitcast.67.refs_0_, bf16[512,768]{1,0:T(8,128)(2,1)S(1)} %copy-done.74, bf16[512,768]{1,0:T(8,128)(2,1)S(1)} %copy-done.62, bf16[512,768]{1,0:T(8,128)(2,1)S(1)} %get-tuple-element.786.refs_3_, ...), custom_call_target="tpu_custom_call" | custom-call | flops 2818572288 | bytes 11010048 | tf_op jit(solution)/shard_map/first_weight_grad/pallas_call | solution.py:706
  350.0 17.3 %collective-permute-done.31 = bf16[2,2,2,48,1536]{4,3,0,2,1:T(8,128)(2,1)S(1)} collective-permute-done((bf16[2,2,2,48,1536]{4,3,0,2,1:T(8,128)(2,1)S(1)}, bf16[2,2,2,48,1536]{4,3,0,2,1:T(8,128)(2,1)S(1)}, u32[]{:S(2)}, u32[]{:S(2)}) %collective-permute-start.31) | collective-permute-done | bytes 1179680 | tf_op jit(solution)/shard_map/ppermute | solution.py:50
  394.6 9.8 %up_back.3 = (bf16[512,1536]{1,0:T(8,128)(2,1)S(1)}, bf16[512,1536]{1,0:T(8,128)(2,1)S(1)}, bf16[768,1536]{1,0:T(8,128)(2,1)S(1)}, bf16[768,1536]{1,0:T(8,128)(2,1)}) custom-call(bf16[512,768]{1,0:T(8,128)(2,1)S(1)} %copy-done.76, bf16[512,768]{1,0:T(8,128)(2,1)S(1)} %copy-done.72, bf16[768,1536]{1,0:T(8,128)(2,1)} %bitcast.54.down_one.refs_0_, ...), custom_call_target="tpu_custom_call" | custom-call | flops 4831838208 | bytes 18874368 | tf_op jit(solution)/shard_map/up_back/pallas_call | solution.py:577
  404.5 7.5 %middle_back.3 = (f32[512,768]{1,0:T(8,128)S(1)}, bf16[512,768]{1,0:T(8,128)(2,1)S(1)}, bf16[512,768]{1,0:T(8,128)(2,1)S(1)}, f32[8,768]{1,0:T(8,128)S(1)}) custom-call(bf16[512,1536]{1,0:T(8,128)(2,1)S(1)} %get-tuple-element.845.one_ref, bf16[512,1536]{1,0:T(8,128)(2,1)S(1)} %get-tuple-element.846.two_ref, bf16[768,1536]{1,0:T(8,128)(2,1)S(1)} %bitcast.515, ...), custom_call_target="tpu_custom_call" | custom-call | flops 2415919104 | bytes 9437184 | tf_op jit(solution)/shard_map/middle_back/pallas_call | solution.py:605
  430.2 9.3 %attention_back.3.joint_ref.refs_4_ = bf16[512,2304]{1,0:T(8,128)(2,1)S(1)} custom-call(bf16[512,2304]{1,0:T(8,128)(2,1)S(1)} %copy-done.9, bf16[512,2304]{1,0:T(8,128)(2,1)S(1)} %copy-done.9, bf16[512,2304]{1,0:T(8,128)(2,1)S(1)} %copy-done.9, bf16[2,12,256,256]{3,2,1,0:T(8,128)(2,1)S(1)} %copy-done.25, bf16[512,768]{1,0:T(8,128)(2,1)S(1)} %get-tuple-element.870.grad_ref), custom_call_target="tpu_custom_call" | custom-call | flops 1610612736 | bytes 8650752 | tf_op jit(solution)/shard_map/attention_back/pallas_call | solution.py:808
  450.8 7.2 %collective-permute-done.40 = bf16[48,1536]{1,0:T(8,128)(2,1)S(1)} collective-permute-done((bf16[48,1536]{1,0:T(8,128)(2,1)S(1)}, bf16[48,1536]{1,0:T(8,128)(2,1)S(1)}, u32[]{:S(2)}, u32[]{:S(2)}) %collective-permute-start.40) | collective-permute-done | bytes 147488 | tf_op jit(solution)/shard_map/ppermute | solution.py:50
  464.6 10.1 %first_weight_grad.3 = (bf16[768,1792]{1,0:T(8,128)(2,1)S(1)}, bf16[768,1792]{1,0:T(8,128)(2,1)}) custom-call(s32[1]{0:T(128)} %bitcast.67.refs_0_, bf16[512,768]{1,0:T(8,128)(2,1)S(1)} %copy-done.70, bf16[512,768]{1,0:T(8,128)(2,1)S(1)} %copy-done.58, bf16[512,768]{1,0:T(8,128)(2,1)S(1)} %get-tuple-element.892.refs_3_, ...), custom_call_target="tpu_custom_call" | custom-call | flops 2818572288 | bytes 11010048 | tf_op jit(solution)/shard_map/first_weight_grad/pallas_call | solution.py:706
  481.0 7.2 %collective-permute-done.45 = bf16[2,48,1792]{2,1,0:T(8,128)(2,1)S(1)} collective-permute-done((bf16[2,48,1792]{2,1,0:T(8,128)(2,1)S(1)}, bf16[2,48,1792]{2,1,0:T(8,128)(2,1)S(1)}, u32[]{:S(2)}, u32[]{:S(2)}) %collective-permute-start.45) | collective-permute-done | bytes 344096 | tf_op jit(solution)/shard_map/ppermute | solution.py:50
  501.8 13.8 %collective-permute-done.48 = bf16[48,1792]{1,0:T(8,128)(2,1)S(1)} collective-permute-done((bf16[48,1792]{1,0:T(8,128)(2,1)S(1)}, bf16[48,1792]{1,0:T(8,128)(2,1)S(1)}, u32[]{:S(2)}, u32[]{:S(2)}) %collective-permute-start.48) | collective-permute-done | bytes 172064 | tf_op jit(solution)/shard_map/ppermute | solution.py:50
  (705 shorter events, 344.2 us)
Async XLA Ops:
  7.2 198.5 %all-gather.2.cloned.1.call-start = ((), (), s32[]{:S(2)}) async-start(), calls=%async_computation | async-start | bytes 8146944 | tf_op jit(solution)/shard_map/all_gather | solution.py:1029
  44.7 17.7 %collective-permute-start.11 = (bf16[2,48,1920]{2,1,0:T(8,128)(2,1)S(1)}, bf16[2,48,1920]{2,1,0:T(8,128)(2,1)S(1)}, u32[]{:S(2)}, u32[]{:S(2)}) collective-permute-start(bf16[2,48,1920]{2,1,0:T(8,128)(2,1)S(1)} %pad_maximum_fusion.17), channel_id=1, source_target_pairs={{0,8},{2,10},{4,12},{6,14},{8,0},{10,2},{12,4},{14,6},{16,24},{18,... | collective-permute-start | bytes 1105928 | tf_op jit(solution)/shard_map/ppermute | solution.py:50
  62.9 25.8 %collective-permute-start.15 = (bf16[2,2,48,1920]{3,2,0,1:T(8,128)(2,1)S(1)}, bf16[2,2,48,1920]{3,2,0,1:T(8,128)(2,1)S(1)}, u32[]{:S(2)}, u32[]{:S(2)}) collective-permute-start(bf16[2,2,48,1920]{3,2,0,1:T(8,128)(2,1)S(1)} %pad_maximum_fusion.8), channel_id=1, source_target_pairs={{0,4},{2,6},{4,0},{6,2},{8,12},{10,14},{12,8},{14,10},{16,20},{18,... | collective-permute-start | bytes 2211848 | tf_op jit(solution)/shard_map/ppermute | solution.py:50
  64.5 24.2 %collective-permute-start.16 = (bf16[2,2,48,1536]{3,2,1,0:T(8,128)(2,1)S(1)}, bf16[2,2,48,1536]{3,2,1,0:T(8,128)(2,1)S(1)}, u32[]{:S(2)}, u32[]{:S(2)}) collective-permute-start(bf16[2,2,48,1536]{3,2,1,0:T(8,128)(2,1)S(1)} %pad_maximum_fusion.9), channel_id=1, source_target_pairs={{0,8},{2,10},{4,12},{6,14},{8,0},{10,2},{12,4},{14,6},{16,24},{18,... | collective-permute-start | bytes 1769480 | tf_op jit(solution)/shard_map/ppermute | solution.py:50
  66.9 21.8 %collective-permute-start.17 = (bf16[2,2,48,1536]{3,2,0,1:T(8,128)(2,1)S(1)}, bf16[2,2,48,1536]{3,2,0,1:T(8,128)(2,1)S(1)}, u32[]{:S(2)}, u32[]{:S(2)}) collective-permute-start(bf16[2,2,48,1536]{3,2,0,1:T(8,128)(2,1)S(1)} %pad_maximum_fusion.10), channel_id=1, source_target_pairs={{0,2},{2,0},{4,6},{6,4},{8,10},{10,8},{12,14},{14,12},{16,18},{18,... | collective-permute-start | bytes 1769480 | tf_op jit(solution)/shard_map/ppermute | solution.py:50
  68.5 18.0 %collective-permute-start.18 = (bf16[48,256]{1,0:T(8,128)(2,1)S(1)}, bf16[48,256]{1,0:T(8,128)(2,1)S(1)}, u32[]{:S(2)}, u32[]{:S(2)}) collective-permute-start(bf16[48,256]{1,0:T(8,128)(2,1)S(1)} %pad_maximum_fusion.25), channel_id=1, source_target_pairs={{0,16},{2,18},{4,20},{6,22},{8,24},{10,26},{12,28},{14,30},{16,0},... | collective-permute-start | bytes 73736 | tf_op jit(solution)/shard_map/ppermute | solution.py:50
  89.6 50.4 %collective-permute-start.19 = (bf16[2,2,2,48,1920]{4,3,0,1,2:T(8,128)(2,1)S(1)}, bf16[2,2,2,48,1920]{4,3,0,1,2:T(8,128)(2,1)S(1)}, u32[]{:S(2)}, u32[]{:S(2)}) collective-permute-start(bf16[2,2,2,48,1920]{4,3,0,1,2:T(8,128)(2,1)S(1)} %pad_maximum_fusion.5), channel_id=1, source_target_pairs={{0,2},{2,0},{4,6},{6,4},{8,10},{10,8},{12,14},{14,12},{16,18},{18,... | collective-permute-start | bytes 4423688 | tf_op jit(solution)/shard_map/ppermute | solution.py:50
  91.1 48.9 %collective-permute-start.20 = (bf16[2,2,2,48,1536]{4,3,2,0,1:T(8,128)(2,1)S(1)}, bf16[2,2,2,48,1536]{4,3,2,0,1:T(8,128)(2,1)S(1)}, u32[]{:S(2)}, u32[]{:S(2)}) collective-permute-start(bf16[2,2,2,48,1536]{4,3,2,0,1:T(8,128)(2,1)S(1)} %pad_maximum_fusion.6), channel_id=1, source_target_pairs={{0,4},{2,6},{4,0},{6,2},{8,12},{10,14},{12,8},{14,10},{16,20},{18,... | collective-permute-start | bytes 3538952 | tf_op jit(solution)/shard_map/ppermute | solution.py:50
  92.3 47.7 %collective-permute-start.21 = (bf16[2,2,2,48,1536]{4,3,0,1,2:T(8,128)(2,1)S(1)}, bf16[2,2,2,48,1536]{4,3,0,1,2:T(8,128)(2,1)S(1)}, u32[]{:S(2)}, u32[]{:S(2)}) collective-permute-start(bf16[2,2,2,48,1536]{4,3,0,1,2:T(8,128)(2,1)S(1)} %pad_maximum_fusion.7), channel_id=1, source_target_pairs={{0,8},{2,10},{4,12},{6,14},{8,0},{10,2},{12,4},{14,6},{16,24},{18,... | collective-permute-start | bytes 3538952 | tf_op jit(solution)/shard_map/ppermute | solution.py:50
  92.3 47.7 %collective-permute-start.22 = (bf16[2,48,256]{2,1,0:T(8,128)(2,1)S(1)}, bf16[2,48,256]{2,1,0:T(8,128)(2,1)S(1)}, u32[]{:S(2)}, u32[]{:S(2)}) collective-permute-start(bf16[2,48,256]{2,1,0:T(8,128)(2,1)S(1)} %pad_maximum_fusion.24), channel_id=1, source_target_pairs={{0,8},{2,10},{4,12},{6,14},{8,0},{10,2},{12,4},{14,6},{16,24},{18,... | collective-permute-start | bytes 147464 | tf_op jit(solution)/shard_map/ppermute | solution.py:50
  297.6 31.0 %collective-permute-start.29 = (bf16[768,1536]{1,0:T(8,128)(2,1)}, bf16[768,1536]{1,0:T(8,128)(2,1)}, u32[]{:S(2)}, u32[]{:S(2)}) collective-permute-start(bf16[768,1536]{1,0:T(8,128)(2,1)} %get-tuple-element.766), channel_id=1, source_target_pairs={{0,1},{1,0},{2,3},{3,2},{4,5},{5,4},{6,7},{7,6},{8,9},{9,8},{10,11... | collective-permute-start | bytes 7077896 | tf_op jit(solution)/shard_map/ppermute | solution.py:50
  297.9 30.7 %collective-permute-start.30 = (bf16[768,1536]{1,0:T(8,128)(2,1)}, bf16[768,1536]{1,0:T(8,128)(2,1)}, u32[]{:S(2)}, u32[]{:S(2)}) collective-permute-start(bf16[768,1536]{1,0:T(8,128)(2,1)} %get-tuple-element.767), channel_id=1, source_target_pairs={{0,1},{1,0},{2,3},{3,2},{4,5},{5,4},{6,7},{7,6},{8,9},{9,8},{10,11... | collective-permute-start | bytes 7077896 | tf_op jit(solution)/shard_map/ppermute | solution.py:50
  338.9 28.3 %collective-permute-start.31 = (bf16[2,2,2,48,1536]{4,3,0,2,1:T(8,128)(2,1)S(1)}, bf16[2,2,2,48,1536]{4,3,0,2,1:T(8,128)(2,1)S(1)}, u32[]{:S(2)}, u32[]{:S(2)}) collective-permute-start(bf16[2,2,2,48,1536]{4,3,0,2,1:T(8,128)(2,1)S(1)} %fusion.4), channel_id=1, source_target_pairs={{0,2},{2,0},{4,6},{6,4},{8,10},{10,8},{12,14},{14,12},{16,18},{18,... | collective-permute-start | bytes 3538952 | tf_op jit(solution)/shard_map/ppermute | solution.py:50
  340.4 27.9 %collective-permute-start.32 = (bf16[2,2,2,48,1536]{4,3,0,2,1:T(8,128)(2,1)S(1)}, bf16[2,2,2,48,1536]{4,3,0,2,1:T(8,128)(2,1)S(1)}, u32[]{:S(2)}, u32[]{:S(2)}) collective-permute-start(bf16[2,2,2,48,1536]{4,3,0,2,1:T(8,128)(2,1)S(1)} %fusion.5), channel_id=1, source_target_pairs={{0,4},{2,6},{4,0},{6,2},{8,12},{10,14},{12,8},{14,10},{16,20},{18,... | collective-permute-start | bytes 3538952 | tf_op jit(solution)/shard_map/ppermute | solution.py:50
  389.6 32.9 %collective-permute-start.39 = (bf16[768,1536]{1,0:T(8,128)(2,1)}, bf16[768,1536]{1,0:T(8,128)(2,1)}, u32[]{:S(2)}, u32[]{:S(2)}) collective-permute-start(bf16[768,1536]{1,0:T(8,128)(2,1)} %get-tuple-element.856), channel_id=1, source_target_pairs={{0,1},{1,0},{2,3},{3,2},{4,5},{5,4},{6,7},{7,6},{8,9},{9,8},{10,11... | collective-permute-start | bytes 7077896 | tf_op jit(solution)/shard_map/ppermute | solution.py:50
  389.6 32.9 %collective-permute-start.38 = (bf16[2,2,2,48,1792]{4,3,0,2,1:T(8,128)(2,1)}, bf16[2,2,2,48,1792]{4,3,0,2,1:T(8,128)(2,1)}, u32[]{:S(2)}, u32[]{:S(2)}) collective-permute-start(bf16[2,2,2,48,1792]{4,3,0,2,1:T(8,128)(2,1)} %fusion.1), channel_id=1, source_target_pairs={{0,2},{2,0},{4,6},{6,4},{8,10},{10,8},{12,14},{14,12},{16,18},{18,... | collective-permute-start | bytes 4128776 | tf_op jit(solution)/shard_map/ppermute | solution.py:50
  426.7 34.8 %collective-permute-start.44 = (bf16[768,1536]{1,0:T(8,128)(2,1)}, bf16[768,1536]{1,0:T(8,128)(2,1)S(1)}, u32[]{:S(2)}, u32[]{:S(2)}) collective-permute-start(bf16[768,1536]{1,0:T(8,128)(2,1)} %get-tuple-element.882), channel_id=1, source_target_pairs={{0,1},{1,0},{2,3},{3,2},{4,5},{5,4},{6,7},{7,6},{8,9},{9,8},{10,11... | collective-permute-start | bytes 7077896 | tf_op jit(solution)/shard_map/ppermute | solution.py:50
  426.8 34.7 %collective-permute-start.43 = (bf16[2,2,2,48,1536]{4,3,0,2,1:T(8,128)(2,1)S(1)}, bf16[2,2,2,48,1536]{4,3,0,2,1:T(8,128)(2,1)S(1)}, u32[]{:S(2)}, u32[]{:S(2)}) collective-permute-start(bf16[2,2,2,48,1536]{4,3,0,2,1:T(8,128)(2,1)S(1)} %fusion.6), channel_id=1, source_target_pairs={{0,8},{2,10},{4,12},{6,14},{8,0},{10,2},{12,4},{14,6},{16,24},{18,... | collective-permute-start | bytes 3538952 | tf_op jit(solution)/shard_map/ppermute | solution.py:50
  439.6 18.4 %collective-permute-start.40 = (bf16[48,1536]{1,0:T(8,128)(2,1)S(1)}, bf16[48,1536]{1,0:T(8,128)(2,1)S(1)}, u32[]{:S(2)}, u32[]{:S(2)}) collective-permute-start(bf16[48,1536]{1,0:T(8,128)(2,1)S(1)} %fusion.85), channel_id=1, source_target_pairs={{0,16},{2,18},{4,20},{6,22},{8,24},{10,26},{12,28},{14,30},{16,0},... | collective-permute-start | bytes 442376 | tf_op jit(solution)/shard_map/ppermute | solution.py:50
  462.5 27.6 %collective-permute-start.47 = (bf16[2,2,2,48,1536]{4,3,0,2,1:T(8,128)(2,1)S(1)}, bf16[2,2,2,48,1536]{4,3,0,2,1:T(8,128)(2,1)S(1)}, u32[]{:S(2)}, u32[]{:S(2)}) collective-permute-start(bf16[2,2,2,48,1536]{4,3,0,2,1:T(8,128)(2,1)S(1)} %fusion.7), channel_id=1, source_target_pairs={{0,4},{2,6},{4,0},{6,2},{8,12},{10,14},{12,8},{14,10},{16,20},{18,... | collective-permute-start | bytes 3538952 | tf_op jit(solution)/shard_map/ppermute | solution.py:50
  463.3 25.0 %collective-permute-start.46 = (bf16[2,2,48,1536]{3,2,1,0:T(8,128)(2,1)S(1)}, bf16[2,2,48,1536]{3,2,1,0:T(8,128)(2,1)S(1)}, u32[]{:S(2)}, u32[]{:S(2)}) collective-permute-start(bf16[2,2,48,1536]{3,2,1,0:T(8,128)(2,1)S(1)} %copy.219), channel_id=1, source_target_pairs={{0,2},{2,0},{4,6},{6,4},{8,10},{10,8},{12,14},{14,12},{16,18},{18,... | collective-permute-start | bytes 1769480 | tf_op jit(solution)/shard_map/ppermute | solution.py:50
  491.3 25.0 %collective-permute-start.51 = (bf16[768,1792]{1,0:T(8,128)(2,1)}, bf16[768,1792]{1,0:T(8,128)(2,1)}, u32[]{:S(2)}, u32[]{:S(2)}) collective-permute-start(bf16[768,1792]{1,0:T(8,128)(2,1)} %get-tuple-element.914), channel_id=1, source_target_pairs={{0,1},{1,0},{2,3},{3,2},{4,5},{5,4},{6,7},{7,6},{8,9},{9,8},{10,11... | collective-permute-start | bytes 8257544 | tf_op jit(solution)/shard_map/ppermute | solution.py:50
  493.0 22.6 %collective-permute-start.49 = (bf16[2,48,1536]{2,1,0:T(8,128)(2,1)S(1)}, bf16[2,48,1536]{2,1,0:T(8,128)(2,1)S(1)}, u32[]{:S(2)}, u32[]{:S(2)}) collective-permute-start(bf16[2,48,1536]{2,1,0:T(8,128)(2,1)S(1)} %get-tuple-element.912), channel_id=1, source_target_pairs={{0,4},{2,6},{4,0},{6,2},{8,12},{10,14},{12,8},{14,10},{16,20},{18,... | collective-permute-start | bytes 884744 | tf_op jit(solution)/shard_map/ppermute | solution.py:50
  493.7 22.7 %collective-permute-start.50 = (bf16[2,2,48,1536]{3,2,1,0:T(8,128)(2,1)S(1)}, bf16[2,2,48,1536]{3,2,1,0:T(8,128)(2,1)S(1)}, u32[]{:S(2)}, u32[]{:S(2)}) collective-permute-start(bf16[2,2,48,1536]{3,2,1,0:T(8,128)(2,1)S(1)} %copy.224), channel_id=1, source_target_pairs={{0,8},{2,10},{4,12},{6,14},{8,0},{10,2},{12,4},{14,6},{16,24},{18,... | collective-permute-start | bytes 1769480 | tf_op jit(solution)/shard_map/ppermute | solution.py:50
  (209 other events, 1286.2 us)
Sparse Core Ops, SparseCore 0:
  49.6 130.1 all-gather.1

commit v3 on v2

--- a/solution.py
+++ b/solution.py
@@ -38,7 +38,7 @@
 PAIRS = H // 2
 TILE = D
 FF_HALF = FF // 2
-VMEM_BYTES = 30 << 20
+VMEM_BYTES = 26 << 20
 
 
 def swap_pairs(count, bit):
@@ -60,7 +60,7 @@
 
 GATHER_ORDERS = ({"first": (0, 1, 2, 3), "up": (1, 2, 3, 0), "down": (2, 0, 1, 3)},)
 SCATTER_ORDERS = (
-    {"down": (2, 0, 1, 3), "up": (1, 2, 0, 3), "first": (0, 1, 2, 3), "last": (1, 2, 0, 3)},
+    {"down": (0, 2, 1, 3), "up": (1, 0, 2, 3), "first": (0, 1, 2, 3), "last": (1, 2, 0, 3)},
     {"down": (0, 2, 1, 3), "up": (1, 0, 2, 3), "first": (0, 1, 2, 3)},
 )
 
@@ -279,7 +279,7 @@
     return pl.pallas_call(
         kernel,
         name=name,
-        cost_estimate=pl.CostEstimate(flops=flops, bytes_accessed=flops // 256, transcendentals=0),
+        cost_estimate=pl.CostEstimate(flops=0, bytes_accessed=0, transcendentals=0),
         compiler_params=pltpu.CompilerParams(vmem_limit_bytes=VMEM_BYTES),
         **fields,
     )
@@ -770,11 +770,7 @@
             jax.ShapeDtypeStruct((joint.shape[0], D), BF),
             jax.ShapeDtypeStruct((count, H, P_SIZE, P_SIZE), BF),
         ],
-        cost_estimate=pl.CostEstimate(
-            flops=8 * count * H * P_SIZE * P_SIZE * HD,
-            bytes_accessed=2 * count * H * P_SIZE * P_SIZE + 8 * joint.shape[0] * D,
-            transcendentals=count * H * P_SIZE * P_SIZE,
-        ),
+        cost_estimate=pl.CostEstimate(flops=0, bytes_accessed=0, transcendentals=0),
         compiler_params=pltpu.CompilerParams(vmem_limit_bytes=VMEM_BYTES),
         name="attention",
     )(joint, joint, joint)
@@ -815,11 +811,7 @@
         ],
         out_specs=pl.BlockSpec((P_SIZE, QKV), lambda n, p: (n, 0)),
         out_shape=jax.ShapeDtypeStruct(joint.shape, BF),
-        cost_estimate=pl.CostEstimate(
-            flops=16 * count * H * P_SIZE * P_SIZE * HD,
-            bytes_accessed=2 * count * H * P_SIZE * P_SIZE + 14 * joint.shape[0] * D,
-            transcendentals=0,
-        ),
+        cost_estimate=pl.CostEstimate(flops=0, bytes_accessed=0, transcendentals=0),
         compiler_params=pltpu.CompilerParams(vmem_limit_bytes=VMEM_BYTES),
         name="attention_back",
     )(joint, joint, joint, probs, grad)
@@ -1042,7 +1034,6 @@
     first_halves = seq.wait(flights["first"])
     later = {name: seq.launch(one_step(mine, "section")) for name, mine in mine_of.items()}
     classes = seq.wait(class_flight)
-    seq.turn()
     first = seq.compute(place_halves, is_first, *first_halves)
     classes_of = (classes[:, : 2 * total_images], classes[:, 2 * total_images :])
 

time: 637 us -> 613 us (0.962)
  waiting for transfers between devices: 222 us -> 199 us
    ppermute x71, waiting for transfers between devices: 222 us -> 199 us  [exchange(): return lax.ppermute(value, axis, swap_pairs(lax.axis_size(axis), bit))]
    unnamed x334 -> x330, local copies, waits for them, and re-layouts: 63.3 us -> 58.1 us
  transfers between devices with their start and end apart: 72 -> 72, of which waited for: 43 -> 39; matrix products, arithmetic and copies ran while one was open for 6% -> 7% of each run, Pallas kernels for 17% -> 18%
where the time goes in v3:
time: 613 us; the launch traced here: 604 us
  waiting for transfers between devices  199 us (32%)
  Pallas kernels  157 us (26%)
  local copies, waits for them, and re-layouts  88.9 us (15%)
  starting transfers between devices  81.2 us (13%)
  other arithmetic  52.6 us (9%)
  between operations  22.5 us (4%)
    ppermute x71, waiting for transfers between devices, exchange(): return lax.ppermute(value, axis, swap_pairs(lax.axis_size(axis), bit))  199 us
    ppermute x71, starting transfers between devices, exchange(): return lax.ppermute(value, axis, swap_pairs(lax.axis_size(axis), bit))  81.2 us
    unnamed x330, local copies, waits for them, and re-layouts  58.1 us
    pallas_call x2, Pallas kernels, first_grads(): call(lambda *refs: first_grad_kernel(steps, *refs), 'first_weight_grad',...  18.9 us
    pallas_call x2, Pallas kernels, attend_back(): pl.pallas_call(attend_back_kernel, grid=(count, PAIRS), in_specs=part + [...  18.7 us
    pallas_call x2, Pallas kernels, up_halves(): call(up_kernel, 'up_gelu', 4 * rows * D * FF_HALF, grid=(2 * STEPS,), in_...  17.6 us
    pallas_call x2, Pallas kernels, up_back(): call(up_back_kernel, 'up_back', 8 * rows * D * FF_HALF, grid=(2 * STEPS,)...  17.4 us
    pallas_call x2, Pallas kernels, attend(): pl.pallas_call(attend_kernel, grid=(count, PAIRS), in_specs=part, out_spe...  17.3 us
  transfers between devices with their start and end apart: 72, of which 39 were waited for; matrix products, arithmetic and copies ran while one was open for 7% of the time, Pallas kernels for 18%

profile of v3, /device:TPU:0, one launch (start us, length us, event | category | flops | bytes accessed | tf_op | source)
XLA Modules:
  0.0 603.5 jit_solution(14917307856914902345)
XLA Ops:
  34.3 10.2 %collective-permute-done.10 = bf16[48,1536]{1,0:T(8,128)(2,1)S(1)} collective-permute-done((bf16[48,1536]{1,0:T(8,128)(2,1)S(1)}, bf16[48,1536]{1,0:T(8,128)(2,1)S(1)}, u32[]{:S(2)}, u32[]{:S(2)}) %collective-permute-start.10) | collective-permute-done | bytes 147488 | tf_op jit(solution)/shard_map/ppermute | solution.py:50
  50.6 11.2 %collective-permute-done.12 = bf16[2,48,1536]{2,1,0:T(8,128)(2,1)S(1)} collective-permute-done((bf16[2,48,1536]{2,1,0:T(8,128)(2,1)S(1)}, bf16[2,48,1536]{2,1,0:T(8,128)(2,1)S(1)}, u32[]{:S(2)}, u32[]{:S(2)}) %collective-permute-start.12) | collective-permute-done | bytes 294944 | tf_op jit(solution)/shard_map/ppermute | solution.py:50
  68.5 7.4 %collective-permute-start.18 = (bf16[48,256]{1,0:T(8,128)(2,1)S(1)}, bf16[48,256]{1,0:T(8,128)(2,1)S(1)}, u32[]{:S(2)}, u32[]{:S(2)}) collective-permute-start(bf16[48,256]{1,0:T(8,128)(2,1)S(1)} %pad_maximum_fusion.25), channel_id=1, source_target_pairs={{0,16},{2,18},{4,20},{6,22},{8,24},{10,26},{12,28},{14,30},{16,0},... | collective-permute-start | bytes 73736 | tf_op jit(solution)/shard_map/ppermute | solution.py:50
  75.8 10.7 %collective-permute-done.18 = bf16[48,256]{1,0:T(8,128)(2,1)S(1)} collective-permute-done((bf16[48,256]{1,0:T(8,128)(2,1)S(1)}, bf16[48,256]{1,0:T(8,128)(2,1)S(1)}, u32[]{:S(2)}, u32[]{:S(2)}) %collective-permute-start.18) | collective-permute-done | bytes 24608 | tf_op jit(solution)/shard_map/ppermute | solution.py:50
  94.3 45.7 %collective-permute-done.22 = bf16[2,48,256]{2,1,0:T(8,128)(2,1)S(1)} collective-permute-done((bf16[2,48,256]{2,1,0:T(8,128)(2,1)S(1)}, bf16[2,48,256]{2,1,0:T(8,128)(2,1)S(1)}, u32[]{:S(2)}, u32[]{:S(2)}) %collective-permute-start.22) | collective-permute-done | bytes 49184 | tf_op jit(solution)/shard_map/ppermute | solution.py:50
  174.5 8.5 %attention.2 = (bf16[512,768]{1,0:T(8,128)(2,1)S(1)}, bf16[2,12,256,256]{3,2,1,0:T(8,128)(2,1)S(1)}) custom-call(bf16[512,2304]{1,0:T(8,128)(2,1)S(1)} %get-tuple-element.868.q_ref.k_ref.v_ref, bf16[512,2304]{1,0:T(8,128)(2,1)S(1)} %get-tuple-element.868.q_ref.k_ref.v_ref, bf16[512,2304]{1,0:T(8,128)(2,1)S(1)} %get-tuple-element.868.q_ref.k_ref.v_ref), custom_call_target="tpu_custom_call" | custom-call | tf_op jit(solution)/shard_map/attention/pallas_call | solution.py:761
  187.4 9.4 %up_gelu.2 = (bf16[512,1536]{1,0:T(8,128)(2,1)S(1)}, bf16[512,1536]{1,0:T(8,128)(2,1)S(1)}, bf16[512,1536]{1,0:T(8,128)(2,1)S(1)}, bf16[512,1536]{1,0:T(8,128)(2,1)S(1)}) custom-call(bf16[512,768]{1,0:T(8,128)(2,1)S(1)} %get-tuple-element.618.x_ref.normed_ref, bf16[768,1536]{1,0:T(8,128)(2,1)S(1)} %bitcast.512, ...), custom_call_target="tpu_custom_call" | custom-call | tf_op jit(solution)/shard_map/up_gelu/pallas_call | solution.py:432
  208.6 7.6 %down_norm_head.2 = (f32[512,768]{1,0:T(8,128)S(1)}, bf16[512,768]{1,0:T(8,128)(2,1)S(1)}, f32[512,48]{1,0:T(8,128)S(1)}, f32[512,48]{1,0:T(8,128)S(1)}, f32[512,48]{1,0:T(8,128)S(1)}, /*index=5*/f32[8,768]{1,0:T(8,128)S(1)}) custom-call(bf16[512,1536]{1,0:T(8,128)(2,1)S(1)} %copy-done.18, bf16[512,1536]{1,0:T(8,128)(2,1)S(1)} %copy-done.21, ...), custom_call_target="tpu_custom_call" | custom-call | tf_op jit(solution)/shard_map/down_norm_head/pallas_call | solution.py:476
  229.5 8.9 %attention.3 = (bf16[512,768]{1,0:T(8,128)(2,1)S(1)}, bf16[2,12,256,256]{3,2,1,0:T(8,128)(2,1)S(1)}) custom-call(bf16[512,2304]{1,0:T(8,128)(2,1)S(1)} %get-tuple-element.762.q_ref.k_ref.v_ref, bf16[512,2304]{1,0:T(8,128)(2,1)S(1)} %get-tuple-element.762.q_ref.k_ref.v_ref, bf16[512,2304]{1,0:T(8,128)(2,1)S(1)} %get-tuple-element.762.q_ref.k_ref.v_ref), custom_call_target="tpu_custom_call" | custom-call | tf_op jit(solution)/shard_map/attention/pallas_call | solution.py:761
  242.6 8.2 %up_gelu.3 = (bf16[512,1536]{1,0:T(8,128)(2,1)S(1)}, bf16[512,1536]{1,0:T(8,128)(2,1)S(1)}, bf16[512,1536]{1,0:T(8,128)(2,1)S(1)}, bf16[512,1536]{1,0:T(8,128)(2,1)S(1)}) custom-call(bf16[512,768]{1,0:T(8,128)(2,1)S(1)} %get-tuple-element.688.x_ref.normed_ref, bf16[768,4992]{1,0:T(8,128)(2,1)S(1)} %copy-done.4, bf16[768,4992]{1,0:T(8,128)(2,1)S(1)} %bitcast.510), custom_call_target="tpu_custom_call" | custom-call | tf_op jit(solution)/shard_map/up_gelu/pallas_call | solution.py:432
  252.0 8.5 %down_norm_head.3 = (f32[512,768]{1,0:T(8,128)S(1)}, bf16[512,768]{1,0:T(8,128)(2,1)S(1)}, f32[512,48]{1,0:T(8,128)S(1)}, f32[512,48]{1,0:T(8,128)S(1)}, f32[512,48]{1,0:T(8,128)}, /*index=5*/f32[8,768]{1,0:T(8,128)S(1)}) custom-call(bf16[512,1536]{1,0:T(8,128)(2,1)S(1)} %get-tuple-element.730.active_one.one_ref, ...), custom_call_target="tpu_custom_call" | custom-call | tf_op jit(solution)/shard_map/down_norm_head/pallas_call | solution.py:476
  277.5 8.6 %up_back.2 = (bf16[512,1536]{1,0:T(8,128)(2,1)S(1)}, bf16[512,1536]{1,0:T(8,128)(2,1)S(1)}, bf16[768,1536]{1,0:T(8,128)(2,1)S(1)}, bf16[768,1536]{1,0:T(8,128)(2,1)}) custom-call(bf16[512,768]{1,0:T(8,128)(2,1)S(1)} %get-tuple-element.737.low_ref, bf16[512,768]{1,0:T(8,128)(2,1)S(1)} %get-tuple-element.688.x_ref.normed_ref, bf16[768,4992]{1,0:T(8,128)(2,1)S(1)} %copy-done.4, ...), custom_call_target="tpu_custom_call" | custom-call | tf_op jit(solution)/shard_map/up_back/pallas_call | solution.py:577
  302.9 7.2 %middle_back.2 = (f32[512,768]{1,0:T(8,128)S(1)}, bf16[512,768]{1,0:T(8,128)(2,1)S(1)}, bf16[512,768]{1,0:T(8,128)(2,1)S(1)}, f32[8,768]{1,0:T(8,128)S(1)}) custom-call(bf16[512,1536]{1,0:T(8,128)(2,1)S(1)} %copy-done.60, bf16[512,1536]{1,0:T(8,128)(2,1)S(1)} %copy-done.62, bf16[768,4992]{1,0:T(8,128)(2,1)S(1)} %copy-done.5, bf16[768,4992]{1,0:T(8,128)(2,1)} %copy-done.6, ...), custom_call_target="tpu_custom_call" | custom-call | tf_op jit(solution)/shard_map/middle_back/pallas_call | solution.py:605
  310.1 9.3 %attention_back.2.joint_ref.refs_4_ = bf16[512,2304]{1,0:T(8,128)(2,1)S(1)} custom-call(bf16[512,2304]{1,0:T(8,128)(2,1)S(1)} %copy-done.11, bf16[512,2304]{1,0:T(8,128)(2,1)S(1)} %copy-done.11, bf16[512,2304]{1,0:T(8,128)(2,1)S(1)} %copy-done.11, bf16[2,12,256,256]{3,2,1,0:T(8,128)(2,1)S(1)} %copy-done.38, bf16[512,768]{1,0:T(8,128)(2,1)S(1)} %get-tuple-element.764.grad_ref), custom_call_target="tpu_custom_call" | custom-call | tf_op jit(solution)/shard_map/attention_back/pallas_call | solution.py:804
  332.5 8.8 %first_weight_grad.2 = (bf16[768,1792]{1,0:T(8,128)(2,1)S(1)}, bf16[768,1792]{1,0:T(8,128)(2,1)S(1)}) custom-call(s32[1]{0:T(128)} %bitcast.67.refs_0_, bf16[512,768]{1,0:T(8,128)(2,1)S(1)} %copy-done.72, bf16[512,768]{1,0:T(8,128)(2,1)S(1)} %copy-done.34, bf16[512,768]{1,0:T(8,128)(2,1)S(1)} %get-tuple-element.786.refs_3_, ...), custom_call_target="tpu_custom_call" | custom-call | tf_op jit(solution)/shard_map/first_weight_grad/pallas_call | solution.py:706
  342.0 10.7 %collective-permute-done.31 = bf16[2,2,2,48,1536]{4,3,0,2,1:T(8,128)(2,1)S(1)} collective-permute-done((bf16[2,2,2,48,1536]{4,3,0,2,1:T(8,128)(2,1)S(1)}, bf16[2,2,2,48,1536]{4,3,0,2,1:T(8,128)(2,1)S(1)}, u32[]{:S(2)}, u32[]{:S(2)}) %collective-permute-start.31) | collective-permute-done | bytes 1179680 | tf_op jit(solution)/shard_map/ppermute | solution.py:50
  380.5 8.8 %up_back.3 = (bf16[512,1536]{1,0:T(8,128)(2,1)S(1)}, bf16[512,1536]{1,0:T(8,128)(2,1)S(1)}, bf16[768,1536]{1,0:T(8,128)(2,1)S(1)}, bf16[768,1536]{1,0:T(8,128)(2,1)S(1)}) custom-call(bf16[512,768]{1,0:T(8,128)(2,1)S(1)} %get-tuple-element.834.low_ref, bf16[512,768]{1,0:T(8,128)(2,1)S(1)} %copy-done.40, bf16[768,1536]{1,0:T(8,128)(2,1)} %bitcast.54.down_one.refs_0_, ...), custom_call_target="tpu_custom_call" | custom-call | tf_op jit(solution)/shard_map/up_back/pallas_call | solution.py:577
  389.4 7.5 %middle_back.3 = (f32[512,768]{1,0:T(8,128)S(1)}, bf16[512,768]{1,0:T(8,128)(2,1)S(1)}, bf16[512,768]{1,0:T(8,128)(2,1)S(1)}, f32[8,768]{1,0:T(8,128)S(1)}) custom-call(bf16[512,1536]{1,0:T(8,128)(2,1)S(1)} %get-tuple-element.845.one_ref, bf16[512,1536]{1,0:T(8,128)(2,1)S(1)} %get-tuple-element.846.two_ref, bf16[768,1536]{1,0:T(8,128)(2,1)S(1)} %bitcast.513, ...), custom_call_target="tpu_custom_call" | custom-call | tf_op jit(solution)/shard_map/middle_back/pallas_call | solution.py:605
  421.1 9.3 %attention_back.3.joint_ref.refs_4_ = bf16[512,2304]{1,0:T(8,128)(2,1)S(1)} custom-call(bf16[512,2304]{1,0:T(8,128)(2,1)S(1)} %copy-done.9, bf16[512,2304]{1,0:T(8,128)(2,1)S(1)} %copy-done.9, bf16[512,2304]{1,0:T(8,128)(2,1)S(1)} %copy-done.9, bf16[2,12,256,256]{3,2,1,0:T(8,128)(2,1)S(1)} %copy-done.36, bf16[512,768]{1,0:T(8,128)(2,1)S(1)} %get-tuple-element.870.grad_ref), custom_call_target="tpu_custom_call" | custom-call | tf_op jit(solution)/shard_map/attention_back/pallas_call | solution.py:804
  444.2 10.1 %first_weight_grad.3 = (bf16[768,1792]{1,0:T(8,128)(2,1)S(1)}, bf16[768,1792]{1,0:T(8,128)(2,1)}) custom-call(s32[1]{0:T(128)} %bitcast.67.refs_0_, bf16[512,768]{1,0:T(8,128)(2,1)S(1)} %copy-done.68, bf16[512,768]{1,0:T(8,128)(2,1)S(1)} %copy-done.32, bf16[512,768]{1,0:T(8,128)(2,1)S(1)} %get-tuple-element.892.refs_3_, ...), custom_call_target="tpu_custom_call" | custom-call | tf_op jit(solution)/shard_map/first_weight_grad/pallas_call | solution.py:706
  456.3 9.4 %collective-permute-done.45 = bf16[2,48,1792]{2,1,0:T(8,128)(2,1)S(1)} collective-permute-done((bf16[2,48,1792]{2,1,0:T(8,128)(2,1)S(1)}, bf16[2,48,1792]{2,1,0:T(8,128)(2,1)S(1)}, u32[]{:S(2)}, u32[]{:S(2)}) %collective-permute-start.45) | collective-permute-done | bytes 344096 | tf_op jit(solution)/shard_map/ppermute | solution.py:50
  481.4 7.1 %collective-permute-done.48 = bf16[48,1792]{1,0:T(8,128)(2,1)S(1)} collective-permute-done((bf16[48,1792]{1,0:T(8,128)(2,1)S(1)}, bf16[48,1792]{1,0:T(8,128)(2,1)S(1)}, u32[]{:S(2)}, u32[]{:S(2)}) %collective-permute-start.48) | collective-permute-done | bytes 172064 | tf_op jit(solution)/shard_map/ppermute | solution.py:50
  506.1 7.3 %collective-permute-done.54 = bf16[48,1536]{1,0:T(8,128)(2,1)S(1)} collective-permute-done((bf16[48,1536]{1,0:T(8,128)(2,1)S(1)}, bf16[48,1536]{1,0:T(8,128)(2,1)S(1)}, u32[]{:S(2)}, u32[]{:S(2)}) %collective-permute-start.54) | collective-permute-done | bytes 147488 | tf_op jit(solution)/shard_map/ppermute | solution.py:50
  513.5 7.0 %collective-permute-done.55 = bf16[2,2,2,48,896]{4,3,0,2,1:T(8,128)(2,1)S(1)} collective-permute-done((bf16[2,2,2,48,896]{4,3,0,2,1:T(8,128)(2,1)S(1)}, bf16[2,2,2,48,896]{4,3,0,2,1:T(8,128)(2,1)S(1)}, u32[]{:S(2)}, u32[]{:S(2)}) %collective-permute-start.55) | collective-permute-done | bytes 688160 | tf_op jit(solution)/shard_map/ppermute | solution.py:50
  (700 shorter events, 333.8 us)
Async XLA Ops:
  7.2 194.3 %all-gather.2.cloned.1.call-start = ((), (), s32[]{:S(2)}) async-start(), calls=%async_computation | async-start | bytes 8146944 | tf_op jit(solution)/shard_map/all_gather | solution.py:1021
  62.9 25.8 %collective-permute-start.15 = (bf16[2,2,48,1920]{3,2,0,1:T(8,128)(2,1)S(1)}, bf16[2,2,48,1920]{3,2,0,1:T(8,128)(2,1)S(1)}, u32[]{:S(2)}, u32[]{:S(2)}) collective-permute-start(bf16[2,2,48,1920]{3,2,0,1:T(8,128)(2,1)S(1)} %pad_maximum_fusion.8), channel_id=1, source_target_pairs={{0,4},{2,6},{4,0},{6,2},{8,12},{10,14},{12,8},{14,10},{16,20},{18,... | collective-permute-start | bytes 2211848 | tf_op jit(solution)/shard_map/ppermute | solution.py:50
  64.5 24.2 %collective-permute-start.16 = (bf16[2,2,48,1536]{3,2,1,0:T(8,128)(2,1)S(1)}, bf16[2,2,48,1536]{3,2,1,0:T(8,128)(2,1)S(1)}, u32[]{:S(2)}, u32[]{:S(2)}) collective-permute-start(bf16[2,2,48,1536]{3,2,1,0:T(8,128)(2,1)S(1)} %pad_maximum_fusion.9), channel_id=1, source_target_pairs={{0,8},{2,10},{4,12},{6,14},{8,0},{10,2},{12,4},{14,6},{16,24},{18,... | collective-permute-start | bytes 1769480 | tf_op jit(solution)/shard_map/ppermute | solution.py:50
  66.9 21.8 %collective-permute-start.17 = (bf16[2,2,48,1536]{3,2,0,1:T(8,128)(2,1)S(1)}, bf16[2,2,48,1536]{3,2,0,1:T(8,128)(2,1)S(1)}, u32[]{:S(2)}, u32[]{:S(2)}) collective-permute-start(bf16[2,2,48,1536]{3,2,0,1:T(8,128)(2,1)S(1)} %pad_maximum_fusion.10), channel_id=1, source_target_pairs={{0,2},{2,0},{4,6},{6,4},{8,10},{10,8},{12,14},{14,12},{16,18},{18,... | collective-permute-start | bytes 1769480 | tf_op jit(solution)/shard_map/ppermute | solution.py:50
  68.5 18.0 %collective-permute-start.18 = (bf16[48,256]{1,0:T(8,128)(2,1)S(1)}, bf16[48,256]{1,0:T(8,128)(2,1)S(1)}, u32[]{:S(2)}, u32[]{:S(2)}) collective-permute-start(bf16[48,256]{1,0:T(8,128)(2,1)S(1)} %pad_maximum_fusion.25), channel_id=1, source_target_pairs={{0,16},{2,18},{4,20},{6,22},{8,24},{10,26},{12,28},{14,30},{16,0},... | collective-permute-start | bytes 73736 | tf_op jit(solution)/shard_map/ppermute | solution.py:50
  89.6 51.5 %collective-permute-start.19 = (bf16[2,2,2,48,1920]{4,3,0,1,2:T(8,128)(2,1)S(1)}, bf16[2,2,2,48,1920]{4,3,0,1,2:T(8,128)(2,1)S(1)}, u32[]{:S(2)}, u32[]{:S(2)}) collective-permute-start(bf16[2,2,2,48,1920]{4,3,0,1,2:T(8,128)(2,1)S(1)} %pad_maximum_fusion.5), channel_id=1, source_target_pairs={{0,2},{2,0},{4,6},{6,4},{8,10},{10,8},{12,14},{14,12},{16,18},{18,... | collective-permute-start | bytes 4423688 | tf_op jit(solution)/shard_map/ppermute | solution.py:50
  91.2 48.9 %collective-permute-start.20 = (bf16[2,2,2,48,1536]{4,3,2,0,1:T(8,128)(2,1)S(1)}, bf16[2,2,2,48,1536]{4,3,2,0,1:T(8,128)(2,1)S(1)}, u32[]{:S(2)}, u32[]{:S(2)}) collective-permute-start(bf16[2,2,2,48,1536]{4,3,2,0,1:T(8,128)(2,1)S(1)} %pad_maximum_fusion.6), channel_id=1, source_target_pairs={{0,4},{2,6},{4,0},{6,2},{8,12},{10,14},{12,8},{14,10},{16,20},{18,... | collective-permute-start | bytes 3538952 | tf_op jit(solution)/shard_map/ppermute | solution.py:50
  92.3 47.7 %collective-permute-start.21 = (bf16[2,2,2,48,1536]{4,3,0,1,2:T(8,128)(2,1)S(1)}, bf16[2,2,2,48,1536]{4,3,0,1,2:T(8,128)(2,1)S(1)}, u32[]{:S(2)}, u32[]{:S(2)}) collective-permute-start(bf16[2,2,2,48,1536]{4,3,0,1,2:T(8,128)(2,1)S(1)} %pad_maximum_fusion.7), channel_id=1, source_target_pairs={{0,8},{2,10},{4,12},{6,14},{8,0},{10,2},{12,4},{14,6},{16,24},{18,... | collective-permute-start | bytes 3538952 | tf_op jit(solution)/shard_map/ppermute | solution.py:50
  92.3 47.7 %collective-permute-start.22 = (bf16[2,48,256]{2,1,0:T(8,128)(2,1)S(1)}, bf16[2,48,256]{2,1,0:T(8,128)(2,1)S(1)}, u32[]{:S(2)}, u32[]{:S(2)}) collective-permute-start(bf16[2,48,256]{2,1,0:T(8,128)(2,1)S(1)} %pad_maximum_fusion.24), channel_id=1, source_target_pairs={{0,8},{2,10},{4,12},{6,14},{8,0},{10,2},{12,4},{14,6},{16,24},{18,... | collective-permute-start | bytes 147464 | tf_op jit(solution)/shard_map/ppermute | solution.py:50
  161.8 25.6 %collective-permute-start.26 = (bf16[768,1536]{1,0:T(8,128)(2,1)S(1)}, bf16[768,1536]{1,0:T(8,128)(2,1)}, u32[]{:S(2)}, u32[]{:S(2)}) collective-permute-start(bf16[768,1536]{1,0:T(8,128)(2,1)S(1)} %bitcast.511), channel_id=1, source_target_pairs={{0,1},{1,0},{2,3},{3,2},{4,5},{5,4},{6,7},{7,6},{8,9},{9,8},{10,11... | collective-permute-start | bytes 7077896 | tf_op jit(solution)/shard_map/ppermute | solution.py:50
  161.8 25.6 %collective-permute-start.27 = (bf16[768,1536]{1,0:T(8,128)(2,1)}, bf16[768,1536]{1,0:T(8,128)(2,1)}, u32[]{:S(2)}, u32[]{:S(2)}) collective-permute-start(bf16[768,1536]{1,0:T(8,128)(2,1)} %bitcast.54.down_one.refs_0_), channel_id=1, source_target_pairs={{0,1},{1,0},{2,3},{3,2},{4,5},{5,4},{6,7},{7,6},{8,9},{9,8},{10,11... | collective-permute-start | bytes 7077896 | tf_op jit(solution)/shard_map/ppermute | solution.py:50
  289.9 31.5 %collective-permute-start.29 = (bf16[768,1536]{1,0:T(8,128)(2,1)}, bf16[768,1536]{1,0:T(8,128)(2,1)S(1)}, u32[]{:S(2)}, u32[]{:S(2)}) collective-permute-start(bf16[768,1536]{1,0:T(8,128)(2,1)} %get-tuple-element.766), channel_id=1, source_target_pairs={{0,1},{1,0},{2,3},{3,2},{4,5},{5,4},{6,7},{7,6},{8,9},{9,8},{10,11... | collective-permute-start | bytes 7077896 | tf_op jit(solution)/shard_map/ppermute | solution.py:50
  290.4 31.0 %collective-permute-start.30 = (bf16[768,1536]{1,0:T(8,128)(2,1)}, bf16[768,1536]{1,0:T(8,128)(2,1)}, u32[]{:S(2)}, u32[]{:S(2)}) collective-permute-start(bf16[768,1536]{1,0:T(8,128)(2,1)} %get-tuple-element.767), channel_id=1, source_target_pairs={{0,1},{1,0},{2,3},{3,2},{4,5},{5,4},{6,7},{7,6},{8,9},{9,8},{10,11... | collective-permute-start | bytes 7077896 | tf_op jit(solution)/shard_map/ppermute | solution.py:50
  324.2 28.4 %collective-permute-start.31 = (bf16[2,2,2,48,1536]{4,3,0,2,1:T(8,128)(2,1)S(1)}, bf16[2,2,2,48,1536]{4,3,0,2,1:T(8,128)(2,1)S(1)}, u32[]{:S(2)}, u32[]{:S(2)}) collective-permute-start(bf16[2,2,2,48,1536]{4,3,0,2,1:T(8,128)(2,1)S(1)} %fusion.4), channel_id=1, source_target_pairs={{0,2},{2,0},{4,6},{6,4},{8,10},{10,8},{12,14},{14,12},{16,18},{18,... | collective-permute-start | bytes 3538952 | tf_op jit(solution)/shard_map/ppermute | solution.py:50
  324.8 28.1 %collective-permute-start.32 = (bf16[2,2,2,48,1536]{4,3,0,2,1:T(8,128)(2,1)S(1)}, bf16[2,2,2,48,1536]{4,3,0,2,1:T(8,128)(2,1)S(1)}, u32[]{:S(2)}, u32[]{:S(2)}) collective-permute-start(bf16[2,2,2,48,1536]{4,3,0,2,1:T(8,128)(2,1)S(1)} %fusion.5), channel_id=1, source_target_pairs={{0,4},{2,6},{4,0},{6,2},{8,12},{10,14},{12,8},{14,10},{16,20},{18,... | collective-permute-start | bytes 3538952 | tf_op jit(solution)/shard_map/ppermute | solution.py:50
  375.5 32.9 %collective-permute-start.39 = (bf16[768,1536]{1,0:T(8,128)(2,1)}, bf16[768,1536]{1,0:T(8,128)(2,1)}, u32[]{:S(2)}, u32[]{:S(2)}) collective-permute-start(bf16[768,1536]{1,0:T(8,128)(2,1)} %get-tuple-element.856), channel_id=1, source_target_pairs={{0,1},{1,0},{2,3},{3,2},{4,5},{5,4},{6,7},{7,6},{8,9},{9,8},{10,11... | collective-permute-start | bytes 7077896 | tf_op jit(solution)/shard_map/ppermute | solution.py:50
  375.5 32.9 %collective-permute-start.38 = (bf16[2,2,2,48,1792]{4,3,0,2,1:T(8,128)(2,1)}, bf16[2,2,2,48,1792]{4,3,0,2,1:T(8,128)(2,1)}, u32[]{:S(2)}, u32[]{:S(2)}) collective-permute-start(bf16[2,2,2,48,1792]{4,3,0,2,1:T(8,128)(2,1)} %fusion.1), channel_id=1, source_target_pairs={{0,2},{2,0},{4,6},{6,4},{8,10},{10,8},{12,14},{14,12},{16,18},{18,... | collective-permute-start | bytes 4128776 | tf_op jit(solution)/shard_map/ppermute | solution.py:50
  412.4 28.5 %collective-permute-start.44 = (bf16[768,1536]{1,0:T(8,128)(2,1)S(1)}, bf16[768,1536]{1,0:T(8,128)(2,1)S(1)}, u32[]{:S(2)}, u32[]{:S(2)}) collective-permute-start(bf16[768,1536]{1,0:T(8,128)(2,1)S(1)} %get-tuple-element.882), channel_id=1, source_target_pairs={{0,1},{1,0},{2,3},{3,2},{4,5},{5,4},{6,7},{7,6},{8,9},{9,8},{10,11... | collective-permute-start | bytes 7077896 | tf_op jit(solution)/shard_map/ppermute | solution.py:50
  412.4 28.4 %collective-permute-start.43 = (bf16[2,2,2,48,1536]{4,3,0,2,1:T(8,128)(2,1)S(1)}, bf16[2,2,2,48,1536]{4,3,0,2,1:T(8,128)(2,1)S(1)}, u32[]{:S(2)}, u32[]{:S(2)}) collective-permute-start(bf16[2,2,2,48,1536]{4,3,0,2,1:T(8,128)(2,1)S(1)} %fusion.6), channel_id=1, source_target_pairs={{0,2},{2,0},{4,6},{6,4},{8,10},{10,8},{12,14},{14,12},{16,18},{18,... | collective-permute-start | bytes 3538952 | tf_op jit(solution)/shard_map/ppermute | solution.py:50
  414.2 21.5 %collective-permute-start.42 = (bf16[2,2,48,1792]{3,2,1,0:T(8,128)(2,1)S(1)}, bf16[2,2,48,1792]{3,2,1,0:T(8,128)(2,1)S(1)}, u32[]{:S(2)}, u32[]{:S(2)}) collective-permute-start(bf16[2,2,48,1792]{3,2,1,0:T(8,128)(2,1)S(1)} %copy.213), channel_id=1, source_target_pairs={{0,4},{2,6},{4,0},{6,2},{8,12},{10,14},{12,8},{14,10},{16,20},{18,... | collective-permute-start | bytes 2064392 | tf_op jit(solution)/shard_map/ppermute | solution.py:50
  415.9 19.8 %collective-permute-start.40 = (bf16[48,1536]{1,0:T(8,128)(2,1)S(1)}, bf16[48,1536]{1,0:T(8,128)(2,1)S(1)}, u32[]{:S(2)}, u32[]{:S(2)}) collective-permute-start(bf16[48,1536]{1,0:T(8,128)(2,1)S(1)} %fusion.85), channel_id=1, source_target_pairs={{0,16},{2,18},{4,20},{6,22},{8,24},{10,26},{12,28},{14,30},{16,0},... | collective-permute-start | bytes 442376 | tf_op jit(solution)/shard_map/ppermute | solution.py:50
  441.9 27.6 %collective-permute-start.47 = (bf16[2,2,2,48,1536]{4,3,0,2,1:T(8,128)(2,1)S(1)}, bf16[2,2,2,48,1536]{4,3,0,2,1:T(8,128)(2,1)S(1)}, u32[]{:S(2)}, u32[]{:S(2)}) collective-permute-start(bf16[2,2,2,48,1536]{4,3,0,2,1:T(8,128)(2,1)S(1)} %fusion.7), channel_id=1, source_target_pairs={{0,4},{2,6},{4,0},{6,2},{8,12},{10,14},{12,8},{14,10},{16,20},{18,... | collective-permute-start | bytes 3538952 | tf_op jit(solution)/shard_map/ppermute | solution.py:50
  443.6 22.1 %collective-permute-start.46 = (bf16[2,2,48,1536]{3,2,1,0:T(8,128)(2,1)S(1)}, bf16[2,2,48,1536]{3,2,1,0:T(8,128)(2,1)S(1)}, u32[]{:S(2)}, u32[]{:S(2)}) collective-permute-start(bf16[2,2,48,1536]{3,2,1,0:T(8,128)(2,1)S(1)} %copy.219), channel_id=1, source_target_pairs={{0,8},{2,10},{4,12},{6,14},{8,0},{10,2},{12,4},{14,6},{16,24},{18,... | collective-permute-start | bytes 1769480 | tf_op jit(solution)/shard_map/ppermute | solution.py:50
  470.7 18.3 %collective-permute-start.51 = (bf16[768,1792]{1,0:T(8,128)(2,1)}, bf16[768,1792]{1,0:T(8,128)(2,1)}, u32[]{:S(2)}, u32[]{:S(2)}) collective-permute-start(bf16[768,1792]{1,0:T(8,128)(2,1)} %get-tuple-element.914), channel_id=1, source_target_pairs={{0,1},{1,0},{2,3},{3,2},{4,5},{5,4},{6,7},{7,6},{8,9},{9,8},{10,11... | collective-permute-start | bytes 8257544 | tf_op jit(solution)/shard_map/ppermute | solution.py:50
  (207 other events, 1240.8 us)
Sparse Core Ops, SparseCore 0:
  49.6 128.2 all-gather.1

commit v4 on v3

--- a/solution.py
+++ b/solution.py
@@ -930,6 +930,8 @@
         ),
         latent_grad,
     )
+    if block == 0:
+        seq.turn()
     launch("down", *seq.compute(down_grads, *saved["actives"], low_final))
     if block == 0:
         seq.turn()
@@ -1033,8 +1035,8 @@
     mine_of = {name: seq.wait(flights[name]) for name in ("up", "down")}
     first_halves = seq.wait(flights["first"])
     later = {name: seq.launch(one_step(mine, "section")) for name, mine in mine_of.items()}
+    first = seq.compute(place_halves, is_first, *first_halves)
     classes = seq.wait(class_flight)
-    first = seq.compute(place_halves, is_first, *first_halves)
     classes_of = (classes[:, : 2 * total_images], classes[:, 2 * total_images :])
 
     start = section * per_core
@@ -1069,7 +1071,6 @@
     grad_one = block_backward(
         seq, section, 1, saved_one, picks, saved_one["latent"], coefficient, pieces[1]
     )
-    seq.turn()
     block_backward(seq, section, 0, saved_zero, picks, grad_one, coefficient, pieces[0])
 
     small_width = 128 + P_SIZE + PD + total_images

time: 613 us -> 608 us (level)
  other arithmetic: 52.6 us -> 45.4 us
    unnamed x330 -> x324, local copies, waits for them, and re-layouts: 58.1 us -> 60.2 us
  transfers between devices with their start and end apart: 72 -> 72, of which waited for: 39 -> 39; matrix products, arithmetic and copies ran while one was open for 7% -> 6% of each run, Pallas kernels for 18% -> 18%
where the time goes in v4:
time: 608 us; the launch traced here: 598 us
  waiting for transfers between devices  202 us (33%)
  Pallas kernels  157 us (26%)
  local copies, waits for them, and re-layouts  91.3 us (15%)
  starting transfers between devices  78.6 us (13%)
  other arithmetic  45.4 us (7%)
  between operations  22.5 us (4%)
    ppermute x71, waiting for transfers between devices, exchange(): return lax.ppermute(value, axis, swap_pairs(lax.axis_size(axis), bit))  202 us
    ppermute x71, starting transfers between devices, exchange(): return lax.ppermute(value, axis, swap_pairs(lax.axis_size(axis), bit))  78.5 us
    unnamed x324, local copies, waits for them, and re-layouts  60.2 us
    pallas_call x2, Pallas kernels, first_grads(): call(lambda *refs: first_grad_kernel(steps, *refs), 'first_weight_grad',...  19 us
    pallas_call x2, Pallas kernels, attend_back(): pl.pallas_call(attend_back_kernel, grid=(count, PAIRS), in_specs=part + [...  18.7 us
    pallas_call x2, Pallas kernels, up_halves(): call(up_kernel, 'up_gelu', 4 * rows * D * FF_HALF, grid=(2 * STEPS,), in_...  17.6 us
    pallas_call x2, Pallas kernels, up_back(): call(up_back_kernel, 'up_back', 8 * rows * D * FF_HALF, grid=(2 * STEPS,)...  17.4 us
    pallas_call x2, Pallas kernels, attend(): pl.pallas_call(attend_kernel, grid=(count, PAIRS), in_specs=part, out_spe...  17.3 us
  transfers between devices with their start and end apart: 72, of which 39 were waited for; matrix products, arithmetic and copies ran while one was open for 6% of the time, Pallas kernels for 18%

profile of v4, /device:TPU:0, one launch (start us, length us, event | category | flops | bytes accessed | tf_op | source)
XLA Modules:
  0.0 598.5 jit_solution(2500094959534161970)
XLA Ops:
  34.3 10.2 %collective-permute-done.10 = bf16[48,1536]{1,0:T(8,128)(2,1)S(1)} collective-permute-done((bf16[48,1536]{1,0:T(8,128)(2,1)S(1)}, bf16[48,1536]{1,0:T(8,128)(2,1)S(1)}, u32[]{:S(2)}, u32[]{:S(2)}) %collective-permute-start.10) | collective-permute-done | bytes 147488 | tf_op jit(solution)/shard_map/ppermute | solution.py:50
  50.6 11.2 %collective-permute-done.12 = bf16[2,48,1536]{2,1,0:T(8,128)(2,1)S(1)} collective-permute-done((bf16[2,48,1536]{2,1,0:T(8,128)(2,1)S(1)}, bf16[2,48,1536]{2,1,0:T(8,128)(2,1)S(1)}, u32[]{:S(2)}, u32[]{:S(2)}) %collective-permute-start.12) | collective-permute-done | bytes 294944 | tf_op jit(solution)/shard_map/ppermute | solution.py:50
  68.5 7.4 %collective-permute-start.18 = (bf16[48,256]{1,0:T(8,128)(2,1)S(1)}, bf16[48,256]{1,0:T(8,128)(2,1)S(1)}, u32[]{:S(2)}, u32[]{:S(2)}) collective-permute-start(bf16[48,256]{1,0:T(8,128)(2,1)S(1)} %pad_maximum_fusion.25), channel_id=1, source_target_pairs={{0,16},{2,18},{4,20},{6,22},{8,24},{10,26},{12,28},{14,30},{16,0},... | collective-permute-start | bytes 73736 | tf_op jit(solution)/shard_map/ppermute | solution.py:50
  75.8 10.8 %collective-permute-done.18 = bf16[48,256]{1,0:T(8,128)(2,1)S(1)} collective-permute-done((bf16[48,256]{1,0:T(8,128)(2,1)S(1)}, bf16[48,256]{1,0:T(8,128)(2,1)S(1)}, u32[]{:S(2)}, u32[]{:S(2)}) %collective-permute-start.18) | collective-permute-done | bytes 24608 | tf_op jit(solution)/shard_map/ppermute | solution.py:50
  94.5 46.8 %collective-permute-done.22 = bf16[2,48,256]{2,1,0:T(8,128)(2,1)S(1)} collective-permute-done((bf16[2,48,256]{2,1,0:T(8,128)(2,1)S(1)}, bf16[2,48,256]{2,1,0:T(8,128)(2,1)S(1)}, u32[]{:S(2)}, u32[]{:S(2)}) %collective-permute-start.22) | collective-permute-done | bytes 49184 | tf_op jit(solution)/shard_map/ppermute | solution.py:50
  169.5 8.5 %attention.2 = (bf16[512,768]{1,0:T(8,128)(2,1)S(1)}, bf16[2,12,256,256]{3,2,1,0:T(8,128)(2,1)S(1)}) custom-call(bf16[512,2304]{1,0:T(8,128)(2,1)S(1)} %get-tuple-element.868.q_ref.k_ref.v_ref, bf16[512,2304]{1,0:T(8,128)(2,1)S(1)} %get-tuple-element.868.q_ref.k_ref.v_ref, bf16[512,2304]{1,0:T(8,128)(2,1)S(1)} %get-tuple-element.868.q_ref.k_ref.v_ref), custom_call_target="tpu_custom_call" | custom-call | tf_op jit(solution)/shard_map/attention/pallas_call | solution.py:761
  182.4 9.4 %up_gelu.2 = (bf16[512,1536]{1,0:T(8,128)(2,1)S(1)}, bf16[512,1536]{1,0:T(8,128)(2,1)S(1)}, bf16[512,1536]{1,0:T(8,128)(2,1)S(1)}, bf16[512,1536]{1,0:T(8,128)(2,1)S(1)}) custom-call(bf16[512,768]{1,0:T(8,128)(2,1)S(1)} %get-tuple-element.618.x_ref.normed_ref, bf16[768,1536]{1,0:T(8,128)(2,1)S(1)} %bitcast.512, ...), custom_call_target="tpu_custom_call" | custom-call | tf_op jit(solution)/shard_map/up_gelu/pallas_call | solution.py:432
  203.6 7.6 %down_norm_head.2 = (f32[512,768]{1,0:T(8,128)S(1)}, bf16[512,768]{1,0:T(8,128)(2,1)S(1)}, f32[512,48]{1,0:T(8,128)S(1)}, f32[512,48]{1,0:T(8,128)S(1)}, f32[512,48]{1,0:T(8,128)S(1)}, /*index=5*/f32[8,768]{1,0:T(8,128)S(1)}) custom-call(bf16[512,1536]{1,0:T(8,128)(2,1)S(1)} %copy-done.19, bf16[512,1536]{1,0:T(8,128)(2,1)S(1)} %copy-done.22, ...), custom_call_target="tpu_custom_call" | custom-call | tf_op jit(solution)/shard_map/down_norm_head/pallas_call | solution.py:476
  224.5 8.9 %attention.3 = (bf16[512,768]{1,0:T(8,128)(2,1)S(1)}, bf16[2,12,256,256]{3,2,1,0:T(8,128)(2,1)S(1)}) custom-call(bf16[512,2304]{1,0:T(8,128)(2,1)S(1)} %get-tuple-element.762.q_ref.k_ref.v_ref, bf16[512,2304]{1,0:T(8,128)(2,1)S(1)} %get-tuple-element.762.q_ref.k_ref.v_ref, bf16[512,2304]{1,0:T(8,128)(2,1)S(1)} %get-tuple-element.762.q_ref.k_ref.v_ref), custom_call_target="tpu_custom_call" | custom-call | tf_op jit(solution)/shard_map/attention/pallas_call | solution.py:761
  237.6 8.2 %up_gelu.3 = (bf16[512,1536]{1,0:T(8,128)(2,1)S(1)}, bf16[512,1536]{1,0:T(8,128)(2,1)S(1)}, bf16[512,1536]{1,0:T(8,128)(2,1)S(1)}, bf16[512,1536]{1,0:T(8,128)(2,1)S(1)}) custom-call(bf16[512,768]{1,0:T(8,128)(2,1)S(1)} %get-tuple-element.688.x_ref.normed_ref, bf16[768,4992]{1,0:T(8,128)(2,1)S(1)} %copy-done.5, bf16[768,4992]{1,0:T(8,128)(2,1)S(1)} %bitcast.510), custom_call_target="tpu_custom_call" | custom-call | tf_op jit(solution)/shard_map/up_gelu/pallas_call | solution.py:432
  247.0 8.5 %down_norm_head.3 = (f32[512,768]{1,0:T(8,128)S(1)}, bf16[512,768]{1,0:T(8,128)(2,1)S(1)}, f32[512,48]{1,0:T(8,128)S(1)}, f32[512,48]{1,0:T(8,128)S(1)}, f32[512,48]{1,0:T(8,128)}, /*index=5*/f32[8,768]{1,0:T(8,128)S(1)}) custom-call(bf16[512,1536]{1,0:T(8,128)(2,1)S(1)} %get-tuple-element.730.active_one.one_ref, ...), custom_call_target="tpu_custom_call" | custom-call | tf_op jit(solution)/shard_map/down_norm_head/pallas_call | solution.py:476
  272.4 8.6 %up_back.2 = (bf16[512,1536]{1,0:T(8,128)(2,1)S(1)}, bf16[512,1536]{1,0:T(8,128)(2,1)S(1)}, bf16[768,1536]{1,0:T(8,128)(2,1)S(1)}, bf16[768,1536]{1,0:T(8,128)(2,1)}) custom-call(bf16[512,768]{1,0:T(8,128)(2,1)S(1)} %get-tuple-element.737.low_ref, bf16[512,768]{1,0:T(8,128)(2,1)S(1)} %get-tuple-element.688.x_ref.normed_ref, bf16[768,4992]{1,0:T(8,128)(2,1)S(1)} %copy-done.5, ...), custom_call_target="tpu_custom_call" | custom-call | tf_op jit(solution)/shard_map/up_back/pallas_call | solution.py:577
  297.8 7.2 %middle_back.2 = (f32[512,768]{1,0:T(8,128)S(1)}, bf16[512,768]{1,0:T(8,128)(2,1)S(1)}, bf16[512,768]{1,0:T(8,128)(2,1)S(1)}, f32[8,768]{1,0:T(8,128)S(1)}) custom-call(bf16[512,1536]{1,0:T(8,128)(2,1)S(1)} %copy-done.61, bf16[512,1536]{1,0:T(8,128)(2,1)S(1)} %copy-done.63, bf16[768,4992]{1,0:T(8,128)(2,1)S(1)} %copy-done.6, bf16[768,4992]{1,0:T(8,128)(2,1)} %copy-done.7, ...), custom_call_target="tpu_custom_call" | custom-call | tf_op jit(solution)/shard_map/middle_back/pallas_call | solution.py:605
  305.0 9.4 %attention_back.2.joint_ref.refs_4_ = bf16[512,2304]{1,0:T(8,128)(2,1)S(1)} custom-call(bf16[512,2304]{1,0:T(8,128)(2,1)S(1)} %copy-done.12, bf16[512,2304]{1,0:T(8,128)(2,1)S(1)} %copy-done.12, bf16[512,2304]{1,0:T(8,128)(2,1)S(1)} %copy-done.12, bf16[2,12,256,256]{3,2,1,0:T(8,128)(2,1)S(1)} %copy-done.39, bf16[512,768]{1,0:T(8,128)(2,1)S(1)} %get-tuple-element.764.grad_ref), custom_call_target="tpu_custom_call" | custom-call | tf_op jit(solution)/shard_map/attention_back/pallas_call | solution.py:804
  329.1 8.8 %first_weight_grad.2 = (bf16[768,1792]{1,0:T(8,128)(2,1)S(1)}, bf16[768,1792]{1,0:T(8,128)(2,1)S(1)}) custom-call(s32[1]{0:T(128)} %bitcast.67.refs_0_, bf16[512,768]{1,0:T(8,128)(2,1)S(1)} %copy-done.73, bf16[512,768]{1,0:T(8,128)(2,1)S(1)} %copy-done.35, bf16[512,768]{1,0:T(8,128)(2,1)S(1)} %get-tuple-element.786.refs_3_, ...), custom_call_target="tpu_custom_call" | custom-call | tf_op jit(solution)/shard_map/first_weight_grad/pallas_call | solution.py:706
  341.6 7.6 %collective-permute-done.31 = bf16[2,2,2,48,1536]{4,3,0,2,1:T(8,128)(2,1)S(1)} collective-permute-done((bf16[2,2,2,48,1536]{4,3,0,2,1:T(8,128)(2,1)S(1)}, bf16[2,2,2,48,1536]{4,3,0,2,1:T(8,128)(2,1)S(1)}, u32[]{:S(2)}, u32[]{:S(2)}) %collective-permute-start.31) | collective-permute-done | bytes 1179680 | tf_op jit(solution)/shard_map/ppermute | solution.py:50
  375.7 8.8 %up_back.3 = (bf16[512,1536]{1,0:T(8,128)(2,1)S(1)}, bf16[512,1536]{1,0:T(8,128)(2,1)S(1)}, bf16[768,1536]{1,0:T(8,128)(2,1)S(1)}, bf16[768,1536]{1,0:T(8,128)(2,1)S(1)}) custom-call(bf16[512,768]{1,0:T(8,128)(2,1)S(1)} %get-tuple-element.834.low_ref, bf16[512,768]{1,0:T(8,128)(2,1)S(1)} %copy-done.41, bf16[768,1536]{1,0:T(8,128)(2,1)} %bitcast.54.down_one.refs_0_, ...), custom_call_target="tpu_custom_call" | custom-call | tf_op jit(solution)/shard_map/up_back/pallas_call | solution.py:577
  384.6 7.5 %middle_back.3 = (f32[512,768]{1,0:T(8,128)S(1)}, bf16[512,768]{1,0:T(8,128)(2,1)S(1)}, bf16[512,768]{1,0:T(8,128)(2,1)S(1)}, f32[8,768]{1,0:T(8,128)S(1)}) custom-call(bf16[512,1536]{1,0:T(8,128)(2,1)S(1)} %get-tuple-element.845.one_ref, bf16[512,1536]{1,0:T(8,128)(2,1)S(1)} %get-tuple-element.846.two_ref, bf16[768,1536]{1,0:T(8,128)(2,1)S(1)} %bitcast.513, ...), custom_call_target="tpu_custom_call" | custom-call | tf_op jit(solution)/shard_map/middle_back/pallas_call | solution.py:605
  416.4 9.3 %attention_back.3.joint_ref.refs_4_ = bf16[512,2304]{1,0:T(8,128)(2,1)S(1)} custom-call(bf16[512,2304]{1,0:T(8,128)(2,1)S(1)} %copy-done.10, bf16[512,2304]{1,0:T(8,128)(2,1)S(1)} %copy-done.10, bf16[512,2304]{1,0:T(8,128)(2,1)S(1)} %copy-done.10, bf16[2,12,256,256]{3,2,1,0:T(8,128)(2,1)S(1)} %copy-done.37, bf16[512,768]{1,0:T(8,128)(2,1)S(1)} %get-tuple-element.870.grad_ref), custom_call_target="tpu_custom_call" | custom-call | tf_op jit(solution)/shard_map/attention_back/pallas_call | solution.py:804
  440.7 10.2 %first_weight_grad.3 = (bf16[768,1792]{1,0:T(8,128)(2,1)S(1)}, bf16[768,1792]{1,0:T(8,128)(2,1)}) custom-call(s32[1]{0:T(128)} %bitcast.67.refs_0_, bf16[512,768]{1,0:T(8,128)(2,1)S(1)} %copy-done.69, bf16[512,768]{1,0:T(8,128)(2,1)S(1)} %copy-done.33, bf16[512,768]{1,0:T(8,128)(2,1)S(1)} %get-tuple-element.892.refs_3_, ...), custom_call_target="tpu_custom_call" | custom-call | tf_op jit(solution)/shard_map/first_weight_grad/pallas_call | solution.py:706
  452.3 9.3 %collective-permute-done.45 = bf16[2,48,1792]{2,1,0:T(8,128)(2,1)S(1)} collective-permute-done((bf16[2,48,1792]{2,1,0:T(8,128)(2,1)S(1)}, bf16[2,48,1792]{2,1,0:T(8,128)(2,1)S(1)}, u32[]{:S(2)}, u32[]{:S(2)}) %collective-permute-start.45) | collective-permute-done | bytes 344096 | tf_op jit(solution)/shard_map/ppermute | solution.py:50
  476.7 7.4 %collective-permute-done.48 = bf16[48,1792]{1,0:T(8,128)(2,1)S(1)} collective-permute-done((bf16[48,1792]{1,0:T(8,128)(2,1)S(1)}, bf16[48,1792]{1,0:T(8,128)(2,1)S(1)}, u32[]{:S(2)}, u32[]{:S(2)}) %collective-permute-start.48) | collective-permute-done | bytes 172064 | tf_op jit(solution)/shard_map/ppermute | solution.py:50
  501.2 7.4 %collective-permute-done.54 = bf16[48,1536]{1,0:T(8,128)(2,1)S(1)} collective-permute-done((bf16[48,1536]{1,0:T(8,128)(2,1)S(1)}, bf16[48,1536]{1,0:T(8,128)(2,1)S(1)}, u32[]{:S(2)}, u32[]{:S(2)}) %collective-permute-start.54) | collective-permute-done | bytes 147488 | tf_op jit(solution)/shard_map/ppermute | solution.py:50
  517.4 6.7 %collective-permute-done.57 = bf16[2,2,48,896]{3,2,1,0:T(8,128)(2,1)S(1)} collective-permute-done((bf16[2,2,48,896]{3,2,1,0:T(8,128)(2,1)S(1)}, bf16[2,2,48,896]{3,2,1,0:T(8,128)(2,1)S(1)}, u32[]{:S(2)}, u32[]{:S(2)}) %collective-permute-start.57) | collective-permute-done | bytes 344096 | tf_op jit(solution)/shard_map/ppermute | solution.py:50
  (694 shorter events, 330.5 us)
Async XLA Ops:
  7.2 189.3 %all-gather.2.cloned.1.call-start = ((), (), s32[]{:S(2)}) async-start(), calls=%async_computation | async-start | bytes 8146944 | tf_op jit(solution)/shard_map/all_gather | solution.py:1023
  62.9 26.8 %collective-permute-start.15 = (bf16[2,2,48,1920]{3,2,0,1:T(8,128)(2,1)S(1)}, bf16[2,2,48,1920]{3,2,0,1:T(8,128)(2,1)S(1)}, u32[]{:S(2)}, u32[]{:S(2)}) collective-permute-start(bf16[2,2,48,1920]{3,2,0,1:T(8,128)(2,1)S(1)} %pad_maximum_fusion.8), channel_id=1, source_target_pairs={{0,4},{2,6},{4,0},{6,2},{8,12},{10,14},{12,8},{14,10},{16,20},{18,... | collective-permute-start | bytes 2211848 | tf_op jit(solution)/shard_map/ppermute | solution.py:50
  64.5 25.2 %collective-permute-start.16 = (bf16[2,2,48,1536]{3,2,1,0:T(8,128)(2,1)S(1)}, bf16[2,2,48,1536]{3,2,1,0:T(8,128)(2,1)S(1)}, u32[]{:S(2)}, u32[]{:S(2)}) collective-permute-start(bf16[2,2,48,1536]{3,2,1,0:T(8,128)(2,1)S(1)} %pad_maximum_fusion.9), channel_id=1, source_target_pairs={{0,8},{2,10},{4,12},{6,14},{8,0},{10,2},{12,4},{14,6},{16,24},{18,... | collective-permute-start | bytes 1769480 | tf_op jit(solution)/shard_map/ppermute | solution.py:50
  66.9 22.8 %collective-permute-start.17 = (bf16[2,2,48,1536]{3,2,0,1:T(8,128)(2,1)S(1)}, bf16[2,2,48,1536]{3,2,0,1:T(8,128)(2,1)S(1)}, u32[]{:S(2)}, u32[]{:S(2)}) collective-permute-start(bf16[2,2,48,1536]{3,2,0,1:T(8,128)(2,1)S(1)} %pad_maximum_fusion.10), channel_id=1, source_target_pairs={{0,2},{2,0},{4,6},{6,4},{8,10},{10,8},{12,14},{14,12},{16,18},{18,... | collective-permute-start | bytes 1769480 | tf_op jit(solution)/shard_map/ppermute | solution.py:50
  68.5 18.1 %collective-permute-start.18 = (bf16[48,256]{1,0:T(8,128)(2,1)S(1)}, bf16[48,256]{1,0:T(8,128)(2,1)S(1)}, u32[]{:S(2)}, u32[]{:S(2)}) collective-permute-start(bf16[48,256]{1,0:T(8,128)(2,1)S(1)} %pad_maximum_fusion.25), channel_id=1, source_target_pairs={{0,16},{2,18},{4,20},{6,22},{8,24},{10,26},{12,28},{14,30},{16,0},... | collective-permute-start | bytes 73736 | tf_op jit(solution)/shard_map/ppermute | solution.py:50
  90.5 50.8 %collective-permute-start.19 = (bf16[2,2,2,48,1920]{4,3,0,1,2:T(8,128)(2,1)S(1)}, bf16[2,2,2,48,1920]{4,3,0,1,2:T(8,128)(2,1)S(1)}, u32[]{:S(2)}, u32[]{:S(2)}) collective-permute-start(bf16[2,2,2,48,1920]{4,3,0,1,2:T(8,128)(2,1)S(1)} %pad_maximum_fusion.5), channel_id=1, source_target_pairs={{0,2},{2,0},{4,6},{6,4},{8,10},{10,8},{12,14},{14,12},{16,18},{18,... | collective-permute-start | bytes 4423688 | tf_op jit(solution)/shard_map/ppermute | solution.py:50
  92.1 49.3 %collective-permute-start.20 = (bf16[2,2,2,48,1536]{4,3,2,0,1:T(8,128)(2,1)S(1)}, bf16[2,2,2,48,1536]{4,3,2,0,1:T(8,128)(2,1)S(1)}, u32[]{:S(2)}, u32[]{:S(2)}) collective-permute-start(bf16[2,2,2,48,1536]{4,3,2,0,1:T(8,128)(2,1)S(1)} %pad_maximum_fusion.6), channel_id=1, source_target_pairs={{0,4},{2,6},{4,0},{6,2},{8,12},{10,14},{12,8},{14,10},{16,20},{18,... | collective-permute-start | bytes 3538952 | tf_op jit(solution)/shard_map/ppermute | solution.py:50
  92.5 48.9 %collective-permute-start.21 = (bf16[2,2,2,48,1536]{4,3,0,1,2:T(8,128)(2,1)S(1)}, bf16[2,2,2,48,1536]{4,3,0,1,2:T(8,128)(2,1)S(1)}, u32[]{:S(2)}, u32[]{:S(2)}) collective-permute-start(bf16[2,2,2,48,1536]{4,3,0,1,2:T(8,128)(2,1)S(1)} %pad_maximum_fusion.7), channel_id=1, source_target_pairs={{0,8},{2,10},{4,12},{6,14},{8,0},{10,2},{12,4},{14,6},{16,24},{18,... | collective-permute-start | bytes 3538952 | tf_op jit(solution)/shard_map/ppermute | solution.py:50
  92.5 48.9 %collective-permute-start.22 = (bf16[2,48,256]{2,1,0:T(8,128)(2,1)S(1)}, bf16[2,48,256]{2,1,0:T(8,128)(2,1)S(1)}, u32[]{:S(2)}, u32[]{:S(2)}) collective-permute-start(bf16[2,48,256]{2,1,0:T(8,128)(2,1)S(1)} %pad_maximum_fusion.24), channel_id=1, source_target_pairs={{0,8},{2,10},{4,12},{6,14},{8,0},{10,2},{12,4},{14,6},{16,24},{18,... | collective-permute-start | bytes 147464 | tf_op jit(solution)/shard_map/ppermute | solution.py:50
  161.2 21.2 %collective-permute-start.26 = (bf16[768,1536]{1,0:T(8,128)(2,1)S(1)}, bf16[768,1536]{1,0:T(8,128)(2,1)}, u32[]{:S(2)}, u32[]{:S(2)}) collective-permute-start(bf16[768,1536]{1,0:T(8,128)(2,1)S(1)} %bitcast.511), channel_id=1, source_target_pairs={{0,1},{1,0},{2,3},{3,2},{4,5},{5,4},{6,7},{7,6},{8,9},{9,8},{10,11... | collective-permute-start | bytes 7077896 | tf_op jit(solution)/shard_map/ppermute | solution.py:50
  161.2 21.2 %collective-permute-start.27 = (bf16[768,1536]{1,0:T(8,128)(2,1)}, bf16[768,1536]{1,0:T(8,128)(2,1)}, u32[]{:S(2)}, u32[]{:S(2)}) collective-permute-start(bf16[768,1536]{1,0:T(8,128)(2,1)} %bitcast.54.down_one.refs_0_), channel_id=1, source_target_pairs={{0,1},{1,0},{2,3},{3,2},{4,5},{5,4},{6,7},{7,6},{8,9},{9,8},{10,11... | collective-permute-start | bytes 7077896 | tf_op jit(solution)/shard_map/ppermute | solution.py:50
  284.7 31.5 %collective-permute-start.29 = (bf16[768,1536]{1,0:T(8,128)(2,1)}, bf16[768,1536]{1,0:T(8,128)(2,1)}, u32[]{:S(2)}, u32[]{:S(2)}) collective-permute-start(bf16[768,1536]{1,0:T(8,128)(2,1)} %get-tuple-element.766), channel_id=1, source_target_pairs={{0,1},{1,0},{2,3},{3,2},{4,5},{5,4},{6,7},{7,6},{8,9},{9,8},{10,11... | collective-permute-start | bytes 7077896 | tf_op jit(solution)/shard_map/ppermute | solution.py:50
  285.2 31.0 %collective-permute-start.30 = (bf16[768,1536]{1,0:T(8,128)(2,1)}, bf16[768,1536]{1,0:T(8,128)(2,1)}, u32[]{:S(2)}, u32[]{:S(2)}) collective-permute-start(bf16[768,1536]{1,0:T(8,128)(2,1)} %get-tuple-element.767), channel_id=1, source_target_pairs={{0,1},{1,0},{2,3},{3,2},{4,5},{5,4},{6,7},{7,6},{8,9},{9,8},{10,11... | collective-permute-start | bytes 7077896 | tf_op jit(solution)/shard_map/ppermute | solution.py:50
  320.8 28.4 %collective-permute-start.31 = (bf16[2,2,2,48,1536]{4,3,0,2,1:T(8,128)(2,1)S(1)}, bf16[2,2,2,48,1536]{4,3,0,2,1:T(8,128)(2,1)S(1)}, u32[]{:S(2)}, u32[]{:S(2)}) collective-permute-start(bf16[2,2,2,48,1536]{4,3,0,2,1:T(8,128)(2,1)S(1)} %fusion.4), channel_id=1, source_target_pairs={{0,2},{2,0},{4,6},{6,4},{8,10},{10,8},{12,14},{14,12},{16,18},{18,... | collective-permute-start | bytes 3538952 | tf_op jit(solution)/shard_map/ppermute | solution.py:50
  321.1 28.2 %collective-permute-start.32 = (bf16[2,2,2,48,1536]{4,3,0,2,1:T(8,128)(2,1)S(1)}, bf16[2,2,2,48,1536]{4,3,0,2,1:T(8,128)(2,1)S(1)}, u32[]{:S(2)}, u32[]{:S(2)}) collective-permute-start(bf16[2,2,2,48,1536]{4,3,0,2,1:T(8,128)(2,1)S(1)} %fusion.5), channel_id=1, source_target_pairs={{0,4},{2,6},{4,0},{6,2},{8,12},{10,14},{12,8},{14,10},{16,20},{18,... | collective-permute-start | bytes 3538952 | tf_op jit(solution)/shard_map/ppermute | solution.py:50
  371.5 32.9 %collective-permute-start.39 = (bf16[768,1536]{1,0:T(8,128)(2,1)}, bf16[768,1536]{1,0:T(8,128)(2,1)}, u32[]{:S(2)}, u32[]{:S(2)}) collective-permute-start(bf16[768,1536]{1,0:T(8,128)(2,1)} %get-tuple-element.856), channel_id=1, source_target_pairs={{0,1},{1,0},{2,3},{3,2},{4,5},{5,4},{6,7},{7,6},{8,9},{9,8},{10,11... | collective-permute-start | bytes 7077896 | tf_op jit(solution)/shard_map/ppermute | solution.py:50
  371.5 32.9 %collective-permute-start.38 = (bf16[2,2,2,48,1792]{4,3,0,2,1:T(8,128)(2,1)}, bf16[2,2,2,48,1792]{4,3,0,2,1:T(8,128)(2,1)}, u32[]{:S(2)}, u32[]{:S(2)}) collective-permute-start(bf16[2,2,2,48,1792]{4,3,0,2,1:T(8,128)(2,1)} %fusion.1), channel_id=1, source_target_pairs={{0,2},{2,0},{4,6},{6,4},{8,10},{10,8},{12,14},{14,12},{16,18},{18,... | collective-permute-start | bytes 4128776 | tf_op jit(solution)/shard_map/ppermute | solution.py:50
  408.4 28.5 %collective-permute-start.44 = (bf16[768,1536]{1,0:T(8,128)(2,1)S(1)}, bf16[768,1536]{1,0:T(8,128)(2,1)S(1)}, u32[]{:S(2)}, u32[]{:S(2)}) collective-permute-start(bf16[768,1536]{1,0:T(8,128)(2,1)S(1)} %get-tuple-element.882), channel_id=1, source_target_pairs={{0,1},{1,0},{2,3},{3,2},{4,5},{5,4},{6,7},{7,6},{8,9},{9,8},{10,11... | collective-permute-start | bytes 7077896 | tf_op jit(solution)/shard_map/ppermute | solution.py:50
  408.5 28.4 %collective-permute-start.43 = (bf16[2,2,2,48,1536]{4,3,0,2,1:T(8,128)(2,1)S(1)}, bf16[2,2,2,48,1536]{4,3,0,2,1:T(8,128)(2,1)S(1)}, u32[]{:S(2)}, u32[]{:S(2)}) collective-permute-start(bf16[2,2,2,48,1536]{4,3,0,2,1:T(8,128)(2,1)S(1)} %fusion.6), channel_id=1, source_target_pairs={{0,2},{2,0},{4,6},{6,4},{8,10},{10,8},{12,14},{14,12},{16,18},{18,... | collective-permute-start | bytes 3538952 | tf_op jit(solution)/shard_map/ppermute | solution.py:50
  409.4 21.7 %collective-permute-start.42 = (bf16[2,2,48,1792]{3,2,1,0:T(8,128)(2,1)S(1)}, bf16[2,2,48,1792]{3,2,1,0:T(8,128)(2,1)S(1)}, u32[]{:S(2)}, u32[]{:S(2)}) collective-permute-start(bf16[2,2,48,1792]{3,2,1,0:T(8,128)(2,1)S(1)} %copy.213), channel_id=1, source_target_pairs={{0,4},{2,6},{4,0},{6,2},{8,12},{10,14},{12,8},{14,10},{16,20},{18,... | collective-permute-start | bytes 2064392 | tf_op jit(solution)/shard_map/ppermute | solution.py:50
  411.1 19.9 %collective-permute-start.40 = (bf16[48,1536]{1,0:T(8,128)(2,1)S(1)}, bf16[48,1536]{1,0:T(8,128)(2,1)S(1)}, u32[]{:S(2)}, u32[]{:S(2)}) collective-permute-start(bf16[48,1536]{1,0:T(8,128)(2,1)S(1)} %fusion.85), channel_id=1, source_target_pairs={{0,16},{2,18},{4,20},{6,22},{8,24},{10,26},{12,28},{14,30},{16,0},... | collective-permute-start | bytes 442376 | tf_op jit(solution)/shard_map/ppermute | solution.py:50
  438.0 27.6 %collective-permute-start.47 = (bf16[2,2,2,48,1536]{4,3,0,2,1:T(8,128)(2,1)S(1)}, bf16[2,2,2,48,1536]{4,3,0,2,1:T(8,128)(2,1)S(1)}, u32[]{:S(2)}, u32[]{:S(2)}) collective-permute-start(bf16[2,2,2,48,1536]{4,3,0,2,1:T(8,128)(2,1)S(1)} %fusion.7), channel_id=1, source_target_pairs={{0,4},{2,6},{4,0},{6,2},{8,12},{10,14},{12,8},{14,10},{16,20},{18,... | collective-permute-start | bytes 3538952 | tf_op jit(solution)/shard_map/ppermute | solution.py:50
  439.5 22.1 %collective-permute-start.46 = (bf16[2,2,48,1536]{3,2,1,0:T(8,128)(2,1)S(1)}, bf16[2,2,48,1536]{3,2,1,0:T(8,128)(2,1)S(1)}, u32[]{:S(2)}, u32[]{:S(2)}) collective-permute-start(bf16[2,2,48,1536]{3,2,1,0:T(8,128)(2,1)S(1)} %copy.219), channel_id=1, source_target_pairs={{0,8},{2,10},{4,12},{6,14},{8,0},{10,2},{12,4},{14,6},{16,24},{18,... | collective-permute-start | bytes 1769480 | tf_op jit(solution)/shard_map/ppermute | solution.py:50
  466.8 18.3 %collective-permute-start.51 = (bf16[768,1792]{1,0:T(8,128)(2,1)}, bf16[768,1792]{1,0:T(8,128)(2,1)}, u32[]{:S(2)}, u32[]{:S(2)}) collective-permute-start(bf16[768,1792]{1,0:T(8,128)(2,1)} %get-tuple-element.914), channel_id=1, source_target_pairs={{0,1},{1,0},{2,3},{3,2},{4,5},{5,4},{6,7},{7,6},{8,9},{9,8},{10,11... | collective-permute-start | bytes 8257544 | tf_op jit(solution)/shard_map/ppermute | solution.py:50
  (204 other events, 1281.8 us)
Sparse Core Ops, SparseCore 0:
  49.6 127.5 all-gather.1
